TPU v7x, 256 devices: a whole 4x4x8 slice. The times are simulated.
256 devices in a mesh: grid: 32 (over z, y), tile: 8 (over x, core).
Axes of the slice: x: 4, y: 4, z: 8, core: 2. Of those that a mesh axis runs over, the one named last changes fastest.
Arguments:
- point_values: bfloat16 [1024, 16384], P('grid', 'tile'), may hold values from -1.75 to 1.75
- sig_blocks: int32 [32, 16], P('grid'), may hold values from 0 to 31, as said below
- density: bfloat16 [16384, 16384], P('grid', 'tile'), may hold values from -0.0625 to 0.0625
- coulomb_core: bfloat16 [512, 512], replicated, may hold values from -0.25 to 0.25
- screen_mask: int32 [32, 32], replicated, may hold values 0 or 1
- ao_centers: float32 [3, 16384], replicated, may hold values from -1 to 1
- ao_widths: float32 [16384], replicated, may hold values from 0.25 to 1
- point_coords: float32 [3, 1024], P(None, 'grid'), may hold values from -1 to 1
- lmo_coeffs: bfloat16 [16384, 2048], P('tile'), may hold values from -0.0625 to 0.0625
- domain_blocks: int32 [8, 16], replicated, may hold values from 0 to 31, as said below
Outputs:
- half: bfloat16 [2048, 16384], P('tile', 'grid')
Inputs may be any that keep to these rules, and one draw needn't show every extreme that they name: `sig_blocks`: each batch names 16 different AO blocks. `domain_blocks`: each strip's 16 blocks are different, and every AO block lies in the domain of some strip.
All inputs are finite; a program needn't handle non-finite values.
Results may differ from a plain program's by a relative error of at most 0.02.
Values may be sent and summed in bfloat16 or wider, within the bound.
No kernel may reach another device: no remote copies, remote signals or barrier semaphores. Data moves between devices by JAX's collectives and lax.ppermute only.
A program may use at most 64 MiB of HBM per device.

v0:
```python
import jax
import jax.numpy as jnp
from jax import lax
from jax.sharding import PartitionSpec as P

highest = lax.Precision.HIGHEST


def kernel_weights(ao_centers, ao_widths, point_coords):
    offsets = ao_centers[:, None, :] - point_coords[:, :, None]
    return 1.0 / jnp.sqrt(jnp.sum(offsets * offsets, axis=0) + ao_widths[None, :])


def spread_mask(flag_rows, batch_points, block_size):
    batches, block_count = flag_rows.shape
    expanded = jnp.broadcast_to(
        flag_rows[:, None, :, None], (batches, batch_points, block_count, block_size)
    )
    return expanded.reshape(batches * batch_points, block_count * block_size)


def shards(
    point_values,
    sig_blocks,
    density,
    coulomb_core,
    screen_mask,
    ao_centers,
    ao_widths,
    point_coords,
    lmo_coeffs,
    domain_blocks,
):
    grid_count = lax.axis_size("grid")
    panel_index = lax.axis_index("tile")
    batches = sig_blocks.shape[0]
    own_rows, own_cols = density.shape
    points = point_values.shape[0]
    batch_points = points // batches
    block_size = coulomb_core.shape[0]
    total_aos = ao_widths.shape[0]
    all_blocks = total_aos // block_size
    col_blocks = own_cols // block_size
    row_blocks = own_rows // block_size
    block_ids = jnp.arange(all_blocks, dtype=jnp.int32)
    named_blocks = jnp.any(sig_blocks[:, :, None] == block_ids[None, None, :], axis=1).astype(
        jnp.float32
    )
    first_col = panel_index * col_blocks
    named_cols = lax.dynamic_slice_in_dim(named_blocks, first_col, col_blocks, 1)
    col_mask = spread_mask(named_cols, batch_points, block_size)
    masked_local = point_values * col_mask.astype(jnp.bfloat16)
    dest_named = jnp.max(named_blocks.reshape(batches, grid_count, row_blocks), axis=2)
    outgoing = masked_local.reshape(batches, batch_points, 1, own_cols) * dest_named[
        :, None, :, None
    ].astype(jnp.bfloat16)
    product = jnp.einsum(
        "bpgc,rc->bpgr",
        lax.all_to_all(outgoing, "grid", split_axis=2, concat_axis=2, tiled=True),
        density,
        preferred_element_type=jnp.float32,
    )
    arrivals = lax.all_to_all(
        product.astype(jnp.bfloat16), "grid", split_axis=2, concat_axis=2, tiled=True
    )
    row_mask = spread_mask(named_blocks, batch_points, block_size)
    partial_term = arrivals.reshape(points, total_aos).astype(jnp.float32) * row_mask
    coefficient = kernel_weights(ao_centers, ao_widths, point_coords)
    core_float = coulomb_core.astype(jnp.float32)
    screen_float = screen_mask.astype(jnp.float32)
    density_term = lax.psum(partial_term.astype(jnp.bfloat16), "tile").astype(jnp.float32)
    weighted = (coefficient * density_term).reshape(points, all_blocks, block_size)
    screen_rows = lax.dynamic_slice_in_dim(screen_float, first_col, col_blocks, 0)
    screened = jnp.einsum("kj,pja->pka", screen_rows, weighted, precision=highest)
    kernel_part = jnp.einsum(
        "ab,pkb->pka", core_float, screened, preferred_element_type=jnp.float32
    ).reshape(points, own_cols)
    coeff_cols = lax.dynamic_slice_in_dim(coefficient, panel_index * own_cols, own_cols, 1)
    potential = (coeff_cols * kernel_part * col_mask).astype(jnp.bfloat16)
    potential_out = jnp.broadcast_to(
        potential.reshape(batches, batch_points, 1, own_cols),
        (batches, batch_points, grid_count, own_cols),
    )
    whole_points = lax.all_gather(masked_local, "tile", axis=1, tiled=True)
    row_values, col_values = (
        lax.all_to_all(
            whole_points.reshape(batches, batch_points, grid_count, own_rows),
            "grid",
            split_axis=2,
            concat_axis=2,
            tiled=True,
        ),
        lax.all_to_all(potential_out, "grid", split_axis=2, concat_axis=2, tiled=True),
    )
    exch_tile = jnp.einsum(
        "bpgr,bpgc->rc", row_values, col_values, preferred_element_type=jnp.float32
    ).astype(jnp.bfloat16)
    number_of_slabs = domain_blocks.shape[0]
    localized_orbital_total = lmo_coeffs.shape[1]
    strip_width = localized_orbital_total // number_of_slabs
    local_ids = first_col + jnp.arange(col_blocks, dtype=jnp.int32)
    in_domain = jnp.any(domain_blocks[:, :, None] == local_ids[None, None, :], axis=1)
    domain_flags = jnp.transpose(in_domain)
    domain_mask = jnp.broadcast_to(
        domain_flags[:, None, :, None], (col_blocks, block_size, number_of_slabs, strip_width)
    ).reshape(own_cols, localized_orbital_total)
    region_expansion_factor = lmo_coeffs * domain_mask.astype(jnp.bfloat16)
    return lax.psum_scatter(
        lax.dot_general(
            region_expansion_factor,
            exch_tile,
            (((0,), (1,)), ((), ())),
            preferred_element_type=jnp.float32,
        ).astype(jnp.bfloat16),
        "tile",
        scatter_dimension=0,
        tiled=True,
    )


def solution(mesh):
    in_specs = (
        P("grid", "tile"),
        P("grid", None),
        P("grid", "tile"),
        P(),
        P(),
        P(),
        P(),
        P(None, "grid"),
        P("tile", None),
        P(),
    )
    out_specs = P("tile", "grid")
    return jax.shard_map(shards, mesh=mesh, in_specs=in_specs, out_specs=out_specs, check_vma=False)
```

profile of v0, /device:TPU:32, one launch (start us, length us, event | category | flops | bytes accessed | tf_op | source)
XLA Modules:
  0.0 396.5 jit_solution(5231254899903409113)
XLA Ops:
  6.5 0.0 copy-start
  6.5 0.9 fusion.33
  7.4 0.1 dynamic-slice.3
  7.5 0.1 broadcast_bitcast_fusion.1
  7.6 0.9 broadcast_multiply_fusion.1
  8.5 0.0 copy-start.1
  8.5 0.3 broadcast_multiply_fusion
  8.9 105.8 %all_to_all.20 = bf16[1,32,32,2048]{3,1,0,2:T(8,128)(2,1)S(1)} all-to-all(bf16[1,32,32,2048]{3,1,0,2:T(8,128)(2,1)S(1)} %broadcast_multiply_fusion), channel_id=1, replica_groups=mesh['grid'=32,'tile'=8] {'grid'}, dimensions={2} | all-to-all | bytes 8388608 | tf_op jit(solution)/shard_map/all_to_all | solution.py:59
  114.7 0.0 copy-done.1
  114.7 0.0 copy-done
  114.7 2.6 fusion.22
  117.4 1.5 copy.30
  118.9 6.4 %all-to-all-start.2 = ((bf16[1,32,32,512]{3,1,0,2:T(8,128)(2,1)}), bf16[1,32,32,512]{3,1,0,2:T(8,128)(2,1)S(1)}, u32[]{:S(2)}, u32[]{:S(2)}) async-start(bf16[1,32,32,512]{3,1,0,2:T(8,128)(2,1)} %copy.30), calls=%async_computation.2 | async-start | bytes 2097152 | tf_op jit(solution)/shard_map/all_to_all | solution.py:63
  125.3 0.0 copy-start.3
  125.3 0.0 copy-start.6
  125.3 0.0 all-gather.2.cloned.1.call-start
  125.3 0.7 all-gather.2.cloned.1.call-update
  126.0 0.0 all-reduce.2.cloned.1.call-start
  126.1 0.1 broadcast_bitcast_fusion
  126.2 25.6 %all-to-all-done.2 = bf16[1,32,32,512]{3,1,0,2:T(8,128)(2,1)S(1)} async-done(((bf16[1,32,32,512]{3,1,0,2:T(8,128)(2,1)}), bf16[1,32,32,512]{3,1,0,2:T(8,128)(2,1)S(1)}, u32[]{:S(2)}, u32[]{:S(2)}) %all-to-all-start.2) | async-done | bytes 1048608 | tf_op jit(solution)/shard_map/all_to_all | solution.py:63
  151.7 0.3 copy.39
  152.0 1.1 multiply_convert_fusion
  153.1 0.0 all-reduce.2.cloned.1.call-update
  153.2 0.0 copy-done.3
  153.2 0.0 copy-done.6
  153.2 0.0 copy-start.4
  153.2 2.1 multiply_reduce_fusion
  155.3 1.5 copy.38
  156.9 1.6 copy.27
  158.5 9.7 %all-to-all-start = ((bf16[1,32,32,512]{3,1,0,2:T(8,128)(2,1)}), bf16[1,32,32,512]{3,1,0,2:T(8,128)(2,1)S(1)}, u32[]{:S(2)}, u32[]{:S(2)}) async-start(bf16[1,32,32,512]{3,1,0,2:T(8,128)(2,1)} %copy.27), calls=%async_computation | async-start | bytes 2097152 | tf_op jit(solution)/shard_map/all_to_all | solution.py:86
  168.1 57.2 %all-reduce.2.cloned.1.call-done = bf16[32,16384]{1,0:T(8,128)(2,1)} async-done(((bf16[32,16384]{1,0:T(8,128)(2,1)}), bf16[32,16384]{1,0:T(8,128)(2,1)}) %all-reduce.2.cloned.1.call-update) | async-done | bytes 1048592 | tf_op jit(solution)/shard_map/psum | solution.py:71
  225.4 0.0 copy-done.4
  225.4 2.2 convert_multiply_fusion
  227.6 0.0 copy-start.2
  227.6 1.2 copy.41
  228.8 1.9 convolution_bitcast_fusion.1
  230.7 0.3 convolution_bitcast_fusion
  231.1 0.0 all-to-all-done
  231.1 2.5 broadcast_in_dim.49
  233.6 10.3 %all-to-all-start.3 = ((bf16[1,32,32,2048]{3,1,0,2:T(8,128)(2,1)}), bf16[1,32,32,2048]{3,1,0,2:T(8,128)(2,1)}, u32[]{:S(2)}, u32[]{:S(2)}) async-start(bf16[1,32,32,2048]{3,1,0,2:T(8,128)(2,1)} %broadcast_in_dim.49), calls=%async_computation.3 | async-start | bytes 8388608 | tf_op jit(solution)/shard_map/all_to_all | solution.py:93
  243.9 0.2 reduce-scatter.2.cloned.1.call-start
  244.2 0.2 compare_reduce_fusion
  244.4 1.2 broadcast_in_dim.18
  245.5 4.1 %copy.36 = pred[256,8,8,256]{3,1,2,0:T(8,128)(4,1)} copy(pred[256,8,8,256]{3,2,1,0:T(8,128)(4,1)S(1)} %bitcast.64) | data formatting | bytes 8388608
  249.7 86.9 %all-to-all-done.3 = bf16[1,32,32,2048]{3,1,0,2:T(8,128)(2,1)} async-done(((bf16[1,32,32,2048]{3,1,0,2:T(8,128)(2,1)}), bf16[1,32,32,2048]{3,1,0,2:T(8,128)(2,1)}, u32[]{:S(2)}, u32[]{:S(2)}) %all-to-all-start.3) | async-done | bytes 4194336 | tf_op jit(solution)/shard_map/all_to_all | solution.py:93
  336.6 16.0 %fusion.9 = bf16[2048,512]{1,0:T(8,128)(2,1)} fusion(pred[2048,2048]{1,0:T(8,128)(4,1)} %bitcast.69, bf16[2048,2048]{1,0:T(8,128)(2,1)} %param.18, bf16[1,32,32,2048]{3,1,0,2:T(8,128)(2,1)} %all-to-all-done.3, bf16[1,32,32,512]{3,1,0,2:T(8,128)(2,1)S(1)} %all-to-all-done), kind=kOutput, calls=%fused_computation.11 | convolution fusion | flops 6448742400 | bytes 19922944 | tf_op jit(solution)/shard_map/dot_general | solution.py:109
  352.6 0.0 reduce-scatter.2.cloned.1.call-update
  352.6 37.3 %reduce-scatter.2.cloned.1.call-done = bf16[256,512]{1,0:T(8,128)(2,1)} async-done(((bf16[2048,512]{1,0:T(8,128)(2,1)}), bf16[256,512]{1,0:T(8,128)(2,1)}) %reduce-scatter.2.cloned.1.call-update) | async-done | bytes 262160 | tf_op jit(solution)/shard_map/reduce_scatter | solution.py:108
  (11 shorter events, 0.1 us)
Async XLA Ops:
  6.5 108.2 %copy-start = (bf16[512,2048]{1,0:T(8,128)(2,1)S(1)}, bf16[512,2048]{1,0:T(8,128)(2,1)}, u32[]{:S(2)}) copy-start(bf16[512,2048]{1,0:T(8,128)(2,1)} %param.12) | copy-start | bytes 6291460
  8.5 106.2 %copy-start.1 = (bf16[32,2048]{1,0:T(8,128)(2,1)}, bf16[32,2048]{1,0:T(8,128)(2,1)S(1)}, u32[]{:S(2)}) copy-start(bf16[32,2048]{1,0:T(8,128)(2,1)S(1)} %broadcast_multiply_fusion.1) | copy-start | bytes 393220
  118.9 32.8 %all-to-all-start.2 = ((bf16[1,32,32,512]{3,1,0,2:T(8,128)(2,1)}), bf16[1,32,32,512]{3,1,0,2:T(8,128)(2,1)S(1)}, u32[]{:S(2)}, u32[]{:S(2)}) async-start(bf16[1,32,32,512]{3,1,0,2:T(8,128)(2,1)} %copy.30), calls=%async_computation.2 | async-start | bytes 2097152 | tf_op jit(solution)/shard_map/all_to_all | solution.py:63
  125.3 27.9 %copy-start.3 = (f32[3,16384]{1,0:T(4,128)S(1)}, f32[3,16384]{1,0:T(4,128)}, u32[]{:S(2)}) copy-start(f32[3,16384]{1,0:T(4,128)} %param.15) | copy-start | bytes 589828
  125.3 27.9 %copy-start.6 = (f32[3,32]{1,0:T(4,128)S(1)}, f32[3,32]{1,0:T(4,128)}, u32[]{:S(2)}) copy-start(f32[3,32]{1,0:T(4,128)} %param.17) | copy-start | bytes 1156
  125.3 30.0 %all-gather.2.cloned.1.call-start = ((), (), s32[]{:S(2)}) async-start(), calls=%async_computation.5 | async-start | bytes 1179648 | tf_op jit(solution)/shard_map/all_gather | solution.py:84
  126.0 99.3 %all-reduce.2.cloned.1.call-start = ((), (), s32[]{:S(2)}) async-start(), calls=%async_computation.6 | async-start | bytes 2097152 | tf_op jit(solution)/shard_map/psum | solution.py:71
  153.2 72.2 %copy-start.4 = (f32[16384]{0:T(1024)S(1)}, f32[16384]{0:T(1024)}, u32[]{:S(2)}) copy-start(f32[16384]{0:T(1024)} %param.16) | copy-start | bytes 196612
  158.5 72.7 %all-to-all-start = ((bf16[1,32,32,512]{3,1,0,2:T(8,128)(2,1)}), bf16[1,32,32,512]{3,1,0,2:T(8,128)(2,1)S(1)}, u32[]{:S(2)}, u32[]{:S(2)}) async-start(bf16[1,32,32,512]{3,1,0,2:T(8,128)(2,1)} %copy.27), calls=%async_computation | async-start | bytes 2097152 | tf_op jit(solution)/shard_map/all_to_all | solution.py:86
  227.6 3.1 copy-start.2
  233.6 10.5 %copy-start.5 = (s32[8,16]{1,0:T(8,128)S(1)}, s32[8,16]{1,0:T(8,128)}, u32[]{:S(2)}) copy-start(s32[8,16]{1,0:T(8,128)} %param.19) | copy-start | bytes 1540
  233.6 103.0 %all-to-all-start.3 = ((bf16[1,32,32,2048]{3,1,0,2:T(8,128)(2,1)}), bf16[1,32,32,2048]{3,1,0,2:T(8,128)(2,1)}, u32[]{:S(2)}, u32[]{:S(2)}) async-start(bf16[1,32,32,2048]{3,1,0,2:T(8,128)(2,1)} %broadcast_in_dim.49), calls=%async_computation.3 | async-start | bytes 8388608 | tf_op jit(solution)/shard_map/all_to_all | solution.py:93
  243.9 146.1 %reduce-scatter.2.cloned.1.call-start = ((), (), s32[]{:S(2)}) async-start(), calls=%async_computation.7 | async-start | bytes 2359296 | tf_op jit(solution)/shard_map/reduce_scatter | solution.py:108
Sparse Core Ops, SparseCore 0:
  128.0 26.9 all-gather.1
  157.3 68.0 all-reduce.1
  352.8 37.1 reduce-scatter.1
where the time goes:
time: 397 us; the launch traced here: 396 us
  waiting for transfers between devices  208 us (52%)
  blocking collectives  106 us (27%)
  starting transfers between devices  26.6 us (7%)
  matrix products  20.9 us (5%)
  local copies, waits for them, and re-layouts  14.2 us (4%)
  between operations  13.3 us (3%)
  other arithmetic  7.89 us (2%)
    all_to_all x1, blocking collectives, shards(): lax.all_to_all(outgoing, 'grid', split_axis=2, concat_axis=2, tiled=True)  106 us
    all_to_all x1, waiting for transfers between devices, shards(): lax.all_to_all(potential_out, 'grid', split_axis=2, concat_axis=2, tiled=...  86.9 us
    psum x1, waiting for transfers between devices, shards(): lax.psum(partial_term.astype(jnp.bfloat16), 'tile').astype(jnp.float32)  57.2 us
    reduce_scatter x1, waiting for transfers between devices, shards(): lax.psum_scatter(lax.dot_general(region_expansion_factor, exch_tile, (((0...  37.3 us
    all_to_all x1, waiting for transfers between devices, shards(): lax.all_to_all(product.astype(jnp.bfloat16), 'grid', split_axis=2, concat...  25.6 us
    dot_general x1, matrix products, shards(): lax.dot_general(region_expansion_factor, exch_tile, (((0,), (1,)), ((), (...  16 us
    all_to_all x1, starting transfers between devices, shards(): lax.all_to_all(potential_out, 'grid', split_axis=2, concat_axis=2, tiled=...  10.3 us
    all_to_all x1, starting transfers between devices, shards(): lax.all_to_all(whole_points.reshape(batches, batch_points, grid_count, ow...  9.68 us
  transfers between devices with their start and end apart: 6, of which 4 were waited for; matrix products, arithmetic and copies ran while one was open for 5% of the time, Pallas kernels for 0%

commit v1 on v0

v1 whole, which is shorter than its diff:
```python
import jax
import jax.numpy as jnp
from jax import lax
from jax.sharding import PartitionSpec as P

NZ, NY, NT = 8, 4, 8
BP, BLK = 32, 512
bf16, f32 = jnp.bfloat16, jnp.float32


def gid(z, y):
    return (z % NZ) * NY + y % NY


def shift(x, dz, dy):
    pairs = [(gid(z, y), gid(z + dz, y + dy)) for z in range(NZ) for y in range(NY)]
    return lax.ppermute(x, "grid", pairs)


def put(buf, part, index):
    return lax.dynamic_update_slice_in_dim(buf, part[None], index, 0)


def ring(x, n, me, hop):
    buf = put(jnp.zeros((n,) + x.shape, x.dtype), x, me)
    up = down = x
    for s in range(1, (n - 1) // 2 + 1):
        up, down = hop(up, 1), hop(down, -1)
        buf = put(buf, up, (me - s) % n)
        buf = put(buf, down, (me + s) % n)
    h = x.shape[-2] // 2
    last = jnp.concatenate([hop(up[..., :h, :], 1), hop(down[..., h:, :], -1)], -2)
    return put(buf, last, (me + n // 2) % n)


def gather_grid(x, z, y):
    r, c = x.shape
    a, b = x[: r // 2], x[r // 2 :]
    a = ring(a, NY, y, lambda v, d: shift(v, 0, d))
    b = ring(b, NZ, z, lambda v, d: shift(v, d, 0))
    a = ring(a, NZ, z, lambda v, d: shift(v, d, 0))
    b = ring(b, NY, y, lambda v, d: shift(v, 0, d))
    return a, b


def shards(pv, sig, density, core, smask, centers, widths, coords, lmo, dom):
    g, j = lax.axis_index("grid"), lax.axis_index("tile")
    z, y = g // NY, g % NY
    nblk = smask.shape[0]
    ids = jnp.arange(nblk, dtype=jnp.int32)
    named = jnp.any(sig[0][:, None] == ids[None, :], axis=0).astype(f32)
    own = lax.dynamic_slice_in_dim(named, 4 * j, 4, 0)
    masked = pv * jnp.repeat(own, BLK)[None, :].astype(bf16)

    col = jnp.zeros((NY, BP, BLK), bf16)
    for s in range(NY):
        piece = lax.dynamic_slice_in_dim(masked, ((y + s) % NY) * BLK, BLK, 1)
        pairs = [
            (gid(a, b) * NT + t, gid(t, b + s) * NT + a)
            for a in range(NZ)
            for b in range(NY)
            for t in range(NT)
        ]
        piece = lax.ppermute(piece, ("grid", "tile"), pairs)
        col = put(col, piece, (y - s) % NY)
    x_col = lax.all_gather(col.reshape(NY * BP, BLK), "tile", axis=0, tiled=True)

    xa, xb = gather_grid(masked, z, y)
    dot_t = lambda u, v: lax.dot_general(u, v, (((1,), (1,)), ((), ())), preferred_element_type=f32)
    ya = dot_t(xa.reshape(-1, pv.shape[1]), density).astype(bf16).reshape(NZ, NY, 4, 4, BLK)
    yb = dot_t(xb.reshape(-1, pv.shape[1]), density).astype(bf16).reshape(NY, NZ, 4, 4, BLK)
    parts = jnp.concatenate([ya.transpose(2, 0, 1, 3, 4), yb.transpose(2, 1, 0, 3, 4)], 0)
    parts = lax.all_to_all(parts.reshape(NT, 32, 4, BLK), "tile", 0, 0, tiled=True)
    term = jnp.sum(parts.astype(f32), axis=0).astype(bf16)
    term = lax.all_to_all(term, "grid", 0, 0, tiled=True)

    pts = lax.dynamic_slice_in_dim(coords, 4 * j, 4, 1)
    off = centers[:, None, :] - pts[:, :, None]
    coef = 1.0 / jnp.sqrt(jnp.sum(off * off, axis=0) + widths[None, :])
    coef = coef.reshape(4, nblk, BLK).transpose(1, 0, 2) * named[:, None, None]
    weighted = (coef * term.astype(f32)).astype(bf16)
    screened = jnp.einsum("kj,jpa->kpa", smask.astype(bf16), weighted, preferred_element_type=f32)
    mixed = jnp.einsum("kpc,ac->kpa", screened.astype(bf16), core, preferred_element_type=f32)
    pot = (coef * mixed).astype(bf16)
    pot = lax.all_to_all(pot.reshape(NT, 4, 4, BLK), "tile", 0, 0, tiled=True)
    pot = pot.transpose(0, 2, 1, 3).reshape(BP, pv.shape[1])

    local_ids = 4 * j + jnp.arange(4, dtype=jnp.int32)
    in_dom = jnp.any(dom[:, :, None] == local_ids[None, None, :], axis=1).T.astype(bf16)
    dmask = jnp.broadcast_to(in_dom[:, None, :, None], (4, BLK, NT, 256)).reshape(lmo.shape)
    w = jnp.dot(pot, lmo * dmask, preferred_element_type=f32).astype(bf16)
    w = w.reshape(BP, NT, 256).transpose(1, 0, 2)
    w = lax.all_to_all(w, "tile", 0, 0, tiled=True)
    w = jnp.sum(w.astype(f32), axis=0).astype(bf16)
    w_all = lax.all_to_all(jnp.broadcast_to(w[None], (32, BP, 256)), "grid", 0, 0, tiled=True)
    return lax.dot_general(
        w_all.reshape(-1, 256), x_col, (((0,), (0,)), ((), ())), preferred_element_type=f32
    ).astype(bf16)


def solution(mesh):
    in_specs = (
        P("grid", "tile"),
        P("grid", None),
        P("grid", "tile"),
        P(),
        P(),
        P(),
        P(),
        P(None, "grid"),
        P("tile", None),
        P(),
    )
    return jax.shard_map(
        shards, mesh=mesh, in_specs=in_specs, out_specs=P("tile", "grid"), check_vma=False
    )
```

time: 397 us -> 225 us (0.57)
  waiting for transfers between devices: 208 us -> 67.7 us
  blocking collectives: 106 us -> 9.25 us
  starting transfers between devices: 26.6 us -> 79 us
  local copies, waits for them, and re-layouts: 14.2 us -> 32.2 us
  matrix products: 20.9 us -> 16.4 us
    all_to_all x1, blocking collectives: 106 us -> 9.25 us  [shards(): w = lax.all_to_all(w, 'tile', 0, 0, tiled=True)]
    all_to_all x3 -> x4, waiting for transfers between devices: 112 us -> 30.6 us  [the longest x1 17.4 us: shards(): lax.all_to_all(jnp.broadcast_to(w[None], (32, BP, 256)), 'grid', 0, 0, ti...]
    psum x1 -> x0, waiting for transfers between devices: 57.2 us -> none  [shards(): lax.psum(partial_term.astype(jnp.bfloat16), 'tile').astype(jnp.float32)]
    ppermute x0 -> x28, starting transfers between devices: none -> 52.6 us  [the longest x24 43.7 us: shift(): return lax.ppermute(x, 'grid', pairs)]
    reduce_scatter x1 -> x0, waiting for transfers between devices: 37.3 us -> none  [shards(): lax.psum_scatter(lax.dot_general(region_expansion_factor, exch_tile, (((0...]
    ppermute x0 -> x28, waiting for transfers between devices: none -> 37.1 us  [the longest x24 37.1 us: shift(): return lax.ppermute(x, 'grid', pairs)]
    dynamic_update_slice x0 -> x23, local copies, waits for them, and re-layouts: none -> 8.38 us  [put(): return lax.dynamic_update_slice_in_dim(buf, part[None], index, 0)]
    dot_general x4 -> x5, matrix products: 20.9 us -> 16.4 us  [the longest x1 7.48 us: shards(): w = jnp.dot(pot, lmo * dmask, preferred_element_type=f32).astype(bf16)]
  transfers between devices with their start and end apart: 6 -> 33, of which waited for: 4 -> 14; matrix products, arithmetic and copies ran while one was open for 5% -> 22% of each run, Pallas kernels for 0% -> 0%
where the time goes in v1:
time: 225 us; the launch traced here: 224 us
  starting transfers between devices  79 us (35%)
  waiting for transfers between devices  67.7 us (30%)
  local copies, waits for them, and re-layouts  32.2 us (14%)
  matrix products  16.4 us (7%)
  between operations  14.1 us (6%)
  blocking collectives  9.25 us (4%)
  other arithmetic  5.77 us (3%)
    ppermute x24, starting transfers between devices, shift(): return lax.ppermute(x, 'grid', pairs)  43.7 us
    ppermute x24, waiting for transfers between devices, shift(): return lax.ppermute(x, 'grid', pairs)  37.1 us
    all_to_all x1, waiting for transfers between devices, shards(): lax.all_to_all(jnp.broadcast_to(w[None], (32, BP, 256)), 'grid', 0, 0, ti...  17.4 us
    unnamed x22, local copies, waits for them, and re-layouts  11.2 us
    all_to_all x1, starting transfers between devices, shards(): term = lax.all_to_all(term, 'grid', 0, 0, tiled=True)  9.69 us
    all_to_all x1, blocking collectives, shards(): w = lax.all_to_all(w, 'tile', 0, 0, tiled=True)  9.25 us
    ppermute x4, starting transfers between devices, shards(): piece = lax.ppermute(piece, ('grid', 'tile'), pairs)  8.86 us
    all_to_all x1, waiting for transfers between devices, shards(): term = lax.all_to_all(term, 'grid', 0, 0, tiled=True)  8.58 us
  transfers between devices with their start and end apart: 33, of which 14 were waited for; matrix products, arithmetic and copies ran while one was open for 22% of the time, Pallas kernels for 0%

profile of v1, /device:TPU:32, one launch (start us, length us, event | category | flops | bytes accessed | tf_op | source)
XLA Modules:
  0.0 224.4 jit_solution(7172796115749685742)
XLA Ops:
  7.6 0.9 broadcast_multiply_fusion
  8.6 2.0 collective-permute-start.12
  10.7 1.6 collective-permute-start
  12.2 1.7 collective-permute-start.1
  14.6 4.6 %collective-permute-start.24 = (bf16[32,512]{1,0:T(8,128)(2,1)}, bf16[32,512]{1,0:T(8,128)(2,1)}, u32[]{:S(2)}, u32[]{:S(2)}) collective-permute-start(bf16[32,512]{1,0:T(8,128)(2,1)} %get-tuple-element.8), channel_id=1, source_target_pairs={{0,0},{1,32},{2,64},{3,96},{4,128},{5,160},{6,192},{7,224},{8,8},{... | collective-permute-start | bytes 98312 | tf_op jit(solution)/shard_map/ppermute | solution.py:64
  19.6 3.9 %collective-permute-start.26 = (bf16[32,512]{1,0:T(8,128)(2,1)}, bf16[32,512]{1,0:T(8,128)(2,1)}, u32[]{:S(2)}, u32[]{:S(2)}) collective-permute-start(bf16[32,512]{1,0:T(8,128)(2,1)} %get-tuple-element.6), channel_id=1, source_target_pairs={{0,16},{1,48},{2,80},{3,112},{4,144},{5,176},{6,208},{7,240},{8,24... | collective-permute-start | bytes 98312 | tf_op jit(solution)/shard_map/ppermute | solution.py:64
  23.5 1.4 collective-permute-start.3
  25.8 1.8 collective-permute-done.3
  27.5 5.9 %collective-permute-start.14 = (bf16[16,2048]{1,0:T(8,128)(2,1)S(1)}, bf16[16,2048]{1,0:T(8,128)(2,1)S(1)}, u32[]{:S(2)}, u32[]{:S(2)}) collective-permute-start(bf16[16,2048]{1,0:T(8,128)(2,1)S(1)} %collective-permute-done.12), channel_id=1, source_target_pairs={{0,32},{8,40},{16,48},{24,56},{32,64},{40,72},{48,80},{56,88},{64,... | collective-permute-start | bytes 196616 | tf_op jit(solution)/shard_map/ppermute | solution.py:17
  33.4 1.6 broadcast_in_dim.121
  35.7 2.7 %collective-permute-start.16 = (bf16[16,2048]{1,0:T(8,128)(2,1)S(1)}, bf16[16,2048]{1,0:T(8,128)(2,1)S(1)}, u32[]{:S(2)}, u32[]{:S(2)}) collective-permute-start(bf16[16,2048]{1,0:T(8,128)(2,1)S(1)} %collective-permute-done.14), channel_id=1, source_target_pairs={{0,32},{8,40},{16,48},{24,56},{32,64},{40,72},{48,80},{56,88},{64,... | collective-permute-start | bytes 196616 | tf_op jit(solution)/shard_map/ppermute | solution.py:17
  38.4 3.0 %collective-permute-start.17 = (bf16[16,2048]{1,0:T(8,128)(2,1)S(1)}, bf16[16,2048]{1,0:T(8,128)(2,1)S(1)}, u32[]{:S(2)}, u32[]{:S(2)}) collective-permute-start(bf16[16,2048]{1,0:T(8,128)(2,1)S(1)} %collective-permute-done.15), channel_id=1, source_target_pairs={{0,224},{8,232},{16,240},{24,248},{32,0},{40,8},{48,16},{56,24},{6... | collective-permute-start | bytes 196616 | tf_op jit(solution)/shard_map/ppermute | solution.py:17
  41.4 6.8 %collective-permute-done.17 = bf16[16,2048]{1,0:T(8,128)(2,1)S(1)} collective-permute-done((bf16[16,2048]{1,0:T(8,128)(2,1)S(1)}, bf16[16,2048]{1,0:T(8,128)(2,1)S(1)}, u32[]{:S(2)}, u32[]{:S(2)}) %collective-permute-start.17) | collective-permute-done | bytes 65568 | tf_op jit(solution)/shard_map/ppermute | solution.py:17
  48.2 3.3 %collective-permute-start.18 = (bf16[8,2048]{1,0:T(8,128)(2,1)S(1)}, bf16[8,2048]{1,0:T(8,128)(2,1)S(1)}, u32[]{:S(2)}, u32[]{:S(2)}) collective-permute-start(bf16[8,2048]{1,0:T(8,128)(2,1)S(1)} %slice.46), channel_id=1, source_target_pairs={{0,32},{8,40},{16,48},{24,56},{32,64},{40,72},{48,80},{56,88},{64,... | collective-permute-start | bytes 98312 | tf_op jit(solution)/shard_map/ppermute | solution.py:17
  51.5 2.1 collective-permute-done.19
  53.6 3.2 %collective-permute-start.4 = (bf16[4,16,2048]{2,1,0:T(8,128)(2,1)S(1)}, bf16[4,16,2048]{2,1,0:T(8,128)(2,1)S(1)}, u32[]{:S(2)}, u32[]{:S(2)}) collective-permute-start(bf16[4,16,2048]{2,1,0:T(8,128)(2,1)S(1)} %fusion.23), channel_id=1, source_target_pairs={{0,32},{8,40},{16,48},{24,56},{32,64},{40,72},{48,80},{56,88},{64,... | collective-permute-start | bytes 786440 | tf_op jit(solution)/shard_map/ppermute | solution.py:17
  57.2 5.4 %collective-permute-done.4 = bf16[4,16,2048]{2,1,0:T(8,128)(2,1)S(1)} collective-permute-done((bf16[4,16,2048]{2,1,0:T(8,128)(2,1)S(1)}, bf16[4,16,2048]{2,1,0:T(8,128)(2,1)S(1)}, u32[]{:S(2)}, u32[]{:S(2)}) %collective-permute-start.4) | collective-permute-done | bytes 262176 | tf_op jit(solution)/shard_map/ppermute | solution.py:17
  64.1 2.5 %collective-permute-start.6 = (bf16[4,16,2048]{2,1,0:T(8,128)(2,1)S(1)}, bf16[4,16,2048]{2,1,0:T(8,128)(2,1)S(1)}, u32[]{:S(2)}, u32[]{:S(2)}) collective-permute-start(bf16[4,16,2048]{2,1,0:T(8,128)(2,1)S(1)} %collective-permute-done.4), channel_id=1, source_target_pairs={{0,32},{8,40},{16,48},{24,56},{32,64},{40,72},{48,80},{56,88},{64,... | collective-permute-start | bytes 786440 | tf_op jit(solution)/shard_map/ppermute | solution.py:17
  67.3 3.2 %collective-permute-done.6 = bf16[4,16,2048]{2,1,0:T(8,128)(2,1)S(1)} collective-permute-done((bf16[4,16,2048]{2,1,0:T(8,128)(2,1)S(1)}, bf16[4,16,2048]{2,1,0:T(8,128)(2,1)S(1)}, u32[]{:S(2)}, u32[]{:S(2)}) %collective-permute-start.6) | collective-permute-done | bytes 262176 | tf_op jit(solution)/shard_map/ppermute | solution.py:17
  72.0 5.3 %collective-permute-done.7 = bf16[4,16,2048]{2,1,0:T(8,128)(2,1)S(1)} collective-permute-done((bf16[4,16,2048]{2,1,0:T(8,128)(2,1)S(1)}, bf16[4,16,2048]{2,1,0:T(8,128)(2,1)S(1)}, u32[]{:S(2)}, u32[]{:S(2)}) %collective-permute-start.7) | collective-permute-done | bytes 262176 | tf_op jit(solution)/shard_map/ppermute | solution.py:17
  77.3 2.4 %collective-permute-start.21 = (bf16[8,16,2048]{2,1,0:T(8,128)(2,1)S(1)}, bf16[8,16,2048]{2,1,0:T(8,128)(2,1)S(1)}, u32[]{:S(2)}, u32[]{:S(2)}) collective-permute-start(bf16[8,16,2048]{2,1,0:T(8,128)(2,1)S(1)} %fusion.24), channel_id=1, source_target_pairs={{0,24},{8,0},{16,8},{24,16},{32,56},{40,32},{48,40},{56,48},{64,88... | collective-permute-start | bytes 1572872 | tf_op jit(solution)/shard_map/ppermute | solution.py:17
  80.4 2.4 %collective-permute-start.8 = (bf16[4,16,2048]{2,1,0:T(8,128)(2,1)S(1)}, bf16[4,16,2048]{2,1,0:T(8,128)(2,1)S(1)}, u32[]{:S(2)}, u32[]{:S(2)}) collective-permute-start(bf16[4,16,2048]{2,1,0:T(8,128)(2,1)S(1)} %collective-permute-done.6), channel_id=1, source_target_pairs={{0,32},{8,40},{16,48},{24,56},{32,64},{40,72},{48,80},{56,88},{64,... | collective-permute-start | bytes 786440 | tf_op jit(solution)/shard_map/ppermute | solution.py:17
  83.0 6.0 %collective-permute-done.21 = bf16[8,16,2048]{2,1,0:T(8,128)(2,1)S(1)} collective-permute-done((bf16[8,16,2048]{2,1,0:T(8,128)(2,1)S(1)}, bf16[8,16,2048]{2,1,0:T(8,128)(2,1)S(1)}, u32[]{:S(2)}, u32[]{:S(2)}) %collective-permute-start.21) | collective-permute-done | bytes 524320 | tf_op jit(solution)/shard_map/ppermute | solution.py:17
  89.0 1.4 collective-permute-start.9
  90.5 3.8 %collective-permute-start.23 = (bf16[8,8,2048]{2,1,0:T(8,128)(2,1)S(1)}, bf16[8,8,2048]{2,1,0:T(8,128)(2,1)S(1)}, u32[]{:S(2)}, u32[]{:S(2)}) collective-permute-start(bf16[8,8,2048]{2,1,0:T(8,128)(2,1)S(1)} %slice.49), channel_id=1, source_target_pairs={{0,24},{8,0},{16,8},{24,16},{32,56},{40,32},{48,40},{56,48},{64,88... | collective-permute-start | bytes 786440 | tf_op jit(solution)/shard_map/ppermute | solution.py:17
  96.7 1.7 collective-permute-done.23
  98.5 1.1 collective-permute-start.11
  99.5 3.9 %collective-permute-done.22 = bf16[8,8,2048]{2,1,0:T(8,128)(2,1)S(1)} collective-permute-done((bf16[8,8,2048]{2,1,0:T(8,128)(2,1)S(1)}, bf16[8,8,2048]{2,1,0:T(8,128)(2,1)S(1)}, u32[]{:S(2)}, u32[]{:S(2)}) %collective-permute-start.22) | collective-permute-done | bytes 262176 | tf_op jit(solution)/shard_map/ppermute | solution.py:17
  103.4 3.1 %collective-permute-start.10 = (bf16[4,8,2048]{2,1,0:T(8,128)(2,1)S(1)}, bf16[4,8,2048]{2,1,0:T(8,128)(2,1)S(1)}, u32[]{:S(2)}, u32[]{:S(2)}) collective-permute-start(bf16[4,8,2048]{2,1,0:T(8,128)(2,1)S(1)} %slice.43), channel_id=1, source_target_pairs={{0,32},{8,40},{16,48},{24,56},{32,64},{40,72},{48,80},{56,88},{64,... | collective-permute-start | bytes 393224 | tf_op jit(solution)/shard_map/ppermute | solution.py:17
  106.6 1.3 convolution_convert_fusion
  109.8 3.7 %convolution_convert_fusion.1 = bf16[512,512]{1,0:T(8,128)(2,1)} fusion(bf16[512,2048]{1,0:T(8,128)(2,1)} %bitcast.14, bf16[512,2048]{1,0:T(8,128)(2,1)S(1)} %copy-done), kind=kOutput, calls=%fused_computation.4 | convolution fusion | flops 1074003968 | bytes 4718592 | tf_op jit(solution)/shard_map/dot_general | solution.py:69
  113.5 1.2 reshape.63
  115.4 1.6 copy.21
  116.9 7.3 %all-to-all-start = ((bf16[8,32,4,512]{3,2,1,0:T(4,128)(2,1)}), bf16[8,32,4,512]{3,2,1,0:T(4,128)(2,1)S(1)}, u32[]{:S(2)}, u32[]{:S(2)}) async-start(bf16[8,32,4,512]{3,2,1,0:T(4,128)(2,1)} %bitcast.140), calls=%async_computation | async-start | bytes 2097152 | tf_op jit(solution)/shard_map/all_to_all | solution.py:73
  124.6 1.0 multiply_reduce_fusion
  126.2 3.9 %broadcast_in_dim.150 = bf16[4,512,8,256]{3,2,1,0:T(8,128)(2,1)} broadcast(bf16[4,8]{1,0:T(4,128)(2,1)S(1)} %convert_bitcast_fusion), dimensions={0,2} | broadcast | bytes 8388672 | tf_op jit(solution)/shard_map/broadcast_in_dim | solution.py:90
  130.1 10.4 %copy.31 = bf16[256,8,8,256]{3,1,2,0:T(8,128)(2,1)} copy(bf16[256,8,8,256]{3,2,1,0:T(8,128)(2,1)} %bitcast.139) | data formatting | bytes 16777216
  141.3 1.2 reduce_sum.37
  142.5 9.7 %all-to-all-start.1 = ((bf16[32,4,512]{2,1,0:T(4,128)(2,1)}), bf16[32,4,512]{2,1,0:T(4,128)(2,1)S(1)}, u32[]{:S(2)}, u32[]{:S(2)}) async-start(bf16[32,4,512]{2,1,0:T(4,128)(2,1)} %reduce_sum.37), calls=%async_computation.1 | async-start | bytes 262144 | tf_op jit(solution)/shard_map/all_to_all | solution.py:75
  153.7 8.6 %all-to-all-done.1 = bf16[32,4,512]{2,1,0:T(4,128)(2,1)S(1)} async-done(((bf16[32,4,512]{2,1,0:T(4,128)(2,1)}), bf16[32,4,512]{2,1,0:T(4,128)(2,1)S(1)}, u32[]{:S(2)}, u32[]{:S(2)}) %all-to-all-start.1) | async-done | bytes 131104 | tf_op jit(solution)/shard_map/all_to_all | solution.py:75
  162.3 1.5 fusion.5
  164.6 4.4 %all-to-all-start.2 = ((bf16[8,4,4,512]{3,1,2,0:T(4,128)(2,1)}), bf16[8,4,4,512]{3,1,2,0:T(4,128)(2,1)S(1)}, u32[]{:S(2)}, u32[]{:S(2)}) async-start(bf16[8,4,4,512]{3,1,2,0:T(4,128)(2,1)} %copy.24), calls=%async_computation.2 | async-start | bytes 262144 | tf_op jit(solution)/shard_map/all_to_all | solution.py:85
  170.6 4.6 %all-to-all-done.2 = bf16[8,4,4,512]{3,1,2,0:T(4,128)(2,1)S(1)} async-done(((bf16[8,4,4,512]{3,1,2,0:T(4,128)(2,1)}), bf16[8,4,4,512]{3,1,2,0:T(4,128)(2,1)S(1)}, u32[]{:S(2)}, u32[]{:S(2)}) %all-to-all-start.2) | async-done | bytes 131104 | tf_op jit(solution)/shard_map/all_to_all | solution.py:85
  175.2 7.5 %fusion.2 = bf16[32,2048]{1,0:T(8,128)(2,1)S(1)} fusion(bf16[32,2048]{1,0:T(8,128)(2,1)S(1)} %bitcast.144, bf16[2048,2048]{1,0:T(8,128)(2,1)} %param.18, bf16[2048,2048]{1,0:T(8,128)(2,1)} %bitcast.138), kind=kOutput, calls=%fused_computation.2 | convolution fusion | flops 272695296 | bytes 17039360 | tf_op jit(solution)/shard_map/dot_general | solution.py:91
  182.7 9.2 %all_to_all.25 = bf16[8,32,256]{2,1,0:T(8,128)(2,1)S(1)} all-to-all(bf16[8,32,256]{2,1,0:T(8,128)(2,1)S(1)} %bitcast.149), channel_id=1, replica_groups=mesh['grid'=32,'tile'=8] {'tile'}, dimensions={0} | all-to-all | bytes 262144 | tf_op jit(solution)/shard_map/all_to_all | solution.py:93
  192.9 4.9 %all-to-all-start.4 = ((bf16[32,32,256]{2,1,0:T(8,128)(2,1)}), bf16[32,32,256]{2,1,0:T(8,128)(2,1)S(1)}, u32[]{:S(2)}, u32[]{:S(2)}) async-start(bf16[32,32,256]{2,1,0:T(8,128)(2,1)} %broadcast_in_dim.151), calls=%async_computation.4 | async-start | bytes 1048576 | tf_op jit(solution)/shard_map/all_to_all | solution.py:95
  197.8 17.4 %all-to-all-done.4 = bf16[32,32,256]{2,1,0:T(8,128)(2,1)S(1)} async-done(((bf16[32,32,256]{2,1,0:T(8,128)(2,1)}), bf16[32,32,256]{2,1,0:T(8,128)(2,1)S(1)}, u32[]{:S(2)}, u32[]{:S(2)}) %all-to-all-start.4) | async-done | bytes 524320 | tf_op jit(solution)/shard_map/all_to_all | solution.py:95
  215.2 2.4 %convolution_convert_fusion.2 = bf16[256,512]{1,0:T(8,128)(2,1)} fusion(bf16[1024,256]{1,0:T(8,128)(2,1)S(1)} %bitcast.146, bf16[1024,512]{1,0:T(8,128)(2,1)} %all-gather.2.cloned.1.call-done), kind=kOutput, calls=%fused_computation.5 | convolution fusion | flops 268566528 | bytes 1835008 | tf_op jit(solution)/shard_map/dot_general | solution.py:96
  (111 shorter events, 20.1 us)
Async XLA Ops:
  6.5 100.1 %copy-start = (bf16[512,2048]{1,0:T(8,128)(2,1)S(1)}, bf16[512,2048]{1,0:T(8,128)(2,1)}, u32[]{:S(2)}) copy-start(bf16[512,2048]{1,0:T(8,128)(2,1)} %param.12) | copy-start | bytes 6291460
  7.4 11.7 %copy-start.8 = (f32[32]{0:T(128)}, f32[32]{0:T(128)S(1)}, u32[]{:S(2)}) copy-start(f32[32]{0:T(128)S(1)} %convert_element_type.59) | copy-start | bytes 388
  8.6 15.0 %collective-permute-start.12 = (bf16[16,2048]{1,0:T(8,128)(2,1)S(1)}, bf16[16,2048]{1,0:T(8,128)(2,1)S(1)}, u32[]{:S(2)}, u32[]{:S(2)}) collective-permute-start(bf16[16,2048]{1,0:T(8,128)(2,1)S(1)} %get-tuple-element.10), channel_id=1, source_target_pairs={{0,32},{8,40},{16,48},{24,56},{32,64},{40,72},{48,80},{56,88},{64,... | collective-permute-start | bytes 196616 | tf_op jit(solution)/shard_map/ppermute | solution.py:17
  10.5 14.4 %collective-permute-start.13 = (bf16[16,2048]{1,0:T(8,128)(2,1)S(1)}, bf16[16,2048]{1,0:T(8,128)(2,1)S(1)}, u32[]{:S(2)}, u32[]{:S(2)}) collective-permute-start(bf16[16,2048]{1,0:T(8,128)(2,1)S(1)} %get-tuple-element.10), channel_id=1, source_target_pairs={{0,224},{8,232},{16,240},{24,248},{32,0},{40,8},{48,16},{56,24},{6... | collective-permute-start | bytes 196616 | tf_op jit(solution)/shard_map/ppermute | solution.py:17
  10.7 8.8 %collective-permute-start = (bf16[16,2048]{1,0:T(8,128)(2,1)S(1)}, bf16[16,2048]{1,0:T(8,128)(2,1)S(1)}, u32[]{:S(2)}, u32[]{:S(2)}) collective-permute-start(bf16[16,2048]{1,0:T(8,128)(2,1)S(1)} %get-tuple-element.9), channel_id=1, source_target_pairs={{0,8},{8,16},{16,24},{24,0},{32,40},{40,48},{48,56},{56,32},{64,72... | collective-permute-start | bytes 196616 | tf_op jit(solution)/shard_map/ppermute | solution.py:17
  12.2 7.4 %collective-permute-start.1 = (bf16[16,2048]{1,0:T(8,128)(2,1)S(1)}, bf16[16,2048]{1,0:T(8,128)(2,1)S(1)}, u32[]{:S(2)}, u32[]{:S(2)}) collective-permute-start(bf16[16,2048]{1,0:T(8,128)(2,1)S(1)} %get-tuple-element.9), channel_id=1, source_target_pairs={{0,24},{8,0},{16,8},{24,16},{32,56},{40,32},{48,40},{56,48},{64,88... | collective-permute-start | bytes 196616 | tf_op jit(solution)/shard_map/ppermute | solution.py:17
  14.6 125.9 %collective-permute-start.24 = (bf16[32,512]{1,0:T(8,128)(2,1)}, bf16[32,512]{1,0:T(8,128)(2,1)}, u32[]{:S(2)}, u32[]{:S(2)}) collective-permute-start(bf16[32,512]{1,0:T(8,128)(2,1)} %get-tuple-element.8), channel_id=1, source_target_pairs={{0,0},{1,32},{2,64},{3,96},{4,128},{5,160},{6,192},{7,224},{8,8},{... | collective-permute-start | bytes 98312 | tf_op jit(solution)/shard_map/ppermute | solution.py:64
  19.5 132.7 %collective-permute-start.25 = (bf16[32,512]{1,0:T(8,128)(2,1)}, bf16[32,512]{1,0:T(8,128)(2,1)}, u32[]{:S(2)}, u32[]{:S(2)}) collective-permute-start(bf16[32,512]{1,0:T(8,128)(2,1)} %get-tuple-element.7), channel_id=1, source_target_pairs={{0,8},{1,40},{2,72},{3,104},{4,136},{5,168},{6,200},{7,232},{8,16}... | collective-permute-start | bytes 98312 | tf_op jit(solution)/shard_map/ppermute | solution.py:64
  19.6 133.4 %collective-permute-start.26 = (bf16[32,512]{1,0:T(8,128)(2,1)}, bf16[32,512]{1,0:T(8,128)(2,1)}, u32[]{:S(2)}, u32[]{:S(2)}) collective-permute-start(bf16[32,512]{1,0:T(8,128)(2,1)} %get-tuple-element.6), channel_id=1, source_target_pairs={{0,16},{1,48},{2,80},{3,112},{4,144},{5,176},{6,208},{7,240},{8,24... | collective-permute-start | bytes 98312 | tf_op jit(solution)/shard_map/ppermute | solution.py:64
  23.5 4.0 %collective-permute-start.3 = (bf16[8,2048]{1,0:T(8,128)(2,1)S(1)}, bf16[8,2048]{1,0:T(8,128)(2,1)S(1)}, u32[]{:S(2)}, u32[]{:S(2)}) collective-permute-start(bf16[8,2048]{1,0:T(8,128)(2,1)S(1)} %slice.42), channel_id=1, source_target_pairs={{0,24},{8,0},{16,8},{24,16},{32,56},{40,32},{48,40},{56,48},{64,88... | collective-permute-start | bytes 98312 | tf_op jit(solution)/shard_map/ppermute | solution.py:17
  25.0 8.4 %collective-permute-start.2 = (bf16[8,2048]{1,0:T(8,128)(2,1)S(1)}, bf16[8,2048]{1,0:T(8,128)(2,1)S(1)}, u32[]{:S(2)}, u32[]{:S(2)}) collective-permute-start(bf16[8,2048]{1,0:T(8,128)(2,1)S(1)} %slice.41), channel_id=1, source_target_pairs={{0,8},{8,16},{16,24},{24,0},{32,40},{40,48},{48,56},{56,32},{64,72... | collective-permute-start | bytes 98312 | tf_op jit(solution)/shard_map/ppermute | solution.py:17
  27.5 8.2 %collective-permute-start.14 = (bf16[16,2048]{1,0:T(8,128)(2,1)S(1)}, bf16[16,2048]{1,0:T(8,128)(2,1)S(1)}, u32[]{:S(2)}, u32[]{:S(2)}) collective-permute-start(bf16[16,2048]{1,0:T(8,128)(2,1)S(1)} %collective-permute-done.12), channel_id=1, source_target_pairs={{0,32},{8,40},{16,48},{24,56},{32,64},{40,72},{48,80},{56,88},{64,... | collective-permute-start | bytes 196616 | tf_op jit(solution)/shard_map/ppermute | solution.py:17
  33.4 5.0 %collective-permute-start.15 = (bf16[16,2048]{1,0:T(8,128)(2,1)S(1)}, bf16[16,2048]{1,0:T(8,128)(2,1)S(1)}, u32[]{:S(2)}, u32[]{:S(2)}) collective-permute-start(bf16[16,2048]{1,0:T(8,128)(2,1)S(1)} %collective-permute-done.13), channel_id=1, source_target_pairs={{0,224},{8,232},{16,240},{24,248},{32,0},{40,8},{48,16},{56,24},{6... | collective-permute-start | bytes 196616 | tf_op jit(solution)/shard_map/ppermute | solution.py:17
  35.7 12.5 %collective-permute-start.16 = (bf16[16,2048]{1,0:T(8,128)(2,1)S(1)}, bf16[16,2048]{1,0:T(8,128)(2,1)S(1)}, u32[]{:S(2)}, u32[]{:S(2)}) collective-permute-start(bf16[16,2048]{1,0:T(8,128)(2,1)S(1)} %collective-permute-done.14), channel_id=1, source_target_pairs={{0,32},{8,40},{16,48},{24,56},{32,64},{40,72},{48,80},{56,88},{64,... | collective-permute-start | bytes 196616 | tf_op jit(solution)/shard_map/ppermute | solution.py:17
  38.4 9.8 %collective-permute-start.17 = (bf16[16,2048]{1,0:T(8,128)(2,1)S(1)}, bf16[16,2048]{1,0:T(8,128)(2,1)S(1)}, u32[]{:S(2)}, u32[]{:S(2)}) collective-permute-start(bf16[16,2048]{1,0:T(8,128)(2,1)S(1)} %collective-permute-done.15), channel_id=1, source_target_pairs={{0,224},{8,232},{16,240},{24,248},{32,0},{40,8},{48,16},{56,24},{6... | collective-permute-start | bytes 196616 | tf_op jit(solution)/shard_map/ppermute | solution.py:17
  48.2 5.5 %collective-permute-start.19 = (bf16[8,2048]{1,0:T(8,128)(2,1)S(1)}, bf16[8,2048]{1,0:T(8,128)(2,1)S(1)}, u32[]{:S(2)}, u32[]{:S(2)}) collective-permute-start(bf16[8,2048]{1,0:T(8,128)(2,1)S(1)} %slice.47), channel_id=1, source_target_pairs={{0,224},{8,232},{16,240},{24,248},{32,0},{40,8},{48,16},{56,24},{6... | collective-permute-start | bytes 98312 | tf_op jit(solution)/shard_map/ppermute | solution.py:17
  48.2 8.6 %collective-permute-start.18 = (bf16[8,2048]{1,0:T(8,128)(2,1)S(1)}, bf16[8,2048]{1,0:T(8,128)(2,1)S(1)}, u32[]{:S(2)}, u32[]{:S(2)}) collective-permute-start(bf16[8,2048]{1,0:T(8,128)(2,1)S(1)} %slice.46), channel_id=1, source_target_pairs={{0,32},{8,40},{16,48},{24,56},{32,64},{40,72},{48,80},{56,88},{64,... | collective-permute-start | bytes 98312 | tf_op jit(solution)/shard_map/ppermute | solution.py:17
  53.6 8.9 %collective-permute-start.4 = (bf16[4,16,2048]{2,1,0:T(8,128)(2,1)S(1)}, bf16[4,16,2048]{2,1,0:T(8,128)(2,1)S(1)}, u32[]{:S(2)}, u32[]{:S(2)}) collective-permute-start(bf16[4,16,2048]{2,1,0:T(8,128)(2,1)S(1)} %fusion.23), channel_id=1, source_target_pairs={{0,32},{8,40},{16,48},{24,56},{32,64},{40,72},{48,80},{56,88},{64,... | collective-permute-start | bytes 786440 | tf_op jit(solution)/shard_map/ppermute | solution.py:17
  56.8 7.3 %collective-permute-start.5 = (bf16[4,16,2048]{2,1,0:T(8,128)(2,1)S(1)}, bf16[4,16,2048]{2,1,0:T(8,128)(2,1)S(1)}, u32[]{:S(2)}, u32[]{:S(2)}) collective-permute-start(bf16[4,16,2048]{2,1,0:T(8,128)(2,1)S(1)} %fusion.23), channel_id=1, source_target_pairs={{0,224},{8,232},{16,240},{24,248},{32,0},{40,8},{48,16},{56,24},{6... | collective-permute-start | bytes 786440 | tf_op jit(solution)/shard_map/ppermute | solution.py:17
  62.5 17.9 %collective-permute-start.20 = (bf16[8,16,2048]{2,1,0:T(8,128)(2,1)S(1)}, bf16[8,16,2048]{2,1,0:T(8,128)(2,1)S(1)}, u32[]{:S(2)}, u32[]{:S(2)}) collective-permute-start(bf16[8,16,2048]{2,1,0:T(8,128)(2,1)S(1)} %fusion.24), channel_id=1, source_target_pairs={{0,8},{8,16},{16,24},{24,0},{32,40},{40,48},{48,56},{56,32},{64,72... | collective-permute-start | bytes 1572872 | tf_op jit(solution)/shard_map/ppermute | solution.py:17
  64.1 6.4 %collective-permute-start.6 = (bf16[4,16,2048]{2,1,0:T(8,128)(2,1)S(1)}, bf16[4,16,2048]{2,1,0:T(8,128)(2,1)S(1)}, u32[]{:S(2)}, u32[]{:S(2)}) collective-permute-start(bf16[4,16,2048]{2,1,0:T(8,128)(2,1)S(1)} %collective-permute-done.4), channel_id=1, source_target_pairs={{0,32},{8,40},{16,48},{24,56},{32,64},{40,72},{48,80},{56,88},{64,... | collective-permute-start | bytes 786440 | tf_op jit(solution)/shard_map/ppermute | solution.py:17
  70.5 6.8 %collective-permute-start.7 = (bf16[4,16,2048]{2,1,0:T(8,128)(2,1)S(1)}, bf16[4,16,2048]{2,1,0:T(8,128)(2,1)S(1)}, u32[]{:S(2)}, u32[]{:S(2)}) collective-permute-start(bf16[4,16,2048]{2,1,0:T(8,128)(2,1)S(1)} %collective-permute-done.5), channel_id=1, source_target_pairs={{0,224},{8,232},{16,240},{24,248},{32,0},{40,8},{48,16},{56,24},{6... | collective-permute-start | bytes 786440 | tf_op jit(solution)/shard_map/ppermute | solution.py:17
  77.3 11.7 %collective-permute-start.21 = (bf16[8,16,2048]{2,1,0:T(8,128)(2,1)S(1)}, bf16[8,16,2048]{2,1,0:T(8,128)(2,1)S(1)}, u32[]{:S(2)}, u32[]{:S(2)}) collective-permute-start(bf16[8,16,2048]{2,1,0:T(8,128)(2,1)S(1)} %fusion.24), channel_id=1, source_target_pairs={{0,24},{8,0},{16,8},{24,16},{32,56},{40,32},{48,40},{56,48},{64,88... | collective-permute-start | bytes 1572872 | tf_op jit(solution)/shard_map/ppermute | solution.py:17
  80.4 10.0 %collective-permute-start.8 = (bf16[4,16,2048]{2,1,0:T(8,128)(2,1)S(1)}, bf16[4,16,2048]{2,1,0:T(8,128)(2,1)S(1)}, u32[]{:S(2)}, u32[]{:S(2)}) collective-permute-start(bf16[4,16,2048]{2,1,0:T(8,128)(2,1)S(1)} %collective-permute-done.6), channel_id=1, source_target_pairs={{0,32},{8,40},{16,48},{24,56},{32,64},{40,72},{48,80},{56,88},{64,... | collective-permute-start | bytes 786440 | tf_op jit(solution)/shard_map/ppermute | solution.py:17
  89.0 6.4 %collective-permute-start.9 = (bf16[4,16,2048]{2,1,0:T(8,128)(2,1)S(1)}, bf16[4,16,2048]{2,1,0:T(8,128)(2,1)S(1)}, u32[]{:S(2)}, u32[]{:S(2)}) collective-permute-start(bf16[4,16,2048]{2,1,0:T(8,128)(2,1)S(1)} %collective-permute-done.7), channel_id=1, source_target_pairs={{0,224},{8,232},{16,240},{24,248},{32,0},{40,8},{48,16},{56,24},{6... | collective-permute-start | bytes 786440 | tf_op jit(solution)/shard_map/ppermute | solution.py:17
  90.5 8.0 %collective-permute-start.23 = (bf16[8,8,2048]{2,1,0:T(8,128)(2,1)S(1)}, bf16[8,8,2048]{2,1,0:T(8,128)(2,1)S(1)}, u32[]{:S(2)}, u32[]{:S(2)}) collective-permute-start(bf16[8,8,2048]{2,1,0:T(8,128)(2,1)S(1)} %slice.49), channel_id=1, source_target_pairs={{0,24},{8,0},{16,8},{24,16},{32,56},{40,32},{48,40},{56,48},{64,88... | collective-permute-start | bytes 786440 | tf_op jit(solution)/shard_map/ppermute | solution.py:17
  95.3 8.0 %collective-permute-start.22 = (bf16[8,8,2048]{2,1,0:T(8,128)(2,1)S(1)}, bf16[8,8,2048]{2,1,0:T(8,128)(2,1)S(1)}, u32[]{:S(2)}, u32[]{:S(2)}) collective-permute-start(bf16[8,8,2048]{2,1,0:T(8,128)(2,1)S(1)} %slice.48), channel_id=1, source_target_pairs={{0,8},{8,16},{16,24},{24,0},{32,40},{40,48},{48,56},{56,32},{64,72... | collective-permute-start | bytes 786440 | tf_op jit(solution)/shard_map/ppermute | solution.py:17
  98.5 9.8 %collective-permute-start.11 = (bf16[4,8,2048]{2,1,0:T(8,128)(2,1)}, bf16[4,8,2048]{2,1,0:T(8,128)(2,1)S(1)}, u32[]{:S(2)}, u32[]{:S(2)}) collective-permute-start(bf16[4,8,2048]{2,1,0:T(8,128)(2,1)} %slice.44), channel_id=1, source_target_pairs={{0,224},{8,232},{16,240},{24,248},{32,0},{40,8},{48,16},{56,24},{6... | collective-permute-start | bytes 393224 | tf_op jit(solution)/shard_map/ppermute | solution.py:17
  103.4 5.7 %collective-permute-start.10 = (bf16[4,8,2048]{2,1,0:T(8,128)(2,1)S(1)}, bf16[4,8,2048]{2,1,0:T(8,128)(2,1)S(1)}, u32[]{:S(2)}, u32[]{:S(2)}) collective-permute-start(bf16[4,8,2048]{2,1,0:T(8,128)(2,1)S(1)} %slice.43), channel_id=1, source_target_pairs={{0,32},{8,40},{16,48},{24,56},{32,64},{40,72},{48,80},{56,88},{64,... | collective-permute-start | bytes 393224 | tf_op jit(solution)/shard_map/ppermute | solution.py:17
  108.3 60.8 %collective-permute-start.27 = (bf16[32,512]{1,0:T(8,128)(2,1)}, bf16[32,512]{1,0:T(8,128)(2,1)}, u32[]{:S(2)}, u32[]{:S(2)}) collective-permute-start(bf16[32,512]{1,0:T(8,128)(2,1)} %get-tuple-element.5), channel_id=1, source_target_pairs={{0,24},{1,56},{2,88},{3,120},{4,152},{5,184},{6,216},{7,248},{8,0}... | collective-permute-start | bytes 98312 | tf_op jit(solution)/shard_map/ppermute | solution.py:64
  115.3 9.0 %copy-start.6 = (f32[3,32]{1,0:T(4,128)S(1)}, f32[3,32]{1,0:T(4,128)}, u32[]{:S(2)}) copy-start(f32[3,32]{1,0:T(4,128)} %param.17) | copy-start | bytes 1156
  115.3 9.0 %copy-start.5 = (s32[8,16]{1,0:T(8,128)S(1)}, s32[8,16]{1,0:T(8,128)}, u32[]{:S(2)}) copy-start(s32[8,16]{1,0:T(8,128)} %param.19) | copy-start | bytes 1540
  115.3 9.2 %copy-start.2 = (f32[3,16384]{1,0:T(4,128)S(1)}, f32[3,16384]{1,0:T(4,128)}, u32[]{:S(2)}) copy-start(f32[3,16384]{1,0:T(4,128)} %param.15) | copy-start | bytes 589828
  115.3 10.3 %copy-start.4 = (f32[16384]{0:T(1024)S(1)}, f32[16384]{0:T(1024)}, u32[]{:S(2)}) copy-start(f32[16384]{0:T(1024)} %param.16) | copy-start | bytes 196612
  116.9 24.4 %all-to-all-start = ((bf16[8,32,4,512]{3,2,1,0:T(4,128)(2,1)}), bf16[8,32,4,512]{3,2,1,0:T(4,128)(2,1)S(1)}, u32[]{:S(2)}, u32[]{:S(2)}) async-start(bf16[8,32,4,512]{3,2,1,0:T(4,128)(2,1)} %bitcast.140), calls=%async_computation | async-start | bytes 2097152 | tf_op jit(solution)/shard_map/all_to_all | solution.py:73
  130.1 32.2 %copy-start.3 = (f32[4,16384]{1,0:T(4,128)S(1)}, f32[4,16384]{1,0:T(4,128)}, u32[]{:S(2)}) copy-start(f32[4,16384]{1,0:T(4,128)} %multiply_reduce_fusion) | copy-start | bytes 786436
  130.1 32.2 %copy-start.7 = (s32[32,32]{1,0:T(8,128)S(1)}, s32[32,32]{1,0:T(8,128)}, u32[]{:S(2)}) copy-start(s32[32,32]{1,0:T(8,128)} %param.14) | copy-start | bytes 12292
  142.5 19.8 %all-to-all-start.1 = ((bf16[32,4,512]{2,1,0:T(4,128)(2,1)}), bf16[32,4,512]{2,1,0:T(4,128)(2,1)S(1)}, u32[]{:S(2)}, u32[]{:S(2)}) async-start(bf16[32,4,512]{2,1,0:T(4,128)(2,1)} %reduce_sum.37), calls=%async_computation.1 | async-start | bytes 262144 | tf_op jit(solution)/shard_map/all_to_all | solution.py:75
  164.6 10.6 %all-to-all-start.2 = ((bf16[8,4,4,512]{3,1,2,0:T(4,128)(2,1)}), bf16[8,4,4,512]{3,1,2,0:T(4,128)(2,1)S(1)}, u32[]{:S(2)}, u32[]{:S(2)}) async-start(bf16[8,4,4,512]{3,1,2,0:T(4,128)(2,1)} %copy.24), calls=%async_computation.2 | async-start | bytes 262144 | tf_op jit(solution)/shard_map/all_to_all | solution.py:85
  169.1 28.7 %all-gather.2.cloned.1.call-start = ((), (), s32[]{:S(2)}) async-start(), calls=%async_computation.5 | async-start | bytes 1179648 | tf_op jit(solution)/shard_map/all_gather | solution.py:66
  169.9 0.7 copy-start.1
  192.9 22.3 %all-to-all-start.4 = ((bf16[32,32,256]{2,1,0:T(8,128)(2,1)}), bf16[32,32,256]{2,1,0:T(8,128)(2,1)S(1)}, u32[]{:S(2)}, u32[]{:S(2)}) async-start(bf16[32,32,256]{2,1,0:T(8,128)(2,1)} %broadcast_in_dim.151), calls=%async_computation.4 | async-start | bytes 1048576 | tf_op jit(solution)/shard_map/all_to_all | solution.py:95
Sparse Core Ops, SparseCore 0:
  171.8 22.5 all-gather.1

commit v2 on v1

v2 whole, which is shorter than its diff:
```python
import jax
import jax.numpy as jnp
from jax import lax
from jax.sharding import PartitionSpec as P

NZ, NY, NT = 8, 4, 8
BP, BLK = 32, 512
QP = 4
bf16, f32 = jnp.bfloat16, jnp.float32
Y_GROUPS = [[z * NY + y for y in range(NY)] for z in range(NZ)]
tie = lax.optimization_barrier


def along_z(x, d):
    pairs = [(z * NY + y, (z + d) % NZ * NY + y) for z in range(NZ) for y in range(NY)]
    return lax.ppermute(x, "grid", pairs)


def permute_all(x, dest):
    pairs = []
    for z in range(NZ):
        for y in range(NY):
            for t in range(NT):
                a, b, c = dest(z, y, t)
                pairs.append(((z * NY + y) * NT + t, (a * NY + b) * NT + c))
    return lax.ppermute(x, ("grid", "tile"), pairs)


def spread(x, axis, n, groups=None):
    copies = jnp.broadcast_to(x[None], (n,) + x.shape)
    return lax.all_to_all(copies, axis, 0, 0, tiled=True, axis_index_groups=groups)


def dot(u, v, cu, cv):
    return lax.dot_general(u, v, (((cu,), (cv,)), ((), ())), preferred_element_type=f32)


def shards(pv, sig, density, core, smask, centers, widths, coords, lmo, dom):
    g, j = lax.axis_index("grid"), lax.axis_index("tile")
    z, y = g // NY, g % NY
    nblk = smask.shape[0]
    cols = pv.shape[1]
    ids = jnp.arange(nblk, dtype=jnp.int32)
    named = jnp.any(sig[0][:, None] == ids[None, :], axis=0).astype(f32)
    own = lax.dynamic_slice_in_dim(named, 4 * j, 4, 0)
    masked = pv * jnp.repeat(own, BLK)[None, :].astype(bf16)

    xy = spread(masked, "grid", NY, Y_GROUPS)
    info = jnp.concatenate([named, coords.reshape(-1)])[None]
    piece = lax.dynamic_slice_in_dim(xy, y * BLK, BLK, 2).reshape(NY * BP, BLK)

    parts = jnp.zeros((NZ, NY * BP, BLK), bf16)

    def put(parts, x, s, row=0):
        rows = dot(x.reshape(-1, cols), density, 1, 1).astype(bf16)
        return lax.dynamic_update_slice(parts, rows[None], ((z - s) % NZ, row, 0))

    up = down = xy
    parts = put(parts, xy, 0)
    for s in range(1, 4):
        up, down = along_z(up, 1), along_z(down, -1)
        if s == 1:
            info, up, down = tie((info, up, down))
            info = permute_all(info, lambda a, b, c: (2 * b + c // 4, c % 4, a))[0]
        if s == 3:
            piece, up, down = tie((piece, up, down))
            piece = permute_all(piece, lambda a, b, c: (c, b, a))
        parts = put(put(parts, up, s), down, -s)
    up, down = along_z(up[: NY // 2], 1), along_z(down[NY // 2 :], -1)
    parts = put(put(parts, up, 4), down, 4, NY * BP // 2)

    named = info[:nblk]
    pts = lax.dynamic_slice_in_dim(info[nblk:].reshape(3, BP), QP * (g % 8), QP, 1)
    off = centers.reshape(3, nblk, 1, BLK) - pts.reshape(3, 1, QP, 1)
    coef = 1.0 / jnp.sqrt(jnp.sum(off * off, axis=0) + widths.reshape(nblk, 1, BLK))
    coef = coef * named[:, None, None]

    local_ids = 4 * j + jnp.arange(4, dtype=jnp.int32)
    in_dom = jnp.any(dom[:, :, None] == local_ids[None, None, :], axis=1).T.astype(bf16)
    dmask = jnp.broadcast_to(in_dom[:, None, :, None], (4, BLK, NT, 256)).reshape(lmo.shape)
    region = lmo * dmask
    parts, coef, region = tie((parts, coef, region))

    parts = lax.all_to_all(parts, "tile", 0, 0, tiled=True)
    term = jnp.sum(parts.astype(f32), axis=0).astype(bf16).reshape(NZ * NY, QP, BLK)
    term = lax.all_to_all(term, "grid", 0, 0, tiled=True)

    weighted = (coef * term.astype(f32)).astype(bf16)
    screened = jnp.einsum("kj,jpa->kpa", smask.astype(bf16), weighted, preferred_element_type=f32)
    mixed = jnp.einsum("kpc,ac->kpa", screened.astype(bf16), core, preferred_element_type=f32)
    pot = (coef * mixed).astype(bf16)
    pot = lax.all_to_all(pot.reshape(NT, 4, QP, BLK), "tile", 0, 0, tiled=True)
    pot = pot.transpose(0, 2, 1, 3).reshape(NT * QP, cols)

    w = dot(pot, region, 1, 0).astype(bf16)
    w = w.reshape(NT * QP, NT, 256).transpose(1, 0, 2)
    w = lax.all_to_all(w, "tile", 0, 0, tiled=True)
    w = jnp.sum(w.astype(f32), axis=0).astype(bf16)
    w_all = spread(w, "grid", NZ * NY).reshape(-1, 256)

    x_col = lax.all_gather(piece, "tile", axis=0, tiled=True)
    x_col = x_col.reshape(NZ, NY, 8, QP, BLK).transpose(1, 2, 0, 3, 4).reshape(-1, BLK)
    return dot(w_all, x_col, 0, 0).astype(bf16)


def solution(mesh):
    in_specs = (
        P("grid", "tile"),
        P("grid", None),
        P("grid", "tile"),
        P(),
        P(),
        P(),
        P(),
        P(None, "grid"),
        P("tile", None),
        P(),
    )
    return jax.shard_map(
        shards, mesh=mesh, in_specs=in_specs, out_specs=P("tile", "grid"), check_vma=False
    )
```

time: 225 us -> 203 us (0.902)
  starting transfers between devices: 79 us -> 39.1 us
  blocking collectives: 9.25 us -> 43.7 us
  waiting for transfers between devices: 67.7 us -> 47.4 us
  other arithmetic: 5.77 us -> 14.3 us
  local copies, waits for them, and re-layouts: 32.2 us -> 23.8 us
  matrix products: 16.4 us -> 20.1 us
    ppermute x28 -> x10, starting transfers between devices: 52.6 us -> 16.8 us  [the longest x8 12.7 us: along_z(): return lax.ppermute(x, 'grid', pairs)]
    all_to_all x0 -> x2, blocking collectives: none -> 35.1 us  [the longest x1 19.6 us: shards(): parts = lax.all_to_all(parts, 'tile', 0, 0, tiled=True)]
    ppermute x28 -> x10, waiting for transfers between devices: 37.1 us -> 23.3 us  [the longest x2 11.9 us: permute_all(): return lax.ppermute(x, ('grid', 'tile'), pairs)]
    mul x0 -> x2, other arithmetic: none -> 10.6 us  [the longest x1 10.5 us: shards(): region = lmo * dmask]
    dynamic_update_slice x23 -> x0, local copies, waits for them, and re-layouts: 8.38 us -> none  [put(): return lax.dynamic_update_slice_in_dim(buf, part[None], index, 0)]
    all_to_all x1, waiting for transfers between devices: 8.58 us -> 1.76 us  [shards(): term = lax.all_to_all(term, 'grid', 0, 0, tiled=True)]
    dot_general x4 -> x11, matrix products: 14.8 us -> 19.8 us  [dot(): lax.dot_general(u, v, (((cu,), (cv,)), ((), ())), preferred_element_type=...]
    all_to_all x3 -> x2, starting transfers between devices: 16.7 us -> 12.9 us  [spread(): lax.all_to_all(copies, axis, 0, 0, tiled=True, axis_index_groups=groups)]
  transfers between devices with their start and end apart: 33 -> 14, of which waited for: 14 -> 9; matrix products, arithmetic and copies ran while one was open for 22% -> 25% of each run, Pallas kernels for 0% -> 0%
where the time goes in v2:
time: 203 us; the launch traced here: 202 us
  waiting for transfers between devices  47.4 us (23%)
  blocking collectives  43.7 us (22%)
  starting transfers between devices  39.1 us (19%)
  local copies, waits for them, and re-layouts  23.8 us (12%)
  matrix products  20.1 us (10%)
  other arithmetic  14.3 us (7%)
  between operations  13.7 us (7%)
    all_to_all x2, waiting for transfers between devices, spread(): lax.all_to_all(copies, axis, 0, 0, tiled=True, axis_index_groups=groups)  22.3 us
    dot_general x11, matrix products, dot(): lax.dot_general(u, v, (((cu,), (cv,)), ((), ())), preferred_element_type=...  19.8 us
    all_to_all x1, blocking collectives, shards(): parts = lax.all_to_all(parts, 'tile', 0, 0, tiled=True)  19.6 us
    all_to_all x1, blocking collectives, shards(): pot = lax.all_to_all(pot.reshape(NT, 4, QP, BLK), 'tile', 0, 0, tiled=True)  15.5 us
    all_to_all x2, starting transfers between devices, spread(): lax.all_to_all(copies, axis, 0, 0, tiled=True, axis_index_groups=groups)  12.9 us
    ppermute x8, starting transfers between devices, along_z(): return lax.ppermute(x, 'grid', pairs)  12.7 us
    ppermute x2, waiting for transfers between devices, permute_all(): return lax.ppermute(x, ('grid', 'tile'), pairs)  11.9 us
    ppermute x8, waiting for transfers between devices, along_z(): return lax.ppermute(x, 'grid', pairs)  11.4 us
  transfers between devices with their start and end apart: 14, of which 9 were waited for; matrix products, arithmetic and copies ran while one was open for 25% of the time, Pallas kernels for 0%

profile of v2, /device:TPU:32, one launch (start us, length us, event | category | flops | bytes accessed | tf_op | source)
XLA Modules:
  0.0 202.2 jit_solution(16929945470957497153)
XLA Ops:
  6.6 0.9 fusion.29
  7.6 0.9 broadcast_multiply_fusion
  8.5 0.8 broadcast_in_dim.60
  9.4 4.5 %all-to-all-start = ((bf16[4,32,2048]{2,1,0:T(8,128)(2,1)}), bf16[4,32,2048]{2,1,0:T(8,128)(2,1)}, u32[]{:S(2)}, u32[]{:S(2)}) async-start(bf16[4,32,2048]{2,1,0:T(8,128)(2,1)} %broadcast_in_dim.60), calls=%async_computation | async-start | bytes 1048576 | tf_op jit(solution)/shard_map/all_to_all | solution.py:31
  14.1 9.3 %all-to-all-done = bf16[4,32,2048]{2,1,0:T(8,128)(2,1)} async-done(((bf16[4,32,2048]{2,1,0:T(8,128)(2,1)}), bf16[4,32,2048]{2,1,0:T(8,128)(2,1)}, u32[]{:S(2)}, u32[]{:S(2)}) %all-to-all-start) | async-done | bytes 524320 | tf_op jit(solution)/shard_map/all_to_all | solution.py:31
  23.4 1.9 collective-permute-start
  25.6 3.8 %broadcast_in_dim.71 = bf16[4,512,8,256]{3,2,1,0:T(8,128)(2,1)} broadcast(bf16[4,8]{1,0:T(4,128)(2,1)S(1)} %convert_bitcast_fusion), dimensions={0,2} | broadcast | bytes 8388672 | tf_op jit(solution)/shard_map/broadcast_in_dim | solution.py:80
  29.5 10.3 %copy.27 = bf16[256,8,8,256]{3,1,2,0:T(8,128)(2,1)} copy(bf16[256,8,8,256]{3,2,1,0:T(8,128)(2,1)} %bitcast.112) | data formatting | bytes 16777216
  39.8 10.5 %mul.49 = bf16[2048,2048]{1,0:T(8,128)(2,1)} multiply(bf16[2048,2048]{1,0:T(8,128)(2,1)} %param.18, bf16[2048,2048]{1,0:T(8,128)(2,1)} %bitcast.111) | non-fusion elementwise | flops 4194304 | bytes 25165824 | tf_op jit(solution)/shard_map/mul | solution.py:81
  50.3 1.6 constant_dynamic-slice_fusion.1
  52.0 1.9 fusion.2
  53.9 2.0 collective-permute-start.2
  55.9 2.1 %collective-permute-start.3 = (bf16[4,32,2048]{2,1,0:T(8,128)(2,1)}, bf16[4,32,2048]{2,1,0:T(8,128)(2,1)}, u32[]{:S(2)}, u32[]{:S(2)}) collective-permute-start(bf16[4,32,2048]{2,1,0:T(8,128)(2,1)} %collective-permute-done.1), channel_id=1, source_target_pairs={{0,224},{8,232},{16,240},{24,248},{32,0},{40,8},{48,16},{56,24},{6... | collective-permute-start | bytes 1572872 | tf_op jit(solution)/shard_map/ppermute | solution.py:16
  58.0 2.2 %collective-permute-start.8 = (f32[1,128]{1,0:T(1,128)S(1)}, f32[1,128]{1,0:T(1,128)S(1)}, u32[]{:S(2)}, u32[]{:S(2)}) collective-permute-start(f32[1,128]{1,0:T(1,128)S(1)} %maximum_bitcast_fusion), channel_id=1, source_target_pairs={{0,0},{1,8},{2,16},{3,24},{4,32},{5,40},{6,48},{7,56},{8,64},{9,72... | collective-permute-start | bytes 1544 | tf_op jit(solution)/shard_map/ppermute | solution.py:26
  60.2 1.9 fusion.4
  62.1 1.9 fusion.6
  63.9 6.8 %collective-permute-done.8 = f32[1,128]{1,0:T(1,128)S(1)} collective-permute-done((f32[1,128]{1,0:T(1,128)S(1)}, f32[1,128]{1,0:T(1,128)S(1)}, u32[]{:S(2)}, u32[]{:S(2)}) %collective-permute-start.8) | collective-permute-done | bytes 544 | tf_op jit(solution)/shard_map/ppermute | solution.py:26
  71.4 2.0 collective-permute-start.5
  73.4 1.9 fusion.8
  75.2 1.9 fusion.10
  77.1 6.1 %collective-permute-done.4 = bf16[4,32,2048]{2,1,0:T(8,128)(2,1)S(1)} collective-permute-done((bf16[4,32,2048]{2,1,0:T(8,128)(2,1)}, bf16[4,32,2048]{2,1,0:T(8,128)(2,1)S(1)}, u32[]{:S(2)}, u32[]{:S(2)}) %collective-permute-start.4) | collective-permute-done | bytes 524320 | tf_op jit(solution)/shard_map/ppermute | solution.py:16
  83.2 1.0 collective-permute-done.5
  84.3 3.5 %collective-permute-start.6 = (bf16[2,32,2048]{2,1,0:T(8,128)(2,1)S(1)}, bf16[2,32,2048]{2,1,0:T(8,128)(2,1)S(1)}, u32[]{:S(2)}, u32[]{:S(2)}) collective-permute-start(bf16[2,32,2048]{2,1,0:T(8,128)(2,1)S(1)} %slice.14), channel_id=1, source_target_pairs={{0,32},{8,40},{16,48},{24,56},{32,64},{40,72},{48,80},{56,88},{64,... | collective-permute-start | bytes 786440 | tf_op jit(solution)/shard_map/ppermute | solution.py:16
  87.7 1.0 collective-permute-start.7
  88.8 0.8 fusion.12
  89.6 0.8 fusion.14
  90.5 2.6 %collective-permute-done.6 = bf16[2,32,2048]{2,1,0:T(8,128)(2,1)S(1)} collective-permute-done((bf16[2,32,2048]{2,1,0:T(8,128)(2,1)S(1)}, bf16[2,32,2048]{2,1,0:T(8,128)(2,1)S(1)}, u32[]{:S(2)}, u32[]{:S(2)}) %collective-permute-start.6) | collective-permute-done | bytes 262176 | tf_op jit(solution)/shard_map/ppermute | solution.py:16
  93.0 0.8 fusion.17
  93.8 1.7 collective-permute-done.7
  95.5 0.8 fusion.19
  96.2 19.6 %all_to_all.30 = bf16[8,128,512]{2,1,0:T(8,128)(2,1)} all-to-all(bf16[8,128,512]{2,1,0:T(8,128)(2,1)S(1)} %fusion.19), channel_id=1, replica_groups=mesh['grid'=32,'tile'=8] {'tile'}, dimensions={0} | all-to-all | bytes 2097152 | tf_op jit(solution)/shard_map/all_to_all | solution.py:84
  115.9 1.4 reduce_sum.34
  117.3 0.7 reshape.101
  118.0 9.4 %all-to-all-start.2 = ((bf16[32,4,512]{2,1,0:T(4,128)(2,1)}), bf16[32,4,512]{2,1,0:T(4,128)(2,1)S(1)}, u32[]{:S(2)}, u32[]{:S(2)}) async-start(bf16[32,4,512]{2,1,0:T(4,128)(2,1)} %reshape.101), calls=%async_computation.2 | async-start | bytes 262144 | tf_op jit(solution)/shard_map/all_to_all | solution.py:86
  127.5 1.9 collective-permute-start.9
  129.4 5.1 %collective-permute-done.9 = bf16[128,512]{1,0:T(8,128)(2,1)S(1)} collective-permute-done((bf16[128,512]{1,0:T(8,128)(2,1)S(1)}, bf16[128,512]{1,0:T(8,128)(2,1)S(1)}, u32[]{:S(2)}, u32[]{:S(2)}) %collective-permute-start.9) | collective-permute-done | bytes 131104 | tf_op jit(solution)/shard_map/ppermute | solution.py:26
  134.5 0.6 copy-done.4
  135.2 1.8 all-to-all-done.2
  137.4 15.5 %all_to_all.31 = bf16[8,4,4,512]{3,1,2,0:T(4,128)(2,1)S(1)} all-to-all(bf16[8,4,4,512]{3,1,2,0:T(4,128)(2,1)S(1)} %copy.21), channel_id=1, replica_groups=mesh['grid'=32,'tile'=8] {'tile'}, dimensions={0} | all-to-all | bytes 262144 | tf_op jit(solution)/shard_map/all_to_all | solution.py:92
  153.0 5.0 %convolution_convert_fusion = bf16[32,2048]{1,0:T(8,128)(2,1)S(1)} fusion(bf16[32,2048]{1,0:T(8,128)(2,1)S(1)} %bitcast.116, bf16[2048,2048]{1,0:T(8,128)(2,1)} %mul.49), kind=kOutput, calls=%fused_computation | convolution fusion | flops 268500992 | bytes 8650752 | tf_op jit(solution)/shard_map/dot_general | solution.py:35
  158.0 8.6 %all_to_all.32 = bf16[8,32,256]{2,1,0:T(8,128)(2,1)S(1)} all-to-all(bf16[8,32,256]{2,1,0:T(8,128)(2,1)S(1)} %bitcast.120), channel_id=1, replica_groups=mesh['grid'=32,'tile'=8] {'tile'}, dimensions={0} | all-to-all | bytes 262144 | tf_op jit(solution)/shard_map/all_to_all | solution.py:97
  166.6 0.9 broadcast_in_dim.72
  167.5 8.4 %all-to-all-start.5 = ((bf16[32,32,256]{2,1,0:T(8,128)(2,1)}), bf16[32,32,256]{2,1,0:T(8,128)(2,1)}, u32[]{:S(2)}, u32[]{:S(2)}) async-start(bf16[32,32,256]{2,1,0:T(8,128)(2,1)} %broadcast_in_dim.72), calls=%async_computation.5 | async-start | bytes 1048576 | tf_op jit(solution)/shard_map/all_to_all | solution.py:31
  176.0 1.3 reshape.106
  177.3 1.6 copy.23
  178.9 1.3 reshape.107
  180.2 12.9 %all-to-all-done.5 = bf16[32,32,256]{2,1,0:T(8,128)(2,1)} async-done(((bf16[32,32,256]{2,1,0:T(8,128)(2,1)}), bf16[32,32,256]{2,1,0:T(8,128)(2,1)}, u32[]{:S(2)}, u32[]{:S(2)}) %all-to-all-start.5) | async-done | bytes 524320 | tf_op jit(solution)/shard_map/all_to_all | solution.py:31
  193.1 2.2 %convolution_convert_fusion.1 = bf16[256,512]{1,0:T(8,128)(2,1)} fusion(bf16[1024,256]{1,0:T(8,128)(2,1)} %bitcast.28, bf16[1024,512]{1,0:T(8,128)(2,1)S(1)} %reshape.107), kind=kOutput, calls=%fused_computation.1 | convolution fusion | flops 268566528 | bytes 1835008 | tf_op jit(solution)/shard_map/dot_general | solution.py:35
  (52 shorter events, 2.1 us)
Async XLA Ops:
  6.5 45.5 %copy-start = (bf16[512,2048]{1,0:T(8,128)(2,1)S(1)}, bf16[512,2048]{1,0:T(8,128)(2,1)}, u32[]{:S(2)}) copy-start(bf16[512,2048]{1,0:T(8,128)(2,1)} %param.12) | copy-start | bytes 6291460
  6.5 7.3 %copy-start.7 = (s32[8,16]{1,0:T(8,128)S(1)}, s32[8,16]{1,0:T(8,128)}, u32[]{:S(2)}) copy-start(s32[8,16]{1,0:T(8,128)} %param.19) | copy-start | bytes 1540
  6.5 18.9 %copy-start.8 = (f32[3,32]{1,0:T(4,128)S(1)}, f32[3,32]{1,0:T(4,128)}, u32[]{:S(2)}) copy-start(f32[3,32]{1,0:T(4,128)} %param.17) | copy-start | bytes 1156
  6.5 19.0 %copy-start.2 = (f32[3,16384]{1,0:T(4,128)S(1)}, f32[3,16384]{1,0:T(4,128)}, u32[]{:S(2)}) copy-start(f32[3,16384]{1,0:T(4,128)} %param.15) | copy-start | bytes 589828
  6.5 19.1 %copy-start.5 = (f32[16384]{0:T(1024)S(1)}, f32[16384]{0:T(1024)}, u32[]{:S(2)}) copy-start(f32[16384]{0:T(1024)} %param.16) | copy-start | bytes 196612
  9.4 14.0 %all-to-all-start = ((bf16[4,32,2048]{2,1,0:T(8,128)(2,1)}), bf16[4,32,2048]{2,1,0:T(8,128)(2,1)}, u32[]{:S(2)}, u32[]{:S(2)}) async-start(bf16[4,32,2048]{2,1,0:T(8,128)(2,1)} %broadcast_in_dim.60), calls=%async_computation | async-start | bytes 1048576 | tf_op jit(solution)/shard_map/all_to_all | solution.py:31
  23.4 30.4 %collective-permute-start = (bf16[4,32,2048]{2,1,0:T(8,128)(2,1)}, bf16[4,32,2048]{2,1,0:T(8,128)(2,1)}, u32[]{:S(2)}, u32[]{:S(2)}) collective-permute-start(bf16[4,32,2048]{2,1,0:T(8,128)(2,1)} %all-to-all-done), channel_id=1, source_target_pairs={{0,32},{8,40},{16,48},{24,56},{32,64},{40,72},{48,80},{56,88},{64,... | collective-permute-start | bytes 1572872 | tf_op jit(solution)/shard_map/ppermute | solution.py:16
  25.4 28.5 %collective-permute-start.1 = (bf16[4,32,2048]{2,1,0:T(8,128)(2,1)}, bf16[4,32,2048]{2,1,0:T(8,128)(2,1)}, u32[]{:S(2)}, u32[]{:S(2)}) collective-permute-start(bf16[4,32,2048]{2,1,0:T(8,128)(2,1)} %all-to-all-done), channel_id=1, source_target_pairs={{0,224},{8,232},{16,240},{24,248},{32,0},{40,8},{48,16},{56,24},{6... | collective-permute-start | bytes 1572872 | tf_op jit(solution)/shard_map/ppermute | solution.py:16
  53.9 17.3 %collective-permute-start.2 = (bf16[4,32,2048]{2,1,0:T(8,128)(2,1)}, bf16[4,32,2048]{2,1,0:T(8,128)(2,1)}, u32[]{:S(2)}, u32[]{:S(2)}) collective-permute-start(bf16[4,32,2048]{2,1,0:T(8,128)(2,1)} %collective-permute-done), channel_id=1, source_target_pairs={{0,32},{8,40},{16,48},{24,56},{32,64},{40,72},{48,80},{56,88},{64,... | collective-permute-start | bytes 1572872 | tf_op jit(solution)/shard_map/ppermute | solution.py:16
  55.9 15.5 %collective-permute-start.3 = (bf16[4,32,2048]{2,1,0:T(8,128)(2,1)}, bf16[4,32,2048]{2,1,0:T(8,128)(2,1)}, u32[]{:S(2)}, u32[]{:S(2)}) collective-permute-start(bf16[4,32,2048]{2,1,0:T(8,128)(2,1)} %collective-permute-done.1), channel_id=1, source_target_pairs={{0,224},{8,232},{16,240},{24,248},{32,0},{40,8},{48,16},{56,24},{6... | collective-permute-start | bytes 1572872 | tf_op jit(solution)/shard_map/ppermute | solution.py:16
  58.0 12.7 %collective-permute-start.8 = (f32[1,128]{1,0:T(1,128)S(1)}, f32[1,128]{1,0:T(1,128)S(1)}, u32[]{:S(2)}, u32[]{:S(2)}) collective-permute-start(f32[1,128]{1,0:T(1,128)S(1)} %maximum_bitcast_fusion), channel_id=1, source_target_pairs={{0,0},{1,8},{2,16},{3,24},{4,32},{5,40},{6,48},{7,56},{8,64},{9,72... | collective-permute-start | bytes 1544 | tf_op jit(solution)/shard_map/ppermute | solution.py:26
  71.3 12.0 %collective-permute-start.4 = (bf16[4,32,2048]{2,1,0:T(8,128)(2,1)}, bf16[4,32,2048]{2,1,0:T(8,128)(2,1)S(1)}, u32[]{:S(2)}, u32[]{:S(2)}) collective-permute-start(bf16[4,32,2048]{2,1,0:T(8,128)(2,1)} %collective-permute-done.2), channel_id=1, source_target_pairs={{0,32},{8,40},{16,48},{24,56},{32,64},{40,72},{48,80},{56,88},{64,... | collective-permute-start | bytes 1572872 | tf_op jit(solution)/shard_map/ppermute | solution.py:16
  71.4 12.9 %collective-permute-start.5 = (bf16[4,32,2048]{2,1,0:T(8,128)(2,1)}, bf16[4,32,2048]{2,1,0:T(8,128)(2,1)S(1)}, u32[]{:S(2)}, u32[]{:S(2)}) collective-permute-start(bf16[4,32,2048]{2,1,0:T(8,128)(2,1)} %collective-permute-done.3), channel_id=1, source_target_pairs={{0,224},{8,232},{16,240},{24,248},{32,0},{40,8},{48,16},{56,24},{6... | collective-permute-start | bytes 1572872 | tf_op jit(solution)/shard_map/ppermute | solution.py:16
  84.3 8.7 %collective-permute-start.6 = (bf16[2,32,2048]{2,1,0:T(8,128)(2,1)S(1)}, bf16[2,32,2048]{2,1,0:T(8,128)(2,1)S(1)}, u32[]{:S(2)}, u32[]{:S(2)}) collective-permute-start(bf16[2,32,2048]{2,1,0:T(8,128)(2,1)S(1)} %slice.14), channel_id=1, source_target_pairs={{0,32},{8,40},{16,48},{24,56},{32,64},{40,72},{48,80},{56,88},{64,... | collective-permute-start | bytes 786440 | tf_op jit(solution)/shard_map/ppermute | solution.py:16
  87.7 7.7 %collective-permute-start.7 = (bf16[2,32,2048]{2,1,0:T(8,128)(2,1)S(1)}, bf16[2,32,2048]{2,1,0:T(8,128)(2,1)S(1)}, u32[]{:S(2)}, u32[]{:S(2)}) collective-permute-start(bf16[2,32,2048]{2,1,0:T(8,128)(2,1)S(1)} %slice.15), channel_id=1, source_target_pairs={{0,224},{8,232},{16,240},{24,248},{32,0},{40,8},{48,16},{56,24},{6... | collective-permute-start | bytes 786440 | tf_op jit(solution)/shard_map/ppermute | solution.py:16
  96.2 31.2 %copy-start.3 = (bf16[4,32,512]{2,1,0:T(8,128)(2,1)S(1)}, bf16[4,32,512]{2,1,0:T(8,128)(2,1)}, u32[]{:S(2)}) copy-start(bf16[4,32,512]{2,1,0:T(8,128)(2,1)} %constant_dynamic-slice_fusion.1) | copy-start | bytes 393220
  96.2 40.7 %copy-start.6 = (s32[32,32]{1,0:T(8,128)S(1)}, s32[32,32]{1,0:T(8,128)}, u32[]{:S(2)}) copy-start(s32[32,32]{1,0:T(8,128)} %param.14) | copy-start | bytes 12292
  115.9 21.1 %copy-start.1 = (bf16[512,512]{1,0:T(8,128)(2,1)S(1)}, bf16[512,512]{1,0:T(8,128)(2,1)}, u32[]{:S(2)}) copy-start(bf16[512,512]{1,0:T(8,128)(2,1)} %param.13) | copy-start | bytes 1572868
  118.0 19.0 %all-to-all-start.2 = ((bf16[32,4,512]{2,1,0:T(4,128)(2,1)}), bf16[32,4,512]{2,1,0:T(4,128)(2,1)S(1)}, u32[]{:S(2)}, u32[]{:S(2)}) async-start(bf16[32,4,512]{2,1,0:T(4,128)(2,1)} %reshape.101), calls=%async_computation.2 | async-start | bytes 262144 | tf_op jit(solution)/shard_map/all_to_all | solution.py:86
  127.4 48.5 %all-gather.2.cloned.1.call-start = ((), (), s32[]{:S(2)}) async-start(), calls=%async_computation.6 | async-start | bytes 1179648 | tf_op jit(solution)/shard_map/all_gather | solution.py:101
  127.5 7.1 %collective-permute-start.9 = (bf16[128,512]{1,0:T(8,128)(2,1)S(1)}, bf16[128,512]{1,0:T(8,128)(2,1)S(1)}, u32[]{:S(2)}, u32[]{:S(2)}) collective-permute-start(bf16[128,512]{1,0:T(8,128)(2,1)S(1)} %bitcast.124), channel_id=1, source_target_pairs={{0,0},{1,32},{2,64},{3,96},{4,128},{5,160},{6,192},{7,224},{8,8},{... | collective-permute-start | bytes 393224 | tf_op jit(solution)/shard_map/ppermute | solution.py:26
  134.5 0.6 copy-start.4
  167.5 25.6 %all-to-all-start.5 = ((bf16[32,32,256]{2,1,0:T(8,128)(2,1)}), bf16[32,32,256]{2,1,0:T(8,128)(2,1)}, u32[]{:S(2)}, u32[]{:S(2)}) async-start(bf16[32,32,256]{2,1,0:T(8,128)(2,1)} %broadcast_in_dim.72), calls=%async_computation.5 | async-start | bytes 1048576 | tf_op jit(solution)/shard_map/all_to_all | solution.py:31
Sparse Core Ops, SparseCore 0:
  135.3 32.9 all-gather.1

commit v3 on v2

--- a/solution.py
+++ b/solution.py
@@ -62,7 +62,7 @@
         if s == 1:
             info, up, down = tie((info, up, down))
             info = permute_all(info, lambda a, b, c: (2 * b + c // 4, c % 4, a))[0]
-        if s == 3:
+        if s == 1:
             piece, up, down = tie((piece, up, down))
             piece = permute_all(piece, lambda a, b, c: (c, b, a))
         parts = put(put(parts, up, s), down, -s)
@@ -75,11 +75,9 @@
     coef = 1.0 / jnp.sqrt(jnp.sum(off * off, axis=0) + widths.reshape(nblk, 1, BLK))
     coef = coef * named[:, None, None]
 
-    local_ids = 4 * j + jnp.arange(4, dtype=jnp.int32)
-    in_dom = jnp.any(dom[:, :, None] == local_ids[None, None, :], axis=1).T.astype(bf16)
-    dmask = jnp.broadcast_to(in_dom[:, None, :, None], (4, BLK, NT, 256)).reshape(lmo.shape)
-    region = lmo * dmask
-    parts, coef, region = tie((parts, coef, region))
+    x_col = lax.all_gather(piece, "tile", axis=0, tiled=True)
+    x_col = x_col.reshape(NZ, NY, 8, QP, BLK).transpose(1, 2, 0, 3, 4).reshape(-1, BLK)
+    parts, coef, x_col = tie((parts, coef, x_col))
 
     parts = lax.all_to_all(parts, "tile", 0, 0, tiled=True)
     term = jnp.sum(parts.astype(f32), axis=0).astype(bf16).reshape(NZ * NY, QP, BLK)
@@ -92,14 +90,17 @@
     pot = lax.all_to_all(pot.reshape(NT, 4, QP, BLK), "tile", 0, 0, tiled=True)
     pot = pot.transpose(0, 2, 1, 3).reshape(NT * QP, cols)
 
-    w = dot(pot, region, 1, 0).astype(bf16)
-    w = w.reshape(NT * QP, NT, 256).transpose(1, 0, 2)
+    local_ids = 4 * j + jnp.arange(4, dtype=jnp.int32)
+    in_dom = jnp.any(dom[:, :, None] == local_ids[None, None, :], axis=1).astype(f32)
+    w = jnp.zeros((NT * QP, NT, 256), f32)
+    for k in range(4):
+        rows = slice(k * BLK, (k + 1) * BLK)
+        term = dot(pot[:, rows], lmo[rows], 1, 0).reshape(NT * QP, NT, 256)
+        w = w + term * in_dom[:, k][None, :, None]
+    w = w.astype(bf16).transpose(1, 0, 2)
     w = lax.all_to_all(w, "tile", 0, 0, tiled=True)
     w = jnp.sum(w.astype(f32), axis=0).astype(bf16)
     w_all = spread(w, "grid", NZ * NY).reshape(-1, 256)
-
-    x_col = lax.all_gather(piece, "tile", axis=0, tiled=True)
-    x_col = x_col.reshape(NZ, NY, 8, QP, BLK).transpose(1, 2, 0, 3, 4).reshape(-1, BLK)
     return dot(w_all, x_col, 0, 0).astype(bf16)
 
 

time: 203 us -> 195 us (0.961)
  local copies, waits for them, and re-layouts: 23.8 us -> 12.4 us
  other arithmetic: 14.3 us -> 5.55 us
  blocking collectives: 43.7 us -> 49.3 us
  waiting for transfers between devices: 47.4 us -> 51.2 us
  matrix products: 20.1 us -> 23.4 us
    ppermute x8, waiting for transfers between devices: 11.4 us -> 24.9 us  [along_z(): return lax.ppermute(x, 'grid', pairs)]
    all_to_all x2 -> x1, waiting for transfers between devices: 22.3 us -> 9.58 us  [spread(): lax.all_to_all(copies, axis, 0, 0, tiled=True, axis_index_groups=groups)]
    ppermute x2, waiting for transfers between devices: 11.9 us -> 1.34 us  [permute_all(): return lax.ppermute(x, ('grid', 'tile'), pairs)]
    mul x1 -> x0, other arithmetic: 10.5 us -> none  [shards(): region = lmo * dmask]
    unnamed x23 -> x20, local copies, waits for them, and re-layouts: 11.2 us -> 0.88 us
    all_to_all x2 -> x1, starting transfers between devices: 12.9 us -> 4.46 us  [spread(): lax.all_to_all(copies, axis, 0, 0, tiled=True, axis_index_groups=groups)]
    all_to_all x1, waiting for transfers between devices: 1.76 us -> 9.31 us  [shards(): term = lax.all_to_all(term, 'grid', 0, 0, tiled=True)]
    all_to_all x0 -> x1, waiting for transfers between devices: none -> 6.04 us  [shards(): pot = lax.all_to_all(pot.reshape(NT, 4, QP, BLK), 'tile', 0, 0, tiled=True)]
  transfers between devices with their start and end apart: 14 -> 14, of which waited for: 9 -> 9; matrix products, arithmetic and copies ran while one was open for 25% -> 9% of each run, Pallas kernels for 0% -> 0%
where the time goes in v3:
time: 195 us; the launch traced here: 194 us
  waiting for transfers between devices  51.2 us (26%)
  blocking collectives  49.3 us (25%)
  starting transfers between devices  38 us (19%)
  matrix products  23.4 us (12%)
  between operations  13.7 us (7%)
  local copies, waits for them, and re-layouts  12.4 us (6%)
  other arithmetic  5.55 us (3%)
    ppermute x8, waiting for transfers between devices, along_z(): return lax.ppermute(x, 'grid', pairs)  24.9 us
    dot_general x14, matrix products, dot(): lax.dot_general(u, v, (((cu,), (cv,)), ((), ())), preferred_element_type=...  22 us
    all_to_all x1, blocking collectives, spread(): lax.all_to_all(copies, axis, 0, 0, tiled=True, axis_index_groups=groups)  21.3 us
    all_to_all x1, blocking collectives, shards(): parts = lax.all_to_all(parts, 'tile', 0, 0, tiled=True)  19.3 us
    ppermute x8, starting transfers between devices, along_z(): return lax.ppermute(x, 'grid', pairs)  15 us
    all_to_all x1, waiting for transfers between devices, spread(): lax.all_to_all(copies, axis, 0, 0, tiled=True, axis_index_groups=groups)  9.58 us
    all_to_all x1, waiting for transfers between devices, shards(): term = lax.all_to_all(term, 'grid', 0, 0, tiled=True)  9.31 us
    all_to_all x1, blocking collectives, shards(): w = lax.all_to_all(w, 'tile', 0, 0, tiled=True)  8.65 us
  transfers between devices with their start and end apart: 14, of which 9 were waited for; matrix products, arithmetic and copies ran while one was open for 9% of the time, Pallas kernels for 0%

profile of v3, /device:TPU:32, one launch (start us, length us, event | category | flops | bytes accessed | tf_op | source)
XLA Modules:
  0.0 193.6 jit_solution(4291446591441856103)
XLA Ops:
  6.5 0.9 fusion.46
  7.6 0.9 broadcast_multiply_fusion
  8.5 0.8 broadcast_in_dim.54
  9.4 4.5 %all-to-all-start = ((bf16[4,32,2048]{2,1,0:T(8,128)(2,1)}), bf16[4,32,2048]{2,1,0:T(8,128)(2,1)}, u32[]{:S(2)}, u32[]{:S(2)}) async-start(bf16[4,32,2048]{2,1,0:T(8,128)(2,1)} %broadcast_in_dim.54), calls=%async_computation | async-start | bytes 1048576 | tf_op jit(solution)/shard_map/all_to_all | solution.py:31
  13.8 9.6 %all-to-all-done = bf16[4,32,2048]{2,1,0:T(8,128)(2,1)} async-done(((bf16[4,32,2048]{2,1,0:T(8,128)(2,1)}), bf16[4,32,2048]{2,1,0:T(8,128)(2,1)}, u32[]{:S(2)}, u32[]{:S(2)}) %all-to-all-start) | async-done | bytes 524320 | tf_op jit(solution)/shard_map/all_to_all | solution.py:31
  23.4 1.9 collective-permute-start
  25.5 0.7 copy.55
  26.4 1.6 constant_dynamic-slice_fusion.1
  28.1 1.9 fusion.10
  30.0 5.9 %collective-permute-done = bf16[4,32,2048]{2,1,0:T(8,128)(2,1)} collective-permute-done((bf16[4,32,2048]{2,1,0:T(8,128)(2,1)}, bf16[4,32,2048]{2,1,0:T(8,128)(2,1)}, u32[]{:S(2)}, u32[]{:S(2)}) %collective-permute-start) | collective-permute-done | bytes 524320 | tf_op jit(solution)/shard_map/ppermute | solution.py:16
  35.9 1.8 collective-permute-done.1
  37.8 3.1 %collective-permute-start.2 = (bf16[4,32,2048]{2,1,0:T(8,128)(2,1)}, bf16[4,32,2048]{2,1,0:T(8,128)(2,1)}, u32[]{:S(2)}, u32[]{:S(2)}) collective-permute-start(bf16[4,32,2048]{2,1,0:T(8,128)(2,1)} %collective-permute-done), channel_id=1, source_target_pairs={{0,32},{8,40},{16,48},{24,56},{32,64},{40,72},{48,80},{56,88},{64,... | collective-permute-start | bytes 1572872 | tf_op jit(solution)/shard_map/ppermute | solution.py:16
  40.9 1.9 collective-permute-start.8
  42.8 4.7 %collective-permute-start.9 = (bf16[128,512]{1,0:T(8,128)(2,1)}, bf16[128,512]{1,0:T(8,128)(2,1)}, u32[]{:S(2)}, u32[]{:S(2)}) collective-permute-start(bf16[128,512]{1,0:T(8,128)(2,1)} %bitcast.3), channel_id=1, source_target_pairs={{0,0},{1,32},{2,64},{3,96},{4,128},{5,160},{6,192},{7,224},{8,8},{... | collective-permute-start | bytes 393224 | tf_op jit(solution)/shard_map/ppermute | solution.py:26
  47.5 1.9 fusion.12
  49.4 1.9 fusion.14
  51.3 1.3 collective-permute-done.8
  52.8 1.1 multiply_reduce_fusion
  54.0 0.8 rsqrt_multiply_fusion
  54.8 7.1 %collective-permute-start.4 = (bf16[4,32,2048]{2,1,0:T(8,128)(2,1)}, bf16[4,32,2048]{2,1,0:T(8,128)(2,1)S(1)}, u32[]{:S(2)}, u32[]{:S(2)}) collective-permute-start(bf16[4,32,2048]{2,1,0:T(8,128)(2,1)} %collective-permute-done.2), channel_id=1, source_target_pairs={{0,32},{8,40},{16,48},{24,56},{32,64},{40,72},{48,80},{56,88},{64,... | collective-permute-start | bytes 1572872 | tf_op jit(solution)/shard_map/ppermute | solution.py:16
  61.9 1.9 fusion.16
  63.8 1.9 fusion.18
  65.7 8.4 %collective-permute-done.4 = bf16[4,32,2048]{2,1,0:T(8,128)(2,1)S(1)} collective-permute-done((bf16[4,32,2048]{2,1,0:T(8,128)(2,1)}, bf16[4,32,2048]{2,1,0:T(8,128)(2,1)S(1)}, u32[]{:S(2)}, u32[]{:S(2)}) %collective-permute-start.4) | collective-permute-done | bytes 524320 | tf_op jit(solution)/shard_map/ppermute | solution.py:16
  74.1 2.5 %collective-permute-start.6 = (bf16[2,32,2048]{2,1,0:T(8,128)(2,1)S(1)}, bf16[2,32,2048]{2,1,0:T(8,128)(2,1)S(1)}, u32[]{:S(2)}, u32[]{:S(2)}) collective-permute-start(bf16[2,32,2048]{2,1,0:T(8,128)(2,1)S(1)} %slice.66), channel_id=1, source_target_pairs={{0,32},{8,40},{16,48},{24,56},{32,64},{40,72},{48,80},{56,88},{64,... | collective-permute-start | bytes 786440 | tf_op jit(solution)/shard_map/ppermute | solution.py:16
  76.9 0.8 fusion.20
  77.7 0.8 fusion.22
  78.6 3.6 %collective-permute-done.6 = bf16[2,32,2048]{2,1,0:T(8,128)(2,1)S(1)} collective-permute-done((bf16[2,32,2048]{2,1,0:T(8,128)(2,1)S(1)}, bf16[2,32,2048]{2,1,0:T(8,128)(2,1)S(1)}, u32[]{:S(2)}, u32[]{:S(2)}) %collective-permute-start.6) | collective-permute-done | bytes 262176 | tf_op jit(solution)/shard_map/ppermute | solution.py:16
  82.2 0.8 fusion.25
  83.0 5.0 %collective-permute-done.7 = bf16[2,32,2048]{2,1,0:T(8,128)(2,1)S(1)} collective-permute-done((bf16[2,32,2048]{2,1,0:T(8,128)(2,1)S(1)}, bf16[2,32,2048]{2,1,0:T(8,128)(2,1)S(1)}, u32[]{:S(2)}, u32[]{:S(2)}) %collective-permute-start.7) | collective-permute-done | bytes 262176 | tf_op jit(solution)/shard_map/ppermute | solution.py:16
  88.0 0.8 fusion.27
  88.8 2.2 %reshape.109 = bf16[8,4,8,4,512]{4,3,2,1,0:T(4,128)(2,1)} reshape(bf16[1024,512]{1,0:T(8,128)(2,1)} %all-gather.2.cloned.1.call-done) | data formatting | bytes 2097152 | tf_op jit(solution)/shard_map/reshape | solution.py:79
  91.0 2.8 %copy.23 = bf16[4,8,8,4,512]{4,3,2,1,0:T(4,128)(2,1)} copy(bf16[4,8,8,4,512]{4,3,1,0,2:T(4,128)(2,1)} %bitcast.141) | data formatting | bytes 2097152 | tf_op jit(solution)/shard_map/transpose | solution.py:79
  93.8 2.1 %reshape.110 = bf16[1024,512]{1,0:T(8,128)(2,1)} reshape(bf16[4,8,8,4,512]{4,3,2,1,0:T(4,128)(2,1)} %copy.23) | data formatting | bytes 2097152 | tf_op jit(solution)/shard_map/reshape | solution.py:79
  95.9 19.3 %all_to_all.30 = bf16[8,128,512]{2,1,0:T(8,128)(2,1)} all-to-all(bf16[8,128,512]{2,1,0:T(8,128)(2,1)S(1)} %fusion.27), channel_id=1, replica_groups=mesh['grid'=32,'tile'=8] {'tile'}, dimensions={0} | all-to-all | bytes 2097152 | tf_op jit(solution)/shard_map/all_to_all | solution.py:82
  115.3 1.4 reduce_sum.34
  117.3 8.6 %all-to-all-start.2 = ((bf16[32,4,512]{2,1,0:T(4,128)(2,1)}), bf16[32,4,512]{2,1,0:T(4,128)(2,1)S(1)}, u32[]{:S(2)}, u32[]{:S(2)}) async-start(bf16[32,4,512]{2,1,0:T(4,128)(2,1)} %reshape.111), calls=%async_computation.2 | async-start | bytes 262144 | tf_op jit(solution)/shard_map/all_to_all | solution.py:84
  126.2 9.3 %all-to-all-done.2 = bf16[32,4,512]{2,1,0:T(4,128)(2,1)S(1)} async-done(((bf16[32,4,512]{2,1,0:T(4,128)(2,1)}), bf16[32,4,512]{2,1,0:T(4,128)(2,1)S(1)}, u32[]{:S(2)}, u32[]{:S(2)}) %all-to-all-start.2) | async-done | bytes 131104 | tf_op jit(solution)/shard_map/all_to_all | solution.py:84
  135.5 1.4 fusion.8
  137.0 0.7 copy.25
  137.7 3.4 %all-to-all-start.3 = ((bf16[8,4,4,512]{3,1,2,0:T(4,128)(2,1)}), bf16[8,4,4,512]{3,1,2,0:T(4,128)(2,1)S(1)}, u32[]{:S(2)}, u32[]{:S(2)}) async-start(bf16[8,4,4,512]{3,1,2,0:T(4,128)(2,1)} %copy.25), calls=%async_computation.3 | async-start | bytes 262144 | tf_op jit(solution)/shard_map/all_to_all | solution.py:90
  141.1 6.0 %all-to-all-done.3 = bf16[8,4,4,512]{3,1,2,0:T(4,128)(2,1)S(1)} async-done(((bf16[8,4,4,512]{3,1,2,0:T(4,128)(2,1)}), bf16[8,4,4,512]{3,1,2,0:T(4,128)(2,1)S(1)}, u32[]{:S(2)}, u32[]{:S(2)}) %all-to-all-start.3) | async-done | bytes 131104 | tf_op jit(solution)/shard_map/all_to_all | solution.py:90
  147.2 2.1 %fusion = f32[32,2048]{1,0:T(8,128)S(1)} fusion(bf16[2048,2048]{1,0:T(8,128)(2,1)} %param.18, bf16[32,2048]{1,0:T(8,128)(2,1)S(1)} %bitcast.149), kind=kOutput, calls=%fused_computation | convolution fusion | flops 67108864 | bytes 2392064 | tf_op jit(solution)/shard_map/dot_general | solution.py:35
  149.2 2.1 %fusion.2 = f32[32,2048]{1,0:T(8,128)S(1)} fusion(bf16[2048,2048]{1,0:T(8,128)(2,1)} %param.18, bf16[32,2048]{1,0:T(8,128)(2,1)S(1)} %bitcast.150), kind=kOutput, calls=%fused_computation.2 | convolution fusion | flops 67108864 | bytes 2392064 | tf_op jit(solution)/shard_map/dot_general | solution.py:35
  151.3 2.1 %fusion.4 = f32[32,2048]{1,0:T(8,128)S(1)} fusion(bf16[2048,2048]{1,0:T(8,128)(2,1)} %param.18, bf16[32,2048]{1,0:T(8,128)(2,1)S(1)} %bitcast.151), kind=kOutput, calls=%fused_computation.4 | convolution fusion | flops 67108864 | bytes 2392064 | tf_op jit(solution)/shard_map/dot_general | solution.py:35
  153.3 2.1 %fusion.6 = f32[32,2048]{1,0:T(8,128)S(1)} fusion(bf16[2048,2048]{1,0:T(8,128)(2,1)} %param.18, bf16[32,2048]{1,0:T(8,128)(2,1)S(1)} %bitcast.152), kind=kOutput, calls=%fused_computation.6 | convolution fusion | flops 67108864 | bytes 2392064 | tf_op jit(solution)/shard_map/dot_general | solution.py:35
  155.6 8.7 %all_to_all.31 = bf16[8,32,256]{2,1,0:T(8,128)(2,1)S(1)} all-to-all(bf16[8,32,256]{2,1,0:T(8,128)(2,1)S(1)} %fusion.37), channel_id=1, replica_groups=mesh['grid'=32,'tile'=8] {'tile'}, dimensions={0} | all-to-all | bytes 262144 | tf_op jit(solution)/shard_map/all_to_all | solution.py:101
  164.3 21.3 %all_to_all.32 = bf16[32,32,256]{2,1,0:T(8,128)(2,1)S(1)} all-to-all(bf16[32,32,256]{2,1,0:T(8,128)(2,1)S(1)} %broadcast_in_dim.65), channel_id=1, replica_groups=mesh['grid'=32,'tile'=8] {'grid'}, dimensions={0} | all-to-all | bytes 1048576 | tf_op jit(solution)/shard_map/all_to_all | solution.py:31
  185.6 1.2 convolution_convert_fusion
  (51 shorter events, 2.4 us)
Async XLA Ops:
  6.5 21.5 %copy-start = (bf16[512,2048]{1,0:T(8,128)(2,1)S(1)}, bf16[512,2048]{1,0:T(8,128)(2,1)}, u32[]{:S(2)}) copy-start(bf16[512,2048]{1,0:T(8,128)(2,1)} %param.12) | copy-start | bytes 6291460
  6.5 18.9 %copy-start.7 = (f32[3,32]{1,0:T(4,128)S(1)}, f32[3,32]{1,0:T(4,128)}, u32[]{:S(2)}) copy-start(f32[3,32]{1,0:T(4,128)} %param.17) | copy-start | bytes 1156
  6.5 19.0 %copy-start.3 = (f32[3,16384]{1,0:T(4,128)S(1)}, f32[3,16384]{1,0:T(4,128)}, u32[]{:S(2)}) copy-start(f32[3,16384]{1,0:T(4,128)} %param.15) | copy-start | bytes 589828
  6.5 19.7 %copy-start.4 = (f32[16384]{0:T(1024)S(1)}, f32[16384]{0:T(1024)}, u32[]{:S(2)}) copy-start(f32[16384]{0:T(1024)} %param.16) | copy-start | bytes 196612
  9.4 14.0 %all-to-all-start = ((bf16[4,32,2048]{2,1,0:T(8,128)(2,1)}), bf16[4,32,2048]{2,1,0:T(8,128)(2,1)}, u32[]{:S(2)}, u32[]{:S(2)}) async-start(bf16[4,32,2048]{2,1,0:T(8,128)(2,1)} %broadcast_in_dim.54), calls=%async_computation | async-start | bytes 1048576 | tf_op jit(solution)/shard_map/all_to_all | solution.py:31
  13.8 75.0 %all-gather.2.cloned.1.call-start = ((), (), s32[]{:S(2)}) async-start(), calls=%async_computation.6 | async-start | bytes 1179648 | tf_op jit(solution)/shard_map/all_gather | solution.py:78
  23.4 12.5 %collective-permute-start = (bf16[4,32,2048]{2,1,0:T(8,128)(2,1)}, bf16[4,32,2048]{2,1,0:T(8,128)(2,1)}, u32[]{:S(2)}, u32[]{:S(2)}) collective-permute-start(bf16[4,32,2048]{2,1,0:T(8,128)(2,1)} %all-to-all-done), channel_id=1, source_target_pairs={{0,32},{8,40},{16,48},{24,56},{32,64},{40,72},{48,80},{56,88},{64,... | collective-permute-start | bytes 1572872 | tf_op jit(solution)/shard_map/ppermute | solution.py:16
  25.3 12.4 %collective-permute-start.1 = (bf16[4,32,2048]{2,1,0:T(8,128)(2,1)}, bf16[4,32,2048]{2,1,0:T(8,128)(2,1)}, u32[]{:S(2)}, u32[]{:S(2)}) collective-permute-start(bf16[4,32,2048]{2,1,0:T(8,128)(2,1)} %all-to-all-done), channel_id=1, source_target_pairs={{0,224},{8,232},{16,240},{24,248},{32,0},{40,8},{48,16},{56,24},{6... | collective-permute-start | bytes 1572872 | tf_op jit(solution)/shard_map/ppermute | solution.py:16
  37.8 17.0 %collective-permute-start.2 = (bf16[4,32,2048]{2,1,0:T(8,128)(2,1)}, bf16[4,32,2048]{2,1,0:T(8,128)(2,1)}, u32[]{:S(2)}, u32[]{:S(2)}) collective-permute-start(bf16[4,32,2048]{2,1,0:T(8,128)(2,1)} %collective-permute-done), channel_id=1, source_target_pairs={{0,32},{8,40},{16,48},{24,56},{32,64},{40,72},{48,80},{56,88},{64,... | collective-permute-start | bytes 1572872 | tf_op jit(solution)/shard_map/ppermute | solution.py:16
  40.9 21.0 %collective-permute-start.3 = (bf16[4,32,2048]{2,1,0:T(8,128)(2,1)}, bf16[4,32,2048]{2,1,0:T(8,128)(2,1)}, u32[]{:S(2)}, u32[]{:S(2)}) collective-permute-start(bf16[4,32,2048]{2,1,0:T(8,128)(2,1)} %collective-permute-done.1), channel_id=1, source_target_pairs={{0,224},{8,232},{16,240},{24,248},{32,0},{40,8},{48,16},{56,24},{6... | collective-permute-start | bytes 1572872 | tf_op jit(solution)/shard_map/ppermute | solution.py:16
  40.9 11.7 %collective-permute-start.8 = (f32[1,128]{1,0:T(1,128)S(1)}, f32[1,128]{1,0:T(1,128)S(1)}, u32[]{:S(2)}, u32[]{:S(2)}) collective-permute-start(f32[1,128]{1,0:T(1,128)S(1)} %maximum_bitcast_fusion), channel_id=1, source_target_pairs={{0,0},{1,8},{2,16},{3,24},{4,32},{5,40},{6,48},{7,56},{8,64},{9,72... | collective-permute-start | bytes 1544 | tf_op jit(solution)/shard_map/ppermute | solution.py:26
  42.8 11.1 %collective-permute-start.9 = (bf16[128,512]{1,0:T(8,128)(2,1)}, bf16[128,512]{1,0:T(8,128)(2,1)}, u32[]{:S(2)}, u32[]{:S(2)}) collective-permute-start(bf16[128,512]{1,0:T(8,128)(2,1)} %bitcast.3), channel_id=1, source_target_pairs={{0,0},{1,32},{2,64},{3,96},{4,128},{5,160},{6,192},{7,224},{8,8},{... | collective-permute-start | bytes 393224 | tf_op jit(solution)/shard_map/ppermute | solution.py:26
  54.8 19.3 %collective-permute-start.4 = (bf16[4,32,2048]{2,1,0:T(8,128)(2,1)}, bf16[4,32,2048]{2,1,0:T(8,128)(2,1)S(1)}, u32[]{:S(2)}, u32[]{:S(2)}) collective-permute-start(bf16[4,32,2048]{2,1,0:T(8,128)(2,1)} %collective-permute-done.2), channel_id=1, source_target_pairs={{0,32},{8,40},{16,48},{24,56},{32,64},{40,72},{48,80},{56,88},{64,... | collective-permute-start | bytes 1572872 | tf_op jit(solution)/shard_map/ppermute | solution.py:16
  61.9 14.7 %collective-permute-start.5 = (bf16[4,32,2048]{2,1,0:T(8,128)(2,1)}, bf16[4,32,2048]{2,1,0:T(8,128)(2,1)S(1)}, u32[]{:S(2)}, u32[]{:S(2)}) collective-permute-start(bf16[4,32,2048]{2,1,0:T(8,128)(2,1)} %collective-permute-done.3), channel_id=1, source_target_pairs={{0,224},{8,232},{16,240},{24,248},{32,0},{40,8},{48,16},{56,24},{6... | collective-permute-start | bytes 1572872 | tf_op jit(solution)/shard_map/ppermute | solution.py:16
  74.1 8.1 %collective-permute-start.6 = (bf16[2,32,2048]{2,1,0:T(8,128)(2,1)S(1)}, bf16[2,32,2048]{2,1,0:T(8,128)(2,1)S(1)}, u32[]{:S(2)}, u32[]{:S(2)}) collective-permute-start(bf16[2,32,2048]{2,1,0:T(8,128)(2,1)S(1)} %slice.66), channel_id=1, source_target_pairs={{0,32},{8,40},{16,48},{24,56},{32,64},{40,72},{48,80},{56,88},{64,... | collective-permute-start | bytes 786440 | tf_op jit(solution)/shard_map/ppermute | solution.py:16
  76.6 11.4 %collective-permute-start.7 = (bf16[2,32,2048]{2,1,0:T(8,128)(2,1)S(1)}, bf16[2,32,2048]{2,1,0:T(8,128)(2,1)S(1)}, u32[]{:S(2)}, u32[]{:S(2)}) collective-permute-start(bf16[2,32,2048]{2,1,0:T(8,128)(2,1)S(1)} %slice.67), channel_id=1, source_target_pairs={{0,224},{8,232},{16,240},{24,248},{32,0},{40,8},{48,16},{56,24},{6... | collective-permute-start | bytes 786440 | tf_op jit(solution)/shard_map/ppermute | solution.py:16
  95.9 30.1 %copy-start.6 = (s32[8,16]{1,0:T(8,128)S(1)}, s32[8,16]{1,0:T(8,128)}, u32[]{:S(2)}) copy-start(s32[8,16]{1,0:T(8,128)} %param.19) | copy-start | bytes 1540
  95.9 39.6 %copy-start.2 = (f32[32,4,512]{2,0,1:T(8,128)S(1)}, f32[32,4,512]{2,0,1:T(8,128)}, u32[]{:S(2)}) copy-start(f32[32,4,512]{2,0,1:T(8,128)} %rsqrt_multiply_fusion) | copy-start | bytes 786436
  95.9 39.6 %copy-start.5 = (s32[32,32]{1,0:T(8,128)S(1)}, s32[32,32]{1,0:T(8,128)}, u32[]{:S(2)}) copy-start(s32[32,32]{1,0:T(8,128)} %param.14) | copy-start | bytes 12292
  117.3 18.2 %all-to-all-start.2 = ((bf16[32,4,512]{2,1,0:T(4,128)(2,1)}), bf16[32,4,512]{2,1,0:T(4,128)(2,1)S(1)}, u32[]{:S(2)}, u32[]{:S(2)}) async-start(bf16[32,4,512]{2,1,0:T(4,128)(2,1)} %reshape.111), calls=%async_computation.2 | async-start | bytes 262144 | tf_op jit(solution)/shard_map/all_to_all | solution.py:84
  137.7 9.4 %all-to-all-start.3 = ((bf16[8,4,4,512]{3,1,2,0:T(4,128)(2,1)}), bf16[8,4,4,512]{3,1,2,0:T(4,128)(2,1)S(1)}, u32[]{:S(2)}, u32[]{:S(2)}) async-start(bf16[8,4,4,512]{3,1,2,0:T(4,128)(2,1)} %copy.25), calls=%async_computation.3 | async-start | bytes 262144 | tf_op jit(solution)/shard_map/all_to_all | solution.py:90
  155.4 30.2 %copy-start.1 = (bf16[1024,512]{1,0:T(8,128)(2,1)S(1)}, bf16[1024,512]{1,0:T(8,128)(2,1)}, u32[]{:S(2)}) copy-start(bf16[1024,512]{1,0:T(8,128)(2,1)} %reshape.110) | copy-start | bytes 3145732
Sparse Core Ops, SparseCore 0:
  54.1 32.5 all-gather.1

commit v4 on v3

v4 whole, which is shorter than its diff:
```python
import jax
import jax.numpy as jnp
from jax import lax
from jax.experimental import pallas as pl
from jax.experimental.pallas import tpu as pltpu
from jax.sharding import PartitionSpec as P

NZ, NY, NT = 8, 4, 8
BP, BLK = 32, 512
QP = 4
bf16, f32 = jnp.bfloat16, jnp.float32
Y_GROUPS = [[z * NY + y for y in range(NY)] for z in range(NZ)]
tie = lax.optimization_barrier


def along_z(x, d):
    pairs = [(z * NY + y, (z + d) % NZ * NY + y) for z in range(NZ) for y in range(NY)]
    return lax.ppermute(x, "grid", pairs)


def permute_all(x, dest):
    pairs = []
    for z in range(NZ):
        for y in range(NY):
            for t in range(NT):
                a, b, c = dest(z, y, t)
                pairs.append(((z * NY + y) * NT + t, (a * NY + b) * NT + c))
    return lax.ppermute(x, ("grid", "tile"), pairs)


def spread(x, axis, n, groups=None):
    copies = jnp.broadcast_to(x[None], (n,) + x.shape)
    return lax.all_to_all(copies, axis, 0, 0, tiled=True, axis_index_groups=groups)


def dot(u, v, cu, cv):
    return lax.dot_general(u, v, (((cu,), (cv,)), ((), ())), preferred_element_type=f32)


def region_kernel(flags, pot, lmo, out):
    strip = pl.program_id(0)
    acc = jnp.zeros(out.shape[1:], f32)
    for k in range(flags.shape[1]):
        rows = pl.ds(k * BLK, BLK)
        part = jnp.dot(pot[:, rows], lmo[rows, :], preferred_element_type=f32)
        acc = acc + jnp.where(flags[strip, k] != 0, part, 0.0)
    out[0] = acc.astype(out.dtype)


def region_product(flags, pot, lmo):
    strips = flags.shape[0]
    points, cols = pot.shape
    width = lmo.shape[1] // strips
    return pl.pallas_call(
        region_kernel,
        grid=(strips,),
        in_specs=[
            pl.BlockSpec(memory_space=pltpu.SMEM),
            pl.BlockSpec((points, cols), lambda i: (0, 0)),
            pl.BlockSpec((cols, width), lambda i: (0, i)),
        ],
        out_specs=pl.BlockSpec((1, points, width), lambda i: (i, 0, 0)),
        out_shape=jax.ShapeDtypeStruct((strips, points, width), bf16),
        compiler_params=pltpu.CompilerParams(vmem_limit_bytes=16 * 2**20),
        cost_estimate=pl.CostEstimate(
            flops=2 * points * cols * lmo.shape[1], bytes_accessed=2 * lmo.size, transcendentals=0
        ),
    )(flags, pot, lmo)


def shards(pv, sig, density, core, smask, centers, widths, coords, lmo, dom):
    g, j = lax.axis_index("grid"), lax.axis_index("tile")
    z, y = g // NY, g % NY
    nblk = smask.shape[0]
    cols = pv.shape[1]
    ids = jnp.arange(nblk, dtype=jnp.int32)
    named = jnp.any(sig[0][:, None] == ids[None, :], axis=0).astype(f32)
    own = lax.dynamic_slice_in_dim(named, 4 * j, 4, 0)
    masked = pv * jnp.repeat(own, BLK)[None, :].astype(bf16)

    xy = spread(masked, "grid", NY, Y_GROUPS)
    info = jnp.concatenate([named, coords.reshape(-1)])[None]
    piece = lax.dynamic_slice_in_dim(xy, y * BLK, BLK, 2)
    piece = piece.reshape(NT, NY, QP, BLK).transpose(1, 0, 2, 3).reshape(NY * BP, BLK)

    def product(x):
        rows = dot(x.reshape(-1, cols), density, 1, 1).astype(bf16)
        return rows.reshape(-1, 1, 16, BLK)

    def tile_sum(blocks):
        parts = jnp.concatenate(blocks, 1)
        parts = lax.all_to_all(parts, "tile", 0, 0, tiled=True)
        return jnp.sum(parts.astype(f32), axis=0).astype(bf16)

    blocks = {0: product(xy)}
    up = down = xy
    for s in range(1, 4):
        up, down = along_z(up, 1), along_z(down, -1)
        if s == 1:
            info, piece, up, down = tie((info, piece, up, down))
            info = permute_all(info, lambda a, b, c: (a, c // 2, 2 * b + c % 2))[0]
            piece = permute_all(piece, lambda a, b, c: (c, b, a))
        blocks[s], blocks[-s] = product(up), product(down)
        if s == 2:
            early = tile_sum([blocks[i] for i in (-2, -1, 0, 1, 2)])
    up, down = along_z(up[: NY // 2], 1), along_z(down[NY // 2 :], -1)
    blocks[4] = jnp.concatenate([product(up), product(down)], 0)
    x_col = lax.all_gather(piece, "tile", axis=0, tiled=True)

    named = info[:nblk]
    pts = lax.dynamic_slice_in_dim(info[nblk:].reshape(3, BP), 16 * (j % 2) + QP * y, QP, 1)
    off = centers.reshape(3, nblk, 1, BLK) - pts.reshape(3, 1, QP, 1)
    coef = 1.0 / jnp.sqrt(jnp.sum(off * off, axis=0) + widths.reshape(nblk, 1, BLK))
    coef = coef * named[:, None, None]
    blocks[4], coef, x_col = tie((blocks[4], coef, x_col))
    late = tile_sum([blocks[i] for i in (3, -3, 4)])

    around = [early[2], early[1], early[0], late[1], late[2], late[0], early[4], early[3]]
    term = lax.dynamic_slice_in_dim(jnp.stack(around + around), (NZ - z) % NZ, NZ, 0)
    term = lax.all_to_all(term.reshape(NZ * NY, QP, BLK), "grid", 0, 0, tiled=True)

    weighted = (coef * term.astype(f32)).astype(bf16)
    screened = jnp.einsum("kj,jpa->kpa", smask.astype(bf16), weighted, preferred_element_type=f32)
    mixed = jnp.einsum("kpc,ac->kpa", screened.astype(bf16), core, preferred_element_type=f32)
    pot = (coef * mixed).astype(bf16)
    pot = lax.all_to_all(pot.reshape(NT, 4, QP, BLK), "tile", 0, 0, tiled=True)
    pot = pot.transpose(0, 2, 1, 3).reshape(NT * QP, cols)

    local_ids = 4 * j + jnp.arange(4, dtype=jnp.int32)
    in_dom = jnp.any(dom[:, :, None] == local_ids[None, None, :], axis=1).astype(jnp.int32)
    w = region_product(in_dom, pot, lmo)
    w = lax.all_to_all(w, "tile", 0, 0, tiled=True)
    w = jnp.sum(w.astype(f32), axis=0).astype(bf16)
    w_all = spread(w, "grid", NZ * NY).reshape(-1, 256)
    return dot(w_all, x_col, 0, 0).astype(bf16)


def solution(mesh):
    in_specs = (
        P("grid", "tile"),
        P("grid", None),
        P("grid", "tile"),
        P(),
        P(),
        P(),
        P(),
        P(None, "grid"),
        P("tile", None),
        P(),
    )
    return jax.shard_map(
        shards, mesh=mesh, in_specs=in_specs, out_specs=P("tile", "grid"), check_vma=False
    )
```

time: 195 us -> 198 us (1.015)
  local copies, waits for them, and re-layouts: 12.4 us -> 22.4 us
  matrix products: 23.4 us -> 17.4 us
  starting transfers between devices: 38 us -> 33.1 us
  waiting for transfers between devices: 51.2 us -> 55.3 us
  Pallas kernels: 0 us -> 4.03 us
  other arithmetic: 5.55 us -> 3.36 us
    unnamed x20 -> x45, local copies, waits for them, and re-layouts: 0.88 us -> 14.9 us
    dot_general x14 -> x10, matrix products: 22 us -> 17 us  [dot(): lax.dot_general(u, v, (((cu,), (cv,)), ((), ())), preferred_element_type=...]
    reshape x3, local copies, waits for them, and re-layouts: 5.03 us -> 0.77 us  [the longest x2 0.73 us: shards(): piece.reshape(NT, NY, QP, BLK).transpose(1, 0, 2, 3).reshape(NY * BP, BLK)]
    ppermute x2, waiting for transfers between devices: 1.34 us -> 5.53 us  [permute_all(): return lax.ppermute(x, ('grid', 'tile'), pairs)]
    pallas_call x0 -> x1, Pallas kernels: none -> 4.03 us  [region_product(): pl.pallas_call(region_kernel, grid=(strips,), in_specs=[pl.BlockSpec(memo...]
    ppermute x2, starting transfers between devices: 6.58 us -> 2.57 us  [permute_all(): return lax.ppermute(x, ('grid', 'tile'), pairs)]
    transpose x1, local copies, waits for them, and re-layouts: 2.78 us -> 0.05 us  [shards(): piece.reshape(NT, NY, QP, BLK).transpose(1, 0, 2, 3).reshape(NY * BP, BLK)]
    slice x2, local copies, waits for them, and re-layouts: 0.04 us -> 2.38 us  [shards(): up, down = (along_z(up[:NY // 2], 1), along_z(down[NY // 2:], -1))]
  transfers between devices with their start and end apart: 14 -> 15, of which waited for: 9 -> 10; matrix products, arithmetic and copies ran while one was open for 9% -> 13% of each run, Pallas kernels for 0% -> 0%
where the time goes in v4:
time: 198 us; the launch traced here: 197 us
  waiting for transfers between devices  55.3 us (28%)
  blocking collectives  47.8 us (24%)
  starting transfers between devices  33.1 us (17%)
  local copies, waits for them, and re-layouts  22.4 us (11%)
  matrix products  17.4 us (9%)
  between operations  13.7 us (7%)
  Pallas kernels  4.03 us (2%)
  other arithmetic  3.36 us (2%)
    ppermute x8, waiting for transfers between devices, along_z(): return lax.ppermute(x, 'grid', pairs)  25.2 us
    all_to_all x1, blocking collectives, spread(): lax.all_to_all(copies, axis, 0, 0, tiled=True, axis_index_groups=groups)  21.3 us
    all_to_all x1, blocking collectives, shards(): lax.all_to_all(term.reshape(NZ * NY, QP, BLK), 'grid', 0, 0, tiled=True)  18 us
    dot_general x10, matrix products, dot(): lax.dot_general(u, v, (((cu,), (cv,)), ((), ())), preferred_element_type=...  17 us
    ppermute x8, starting transfers between devices, along_z(): return lax.ppermute(x, 'grid', pairs)  15.3 us
    unnamed x45, local copies, waits for them, and re-layouts  14.9 us
    all_to_all x1, waiting for transfers between devices, spread(): lax.all_to_all(copies, axis, 0, 0, tiled=True, axis_index_groups=groups)  9.47 us
    all_to_all x2, waiting for transfers between devices, tile_sum(): parts = lax.all_to_all(parts, 'tile', 0, 0, tiled=True)  9.27 us
  transfers between devices with their start and end apart: 15, of which 10 were waited for; matrix products, arithmetic and copies ran while one was open for 13% of the time, Pallas kernels for 0%

profile of v4, /device:TPU:32, one launch (start us, length us, event | category | flops | bytes accessed | tf_op | source)
XLA Modules:
  0.0 197.1 jit_solution(3406007416319531102)
XLA Ops:
  6.5 0.9 fusion.11
  7.6 0.9 broadcast_multiply_fusion
  8.5 0.9 broadcast_in_dim.10
  9.4 4.5 %all-to-all-start = ((bf16[4,32,2048]{2,1,0:T(8,128)(2,1)}), bf16[4,32,2048]{2,1,0:T(8,128)(2,1)S(1)}, u32[]{:S(2)}, u32[]{:S(2)}) async-start(bf16[4,32,2048]{2,1,0:T(8,128)(2,1)} %broadcast_in_dim.10), calls=%async_computation | async-start | bytes 1048576 | tf_op jit(solution)/shard_map/all_to_all | solution.py:33
  13.9 9.5 %all-to-all-done = bf16[4,32,2048]{2,1,0:T(8,128)(2,1)S(1)} async-done(((bf16[4,32,2048]{2,1,0:T(8,128)(2,1)}), bf16[4,32,2048]{2,1,0:T(8,128)(2,1)S(1)}, u32[]{:S(2)}, u32[]{:S(2)}) %all-to-all-start) | async-done | bytes 524320 | tf_op jit(solution)/shard_map/all_to_all | solution.py:33
  23.4 1.9 collective-permute-start
  25.7 0.7 reshape.107
  26.4 0.8 convolution_convert_fusion.5
  27.3 8.5 %collective-permute-done.1 = bf16[4,32,2048]{2,1,0:T(8,128)(2,1)} collective-permute-done((bf16[4,32,2048]{2,1,0:T(8,128)(2,1)S(1)}, bf16[4,32,2048]{2,1,0:T(8,128)(2,1)}, u32[]{:S(2)}, u32[]{:S(2)}) %collective-permute-start.1) | collective-permute-done | bytes 524320 | tf_op jit(solution)/shard_map/ppermute | solution.py:18
  35.8 3.8 %collective-permute-done = bf16[4,32,2048]{2,1,0:T(8,128)(2,1)} collective-permute-done((bf16[4,32,2048]{2,1,0:T(8,128)(2,1)S(1)}, bf16[4,32,2048]{2,1,0:T(8,128)(2,1)}, u32[]{:S(2)}, u32[]{:S(2)}) %collective-permute-start) | collective-permute-done | bytes 524320 | tf_op jit(solution)/shard_map/ppermute | solution.py:18
  40.2 3.0 %collective-permute-start.5 = (bf16[4,32,2048]{2,1,0:T(8,128)(2,1)}, bf16[4,32,2048]{2,1,0:T(8,128)(2,1)}, u32[]{:S(2)}, u32[]{:S(2)}) collective-permute-start(bf16[4,32,2048]{2,1,0:T(8,128)(2,1)} %collective-permute-done.1), channel_id=1, source_target_pairs={{0,224},{8,232},{16,240},{24,248},{32,0},{40,8},{48,16},{56,24},{6... | collective-permute-start | bytes 1572872 | tf_op jit(solution)/shard_map/ppermute | solution.py:18
  43.2 1.9 convolution_convert_fusion.6
  45.2 1.9 convolution_convert_fusion.4
  47.1 1.9 collective-permute-start.9
  49.6 5.5 %collective-permute-done.9 = bf16[128,512]{1,0:T(8,128)(2,1)S(1)} collective-permute-done((bf16[128,512]{1,0:T(8,128)(2,1)}, bf16[128,512]{1,0:T(8,128)(2,1)S(1)}, u32[]{:S(2)}, u32[]{:S(2)}) %collective-permute-start.9) | collective-permute-done | bytes 131104 | tf_op jit(solution)/shard_map/ppermute | solution.py:28
  55.8 3.3 %collective-permute-done.2 = bf16[4,32,2048]{2,1,0:T(8,128)(2,1)} collective-permute-done((bf16[4,32,2048]{2,1,0:T(8,128)(2,1)}, bf16[4,32,2048]{2,1,0:T(8,128)(2,1)}, u32[]{:S(2)}, u32[]{:S(2)}) %collective-permute-start.2) | collective-permute-done | bytes 524320 | tf_op jit(solution)/shard_map/ppermute | solution.py:18
  59.1 1.9 convolution_convert_fusion.3
  60.9 1.9 convolution_convert_fusion.7
  62.8 7.6 %collective-permute-start.3 = (bf16[4,32,2048]{2,1,0:T(8,128)(2,1)}, bf16[4,32,2048]{2,1,0:T(8,128)(2,1)}, u32[]{:S(2)}, u32[]{:S(2)}) collective-permute-start(bf16[4,32,2048]{2,1,0:T(8,128)(2,1)} %collective-permute-done.2), channel_id=1, source_target_pairs={{0,32},{8,40},{16,48},{24,56},{32,64},{40,72},{48,80},{56,88},{64,... | collective-permute-start | bytes 1572872 | tf_op jit(solution)/shard_map/ppermute | solution.py:18
  70.5 0.7 constant_dynamic-update-slice_fusion.4
  71.1 0.7 constant_dynamic-update-slice_fusion.3
  71.8 0.7 constant_dynamic-update-slice_fusion.2
  72.5 0.7 constant_dynamic-update-slice_fusion.1
  73.2 0.7 constant_dynamic-update-slice_fusion
  73.8 3.9 %all-to-all-start.1 = ((bf16[8,5,16,512]{3,2,1,0:T(8,128)(2,1)}), bf16[8,5,16,512]{3,2,1,0:T(8,128)(2,1)S(1)}, u32[]{:S(2)}, u32[]{:S(2)}) async-start(bf16[8,5,16,512]{3,2,1,0:T(8,128)(2,1)} %constant_dynamic-update-slice_fusion), calls=%async_computation.1 | async-start | bytes 1310720 | tf_op jit(solution)/shard_map/all_to_all | solution.py:92
  77.7 5.1 %collective-permute-done.3 = bf16[4,32,2048]{2,1,0:T(8,128)(2,1)} collective-permute-done((bf16[4,32,2048]{2,1,0:T(8,128)(2,1)}, bf16[4,32,2048]{2,1,0:T(8,128)(2,1)}, u32[]{:S(2)}, u32[]{:S(2)}) %collective-permute-start.3) | collective-permute-done | bytes 524320 | tf_op jit(solution)/shard_map/ppermute | solution.py:18
  82.8 1.7 slice.49
  84.4 2.5 %collective-permute-start.4 = (bf16[2,32,2048]{2,1,0:T(8,128)(2,1)}, bf16[2,32,2048]{2,1,0:T(8,128)(2,1)}, u32[]{:S(2)}, u32[]{:S(2)}) collective-permute-start(bf16[2,32,2048]{2,1,0:T(8,128)(2,1)} %slice.49), channel_id=1, source_target_pairs={{0,32},{8,40},{16,48},{24,56},{32,64},{40,72},{48,80},{56,88},{64,... | collective-permute-start | bytes 786440 | tf_op jit(solution)/shard_map/ppermute | solution.py:18
  86.9 2.5 %convolution_convert_fusion.2 = bf16[128,512]{1,0:T(8,128)(2,1)} fusion(bf16[128,2048]{1,0:T(8,128)(2,1)} %bitcast.25, bf16[512,2048]{1,0:T(8,128)(2,1)S(1)} %copy-done), kind=kOutput, calls=%fused_computation.4 | convolution fusion | flops 268500992 | bytes 2752512 | tf_op jit(solution)/shard_map/dot_general | solution.py:37
  89.4 1.5 convolution_convert_fusion.1
  90.9 0.7 slice.50
  91.7 1.6 all-to-all-done.1
  94.0 1.7 convolution_convert_fusion.10
  95.8 4.6 %collective-permute-done.7 = bf16[2,32,2048]{2,1,0:T(8,128)(2,1)} collective-permute-done((bf16[2,32,2048]{2,1,0:T(8,128)(2,1)}, bf16[2,32,2048]{2,1,0:T(8,128)(2,1)}, u32[]{:S(2)}, u32[]{:S(2)}) %collective-permute-start.7) | collective-permute-done | bytes 262176 | tf_op jit(solution)/shard_map/ppermute | solution.py:18
  100.3 1.7 convolution_convert_fusion.9
  102.1 0.8 pad_maximum_fusion
  103.0 3.6 %all-to-all-start.2 = ((bf16[8,3,16,512]{3,2,1,0:T(8,128)(2,1)}), bf16[8,3,16,512]{3,2,1,0:T(8,128)(2,1)S(1)}, u32[]{:S(2)}, u32[]{:S(2)}) async-start(bf16[8,3,16,512]{3,2,1,0:T(8,128)(2,1)} %pad_maximum_fusion), calls=%async_computation.2 | async-start | bytes 786432 | tf_op jit(solution)/shard_map/all_to_all | solution.py:92
  107.8 7.6 %all-to-all-done.2 = bf16[8,3,16,512]{3,2,1,0:T(8,128)(2,1)S(1)} async-done(((bf16[8,3,16,512]{3,2,1,0:T(8,128)(2,1)}), bf16[8,3,16,512]{3,2,1,0:T(8,128)(2,1)S(1)}, u32[]{:S(2)}, u32[]{:S(2)}) %all-to-all-start.2) | async-done | bytes 393248 | tf_op jit(solution)/shard_map/all_to_all | solution.py:92
  122.2 0.9 constant_dynamic-slice_fusion
  123.1 18.0 %all_to_all.35 = bf16[32,4,512]{2,1,0:T(4,128)(2,1)S(1)} all-to-all(bf16[32,4,512]{2,1,0:T(4,128)(2,1)S(1)} %reshape.127), channel_id=1, replica_groups=mesh['grid'=32,'tile'=8] {'grid'}, dimensions={0} | all-to-all | bytes 262144 | tf_op jit(solution)/shard_map/all_to_all | solution.py:120
  141.6 0.7 copy.41
  142.3 3.4 %all-to-all-start.4 = ((bf16[8,4,4,512]{3,1,2,0:T(4,128)(2,1)}), bf16[8,4,4,512]{3,1,2,0:T(4,128)(2,1)S(1)}, u32[]{:S(2)}, u32[]{:S(2)}) async-start(bf16[8,4,4,512]{3,1,2,0:T(4,128)(2,1)} %copy.41), calls=%async_computation.4 | async-start | bytes 262144 | tf_op jit(solution)/shard_map/all_to_all | solution.py:126
  146.0 5.7 %all-to-all-done.4 = bf16[8,4,4,512]{3,1,2,0:T(4,128)(2,1)S(1)} async-done(((bf16[8,4,4,512]{3,1,2,0:T(4,128)(2,1)}), bf16[8,4,4,512]{3,1,2,0:T(4,128)(2,1)S(1)}, u32[]{:S(2)}, u32[]{:S(2)}) %all-to-all-start.4) | async-done | bytes 131104 | tf_op jit(solution)/shard_map/all_to_all | solution.py:126
  151.8 3.4 %copy-done.1 = bf16[2048,2048]{1,0:T(8,128)(2,1)S(1)} copy-done((bf16[2048,2048]{1,0:T(8,128)(2,1)S(1)}, bf16[2048,2048]{1,0:T(8,128)(2,1)}, u32[]{:S(2)}) %copy-start.1) | copy-done | bytes 8388632
  155.1 4.0 %shard_map.100 = bf16[8,32,256]{2,1,0:T(8,128)(2,1)S(1)} custom-call(s32[8,4]{1,0:T(8,128)S(1)} %convert_element_type.72.flags, bf16[32,2048]{1,0:T(8,128)(2,1)S(1)} %bitcast.87, bf16[2048,2048]{1,0:T(8,128)(2,1)S(1)} %copy-done.1), custom_call_target="tpu_custom_call" | custom-call | flops 268435456 | bytes 8388608 | tf_op jit(solution)/shard_map/pallas_call | solution.py:54
  159.2 8.5 %all_to_all.36 = bf16[8,32,256]{2,1,0:T(8,128)(2,1)S(1)} all-to-all(bf16[8,32,256]{2,1,0:T(8,128)(2,1)S(1)} %shard_map.100), channel_id=1, replica_groups=mesh['grid'=32,'tile'=8] {'tile'}, dimensions={0} | all-to-all | bytes 262144 | tf_op jit(solution)/shard_map/all_to_all | solution.py:132
  167.8 21.3 %all_to_all.37 = bf16[32,32,256]{2,1,0:T(8,128)(2,1)S(1)} all-to-all(bf16[32,32,256]{2,1,0:T(8,128)(2,1)S(1)} %broadcast_in_dim.11), channel_id=1, replica_groups=mesh['grid'=32,'tile'=8] {'grid'}, dimensions={0} | all-to-all | bytes 1048576 | tf_op jit(solution)/shard_map/all_to_all | solution.py:33
  189.0 1.2 convolution_convert_fusion
  (79 shorter events, 12.1 us)
Async XLA Ops:
  6.5 19.9 %copy-start = (bf16[512,2048]{1,0:T(8,128)(2,1)S(1)}, bf16[512,2048]{1,0:T(8,128)(2,1)}, u32[]{:S(2)}) copy-start(bf16[512,2048]{1,0:T(8,128)(2,1)} %param.12) | copy-start | bytes 6291460
  6.5 18.8 %copy-start.10 = (f32[3,32]{1,0:T(4,128)S(1)}, f32[3,32]{1,0:T(4,128)}, u32[]{:S(2)}) copy-start(f32[3,32]{1,0:T(4,128)} %param.17) | copy-start | bytes 1156
  6.5 18.9 %copy-start.7 = (f32[16384]{0:T(1024)S(1)}, f32[16384]{0:T(1024)}, u32[]{:S(2)}) copy-start(f32[16384]{0:T(1024)} %param.16) | copy-start | bytes 196612
  6.5 18.9 %copy-start.5 = (f32[3,16384]{1,0:T(4,128)S(1)}, f32[3,16384]{1,0:T(4,128)}, u32[]{:S(2)}) copy-start(f32[3,16384]{1,0:T(4,128)} %param.15) | copy-start | bytes 589828
  9.4 13.9 %all-to-all-start = ((bf16[4,32,2048]{2,1,0:T(8,128)(2,1)}), bf16[4,32,2048]{2,1,0:T(8,128)(2,1)S(1)}, u32[]{:S(2)}, u32[]{:S(2)}) async-start(bf16[4,32,2048]{2,1,0:T(8,128)(2,1)} %broadcast_in_dim.10), calls=%async_computation | async-start | bytes 1048576 | tf_op jit(solution)/shard_map/all_to_all | solution.py:33
  13.8 88.3 %all-gather.2.cloned.1.call-start = ((), (), s32[]{:S(2)}) async-start(), calls=%async_computation.7 | async-start | bytes 1179648 | tf_op jit(solution)/shard_map/all_gather | solution.py:108
  23.3 12.5 %collective-permute-start.1 = (bf16[4,32,2048]{2,1,0:T(8,128)(2,1)S(1)}, bf16[4,32,2048]{2,1,0:T(8,128)(2,1)}, u32[]{:S(2)}, u32[]{:S(2)}) collective-permute-start(bf16[4,32,2048]{2,1,0:T(8,128)(2,1)S(1)} %all-to-all-done), channel_id=1, source_target_pairs={{0,224},{8,232},{16,240},{24,248},{32,0},{40,8},{48,16},{56,24},{6... | collective-permute-start | bytes 1572872 | tf_op jit(solution)/shard_map/ppermute | solution.py:18
  23.4 16.1 %collective-permute-start = (bf16[4,32,2048]{2,1,0:T(8,128)(2,1)S(1)}, bf16[4,32,2048]{2,1,0:T(8,128)(2,1)}, u32[]{:S(2)}, u32[]{:S(2)}) collective-permute-start(bf16[4,32,2048]{2,1,0:T(8,128)(2,1)S(1)} %all-to-all-done), channel_id=1, source_target_pairs={{0,32},{8,40},{16,48},{24,56},{32,64},{40,72},{48,80},{56,88},{64,... | collective-permute-start | bytes 1572872 | tf_op jit(solution)/shard_map/ppermute | solution.py:18
  39.6 9.5 %collective-permute-start.8 = (f32[1,128]{1,0:T(1,128)S(1)}, f32[1,128]{1,0:T(1,128)S(1)}, u32[]{:S(2)}, u32[]{:S(2)}) collective-permute-start(f32[1,128]{1,0:T(1,128)S(1)} %maximum_bitcast_fusion), channel_id=1, source_target_pairs={{0,0},{1,1},{2,8},{3,9},{4,16},{5,17},{6,24},{7,25},{8,2},{9,3},{1... | collective-permute-start | bytes 1544 | tf_op jit(solution)/shard_map/ppermute | solution.py:28
  40.2 20.7 %collective-permute-start.5 = (bf16[4,32,2048]{2,1,0:T(8,128)(2,1)}, bf16[4,32,2048]{2,1,0:T(8,128)(2,1)}, u32[]{:S(2)}, u32[]{:S(2)}) collective-permute-start(bf16[4,32,2048]{2,1,0:T(8,128)(2,1)} %collective-permute-done.1), channel_id=1, source_target_pairs={{0,224},{8,232},{16,240},{24,248},{32,0},{40,8},{48,16},{56,24},{6... | collective-permute-start | bytes 1572872 | tf_op jit(solution)/shard_map/ppermute | solution.py:18
  45.2 13.9 %collective-permute-start.2 = (bf16[4,32,2048]{2,1,0:T(8,128)(2,1)}, bf16[4,32,2048]{2,1,0:T(8,128)(2,1)}, u32[]{:S(2)}, u32[]{:S(2)}) collective-permute-start(bf16[4,32,2048]{2,1,0:T(8,128)(2,1)} %collective-permute-done), channel_id=1, source_target_pairs={{0,32},{8,40},{16,48},{24,56},{32,64},{40,72},{48,80},{56,88},{64,... | collective-permute-start | bytes 1572872 | tf_op jit(solution)/shard_map/ppermute | solution.py:18
  47.1 8.0 %collective-permute-start.9 = (bf16[128,512]{1,0:T(8,128)(2,1)}, bf16[128,512]{1,0:T(8,128)(2,1)S(1)}, u32[]{:S(2)}, u32[]{:S(2)}) collective-permute-start(bf16[128,512]{1,0:T(8,128)(2,1)} %reshape.107), channel_id=1, source_target_pairs={{0,0},{1,32},{2,64},{3,96},{4,128},{5,160},{6,192},{7,224},{8,8},{... | collective-permute-start | bytes 393224 | tf_op jit(solution)/shard_map/ppermute | solution.py:28
  55.1 0.6 copy-start.6
  62.8 20.0 %collective-permute-start.3 = (bf16[4,32,2048]{2,1,0:T(8,128)(2,1)}, bf16[4,32,2048]{2,1,0:T(8,128)(2,1)}, u32[]{:S(2)}, u32[]{:S(2)}) collective-permute-start(bf16[4,32,2048]{2,1,0:T(8,128)(2,1)} %collective-permute-done.2), channel_id=1, source_target_pairs={{0,32},{8,40},{16,48},{24,56},{32,64},{40,72},{48,80},{56,88},{64,... | collective-permute-start | bytes 1572872 | tf_op jit(solution)/shard_map/ppermute | solution.py:18
  70.5 19.0 %collective-permute-start.6 = (bf16[4,32,2048]{2,1,0:T(8,128)(2,1)}, bf16[4,32,2048]{2,1,0:T(8,128)(2,1)S(1)}, u32[]{:S(2)}, u32[]{:S(2)}) collective-permute-start(bf16[4,32,2048]{2,1,0:T(8,128)(2,1)} %collective-permute-done.5), channel_id=1, source_target_pairs={{0,224},{8,232},{16,240},{24,248},{32,0},{40,8},{48,16},{56,24},{6... | collective-permute-start | bytes 1572872 | tf_op jit(solution)/shard_map/ppermute | solution.py:18
  73.8 19.5 %all-to-all-start.1 = ((bf16[8,5,16,512]{3,2,1,0:T(8,128)(2,1)}), bf16[8,5,16,512]{3,2,1,0:T(8,128)(2,1)S(1)}, u32[]{:S(2)}, u32[]{:S(2)}) async-start(bf16[8,5,16,512]{3,2,1,0:T(8,128)(2,1)} %constant_dynamic-update-slice_fusion), calls=%async_computation.1 | async-start | bytes 1310720 | tf_op jit(solution)/shard_map/all_to_all | solution.py:92
  84.4 9.6 %collective-permute-start.4 = (bf16[2,32,2048]{2,1,0:T(8,128)(2,1)}, bf16[2,32,2048]{2,1,0:T(8,128)(2,1)}, u32[]{:S(2)}, u32[]{:S(2)}) collective-permute-start(bf16[2,32,2048]{2,1,0:T(8,128)(2,1)} %slice.49), channel_id=1, source_target_pairs={{0,32},{8,40},{16,48},{24,56},{32,64},{40,72},{48,80},{56,88},{64,... | collective-permute-start | bytes 786440 | tf_op jit(solution)/shard_map/ppermute | solution.py:18
  91.7 8.7 %collective-permute-start.7 = (bf16[2,32,2048]{2,1,0:T(8,128)(2,1)}, bf16[2,32,2048]{2,1,0:T(8,128)(2,1)}, u32[]{:S(2)}, u32[]{:S(2)}) collective-permute-start(bf16[2,32,2048]{2,1,0:T(8,128)(2,1)} %slice.50), channel_id=1, source_target_pairs={{0,224},{8,232},{16,240},{24,248},{32,0},{40,8},{48,16},{56,24},{6... | collective-permute-start | bytes 786440 | tf_op jit(solution)/shard_map/ppermute | solution.py:18
  94.0 8.1 %copy-start.3 = (bf16[128,512]{1,0:T(8,128)(2,1)S(1)}, bf16[128,512]{1,0:T(8,128)(2,1)}, u32[]{:S(2)}) copy-start(bf16[128,512]{1,0:T(8,128)(2,1)} %convolution_convert_fusion.2) | copy-start | bytes 393220
  94.0 8.1 %copy-start.4 = (bf16[128,512]{1,0:T(8,128)(2,1)S(1)}, bf16[128,512]{1,0:T(8,128)(2,1)}, u32[]{:S(2)}) copy-start(bf16[128,512]{1,0:T(8,128)(2,1)} %convolution_convert_fusion.1) | copy-start | bytes 393220
  102.1 39.1 %copy-start.2 = (bf16[512,512]{1,0:T(8,128)(2,1)S(1)}, bf16[512,512]{1,0:T(8,128)(2,1)}, u32[]{:S(2)}) copy-start(bf16[512,512]{1,0:T(8,128)(2,1)} %param.13) | copy-start | bytes 1572868
  102.1 39.1 %copy-start.8 = (s32[32,32]{1,0:T(8,128)S(1)}, s32[32,32]{1,0:T(8,128)}, u32[]{:S(2)}) copy-start(s32[32,32]{1,0:T(8,128)} %param.14) | copy-start | bytes 12292
  103.0 42.7 %copy-start.9 = (s32[8,16]{1,0:T(8,128)S(1)}, s32[8,16]{1,0:T(8,128)}, u32[]{:S(2)}) copy-start(s32[8,16]{1,0:T(8,128)} %param.19) | copy-start | bytes 1540
  103.0 12.5 %all-to-all-start.2 = ((bf16[8,3,16,512]{3,2,1,0:T(8,128)(2,1)}), bf16[8,3,16,512]{3,2,1,0:T(8,128)(2,1)S(1)}, u32[]{:S(2)}, u32[]{:S(2)}) async-start(bf16[8,3,16,512]{3,2,1,0:T(8,128)(2,1)} %pad_maximum_fusion), calls=%async_computation.2 | async-start | bytes 786432 | tf_op jit(solution)/shard_map/all_to_all | solution.py:92
  142.3 9.4 %all-to-all-start.4 = ((bf16[8,4,4,512]{3,1,2,0:T(4,128)(2,1)}), bf16[8,4,4,512]{3,1,2,0:T(4,128)(2,1)S(1)}, u32[]{:S(2)}, u32[]{:S(2)}) async-start(bf16[8,4,4,512]{3,1,2,0:T(4,128)(2,1)} %copy.41), calls=%async_computation.4 | async-start | bytes 262144 | tf_op jit(solution)/shard_map/all_to_all | solution.py:126
  151.7 3.4 %copy-start.1 = (bf16[2048,2048]{1,0:T(8,128)(2,1)S(1)}, bf16[2048,2048]{1,0:T(8,128)(2,1)}, u32[]{:S(2)}) copy-start(bf16[2048,2048]{1,0:T(8,128)(2,1)} %lmo.1) | copy-start | bytes 25165828
  155.1 33.9 %copy-start.11 = (bf16[1024,512]{1,0:T(8,128)(2,1)S(1)}, bf16[1024,512]{1,0:T(8,128)(2,1)}, u32[]{:S(2)}) copy-start(bf16[1024,512]{1,0:T(8,128)(2,1)} %all-gather.2.cloned.1.call-done) | copy-start | bytes 3145732
Sparse Core Ops, SparseCore 0:
  55.9 38.9 all-gather.1

commit v5 on v4

--- a/solution.py
+++ b/solution.py
@@ -37,35 +37,65 @@
     return lax.dot_general(u, v, (((cu,), (cv,)), ((), ())), preferred_element_type=f32)
 
 
-def region_kernel(flags, pot, lmo, out):
-    strip = pl.program_id(0)
-    acc = jnp.zeros(out.shape[1:], f32)
-    for k in range(flags.shape[1]):
-        rows = pl.ds(k * BLK, BLK)
-        part = jnp.dot(pot[:, rows], lmo[rows, :], preferred_element_type=f32)
-        acc = acc + jnp.where(flags[strip, k] != 0, part, 0.0)
-    out[0] = acc.astype(out.dtype)
+def region_kernel(flags, pot, lmo, out, acc):
+    step = pl.program_id(0)
+    strips, _, width = acc.shape
+
+    @pl.when(step == 0)
+    def _():
+        acc[...] = jnp.zeros_like(acc)
+
+    for strip in range(strips):
+
+        @pl.when(flags[strip, step * lmo.shape[0] // BLK] != 0)
+        def _():
+            part = lmo[:, strip * width : (strip + 1) * width]
+            acc[strip] += jnp.dot(pot[...], part, preferred_element_type=f32)
+
+    @pl.when(step == pl.num_programs(0) - 1)
+    def _():
+        out[...] = acc[...].astype(out.dtype)
 
 
-def region_product(flags, pot, lmo):
+def region_product(flags, pot, lmo, rows=256):
     strips = flags.shape[0]
     points, cols = pot.shape
     width = lmo.shape[1] // strips
     return pl.pallas_call(
         region_kernel,
-        grid=(strips,),
+        grid=(cols // rows,),
         in_specs=[
             pl.BlockSpec(memory_space=pltpu.SMEM),
-            pl.BlockSpec((points, cols), lambda i: (0, 0)),
-            pl.BlockSpec((cols, width), lambda i: (0, i)),
+            pl.BlockSpec((points, rows), lambda i: (0, i)),
+            pl.BlockSpec((rows, lmo.shape[1]), lambda i: (i, 0)),
         ],
-        out_specs=pl.BlockSpec((1, points, width), lambda i: (i, 0, 0)),
+        out_specs=pl.BlockSpec((strips, points, width), lambda i: (0, 0, 0)),
         out_shape=jax.ShapeDtypeStruct((strips, points, width), bf16),
-        compiler_params=pltpu.CompilerParams(vmem_limit_bytes=16 * 2**20),
+        scratch_shapes=[pltpu.VMEM((strips, points, width), f32)],
+        compiler_params=pltpu.CompilerParams(vmem_limit_bytes=52 * 2**20),
         cost_estimate=pl.CostEstimate(
             flops=2 * points * cols * lmo.shape[1], bytes_accessed=2 * lmo.size, transcendentals=0
         ),
     )(flags, pot, lmo)
+
+
+def place_kernel(z, parts, out):
+    for m in range(NZ):
+        total = jnp.sum(parts[:, m].astype(f32), axis=0).astype(out.dtype)
+        out[pl.ds((z[0] + m) % NZ, 1)] = total[None]
+
+
+def sum_and_place(z, parts):
+    whole = pl.BlockSpec(memory_space=pltpu.VMEM)
+    return pl.pallas_call(
+        place_kernel,
+        in_specs=[pl.BlockSpec(memory_space=pltpu.SMEM), whole],
+        out_specs=whole,
+        out_shape=jax.ShapeDtypeStruct(parts.shape[1:], bf16),
+        cost_estimate=pl.CostEstimate(
+            flops=parts.size, bytes_accessed=2 * parts.size, transcendentals=0
+        ),
+    )(z.reshape(1), parts)
 
 
 def shards(pv, sig, density, core, smask, centers, widths, coords, lmo, dom):
@@ -83,41 +113,34 @@
     piece = lax.dynamic_slice_in_dim(xy, y * BLK, BLK, 2)
     piece = piece.reshape(NT, NY, QP, BLK).transpose(1, 0, 2, 3).reshape(NY * BP, BLK)
 
-    def product(x):
+    def product(buf, x, slot, row=0):
         rows = dot(x.reshape(-1, cols), density, 1, 1).astype(bf16)
-        return rows.reshape(-1, 1, 16, BLK)
+        return lax.dynamic_update_slice(buf, rows.reshape(-1, 1, 16, BLK), (row, slot, 0, 0))
 
-    def tile_sum(blocks):
-        parts = jnp.concatenate(blocks, 1)
-        parts = lax.all_to_all(parts, "tile", 0, 0, tiled=True)
-        return jnp.sum(parts.astype(f32), axis=0).astype(bf16)
-
-    blocks = {0: product(xy)}
+    info = permute_all(info, lambda a, b, c: (a, c // 2, 2 * b + c % 2))[0]
+    info, xy = tie((info, xy))
+    parts = product(jnp.zeros((NT, NZ, 16, BLK), bf16), xy, 0)
     up = down = xy
     for s in range(1, 4):
         up, down = along_z(up, 1), along_z(down, -1)
-        if s == 1:
-            info, piece, up, down = tie((info, piece, up, down))
-            info = permute_all(info, lambda a, b, c: (a, c // 2, 2 * b + c % 2))[0]
-            piece = permute_all(piece, lambda a, b, c: (c, b, a))
-        blocks[s], blocks[-s] = product(up), product(down)
-        if s == 2:
-            early = tile_sum([blocks[i] for i in (-2, -1, 0, 1, 2)])
+        parts = product(parts, up, NZ - s)
+        parts = product(parts, down, s)
     up, down = along_z(up[: NY // 2], 1), along_z(down[NY // 2 :], -1)
-    blocks[4] = jnp.concatenate([product(up), product(down)], 0)
-    x_col = lax.all_gather(piece, "tile", axis=0, tiled=True)
+    parts = product(parts, up, 4)
+    parts = product(parts, down, 4, NT // 2)
 
     named = info[:nblk]
     pts = lax.dynamic_slice_in_dim(info[nblk:].reshape(3, BP), 16 * (j % 2) + QP * y, QP, 1)
     off = centers.reshape(3, nblk, 1, BLK) - pts.reshape(3, 1, QP, 1)
     coef = 1.0 / jnp.sqrt(jnp.sum(off * off, axis=0) + widths.reshape(nblk, 1, BLK))
     coef = coef * named[:, None, None]
-    blocks[4], coef, x_col = tie((blocks[4], coef, x_col))
-    late = tile_sum([blocks[i] for i in (3, -3, 4)])
-
-    around = [early[2], early[1], early[0], late[1], late[2], late[0], early[4], early[3]]
-    term = lax.dynamic_slice_in_dim(jnp.stack(around + around), (NZ - z) % NZ, NZ, 0)
-    term = lax.all_to_all(term.reshape(NZ * NY, QP, BLK), "grid", 0, 0, tiled=True)
+    parts, coef, piece = tie((parts, coef, piece))
+    piece = permute_all(piece, lambda a, b, c: (c, b, a))
+    parts = lax.all_to_all(parts, "tile", 0, 0, tiled=True)
+    term = sum_and_place(z, parts).reshape(NZ * NY, QP, BLK)
+    term, piece = tie((term, piece))
+    x_col = lax.all_gather(piece, "tile", axis=0, tiled=True)
+    term = lax.all_to_all(term, "grid", 0, 0, tiled=True)
 
     weighted = (coef * term.astype(f32)).astype(bf16)
     screened = jnp.einsum("kj,jpa->kpa", smask.astype(bf16), weighted, preferred_element_type=f32)

time: 198 us -> 186 us (0.939)
  blocking collectives: 47.8 us -> 29.5 us
  local copies, waits for them, and re-layouts: 22.4 us -> 12.2 us
  starting transfers between devices: 33.1 us -> 43.3 us
  Pallas kernels: 4.03 us -> 10.4 us
  waiting for transfers between devices: 55.3 us -> 60.3 us
  matrix products: 17.4 us -> 13.3 us
    all_to_all x1 -> x0, blocking collectives: 18 us -> none  [shards(): lax.all_to_all(term.reshape(NZ * NY, QP, BLK), 'grid', 0, 0, tiled=True)]
    unnamed x45 -> x16, local copies, waits for them, and re-layouts: 14.9 us -> 1.17 us
    all_to_all x2, waiting for transfers between devices: 9.27 us -> 21.6 us  [the longest x1 12.8 us: shards(): parts = lax.all_to_all(parts, 'tile', 0, 0, tiled=True)]
    all_to_all x2, starting transfers between devices: 7.43 us -> 16.8 us  [the longest x1 11.7 us: shards(): term = lax.all_to_all(term, 'grid', 0, 0, tiled=True)]
    pallas_call x1 -> x2, Pallas kernels: 4.03 us -> 10.4 us  [the longest x1 8.42 us: region_product(): pl.pallas_call(region_kernel, grid=(cols // rows,), in_specs=[pl.BlockSpe...]
    dynamic_update_slice x0 -> x9, local copies, waits for them, and re-layouts: none -> 6.39 us  [product(): lax.dynamic_update_slice(buf, rows.reshape(-1, 1, 16, BLK), (row, slot, 0...]
    ppermute x2, waiting for transfers between devices: 5.53 us -> 0.01 us  [permute_all(): return lax.ppermute(x, ('grid', 'tile'), pairs)]
    dot_general x10, matrix products: 17 us -> 11.9 us  [dot(): lax.dot_general(u, v, (((cu,), (cv,)), ((), ())), preferred_element_type=...]
  transfers between devices with their start and end apart: 15 -> 15, of which waited for: 10 -> 10; matrix products, arithmetic and copies ran while one was open for 13% -> 11% of each run, Pallas kernels for 0% -> 6%
where the time goes in v5:
time: 186 us; the launch traced here: 185 us
  waiting for transfers between devices  60.3 us (32%)
  starting transfers between devices  43.3 us (23%)
  blocking collectives  29.5 us (16%)
  between operations  13.7 us (7%)
  matrix products  13.3 us (7%)
  local copies, waits for them, and re-layouts  12.2 us (7%)
  Pallas kernels  10.4 us (6%)
  other arithmetic  2.37 us (1%)
    ppermute x8, waiting for transfers between devices, along_z(): return lax.ppermute(x, 'grid', pairs)  23.1 us
    all_to_all x1, blocking collectives, spread(): lax.all_to_all(copies, axis, 0, 0, tiled=True, axis_index_groups=groups)  21 us
    all_to_all x1, waiting for transfers between devices, shards(): parts = lax.all_to_all(parts, 'tile', 0, 0, tiled=True)  12.8 us
    ppermute x8, starting transfers between devices, along_z(): return lax.ppermute(x, 'grid', pairs)  12.8 us
    dot_general x10, matrix products, dot(): lax.dot_general(u, v, (((cu,), (cv,)), ((), ())), preferred_element_type=...  11.9 us
    all_to_all x1, starting transfers between devices, shards(): term = lax.all_to_all(term, 'grid', 0, 0, tiled=True)  11.7 us
    all_to_all x1, waiting for transfers between devices, shards(): term = lax.all_to_all(term, 'grid', 0, 0, tiled=True)  8.81 us
    all_to_all x1, blocking collectives, shards(): w = lax.all_to_all(w, 'tile', 0, 0, tiled=True)  8.52 us
  transfers between devices with their start and end apart: 15, of which 10 were waited for; matrix products, arithmetic and copies ran while one was open for 11% of the time, Pallas kernels for 6%

profile of v5, /device:TPU:32, one launch (start us, length us, event | category | flops | bytes accessed | tf_op | source)
XLA Modules:
  0.0 185.1 jit_solution(13151956041685430601)
XLA Ops:
  6.5 0.9 fusion.11
  7.6 0.9 broadcast_multiply_fusion
  8.5 0.8 broadcast_in_dim.10
  9.4 4.5 %all-to-all-start = ((bf16[4,32,2048]{2,1,0:T(8,128)(2,1)}), bf16[4,32,2048]{2,1,0:T(8,128)(2,1)S(1)}, u32[]{:S(2)}, u32[]{:S(2)}) async-start(bf16[4,32,2048]{2,1,0:T(8,128)(2,1)} %broadcast_in_dim.10), calls=%async_computation | async-start | bytes 1048576 | tf_op jit(solution)/shard_map/all_to_all | solution.py:33
  13.8 0.8 reshape.112
  15.5 7.8 %all-to-all-done = bf16[4,32,2048]{2,1,0:T(8,128)(2,1)S(1)} async-done(((bf16[4,32,2048]{2,1,0:T(8,128)(2,1)}), bf16[4,32,2048]{2,1,0:T(8,128)(2,1)S(1)}, u32[]{:S(2)}, u32[]{:S(2)}) %all-to-all-start) | async-done | bytes 524320 | tf_op jit(solution)/shard_map/all_to_all | solution.py:33
  23.4 1.9 %collective-permute-start.1 = (bf16[4,32,2048]{2,1,0:T(8,128)(2,1)S(1)}, bf16[4,32,2048]{2,1,0:T(8,128)(2,1)}, u32[]{:S(2)}, u32[]{:S(2)}) collective-permute-start(bf16[4,32,2048]{2,1,0:T(8,128)(2,1)S(1)} %all-to-all-done), channel_id=1, source_target_pairs={{0,32},{8,40},{16,48},{24,56},{32,64},{40,72},{48,80},{56,88},{64,... | collective-permute-start | bytes 1572872 | tf_op jit(solution)/shard_map/ppermute | solution.py:18
  25.3 0.8 convolution_convert_fusion.7
  26.5 1.1 dynamic_update_slice.27
  27.9 7.9 %collective-permute-done.2 = bf16[4,32,2048]{2,1,0:T(8,128)(2,1)} collective-permute-done((bf16[4,32,2048]{2,1,0:T(8,128)(2,1)S(1)}, bf16[4,32,2048]{2,1,0:T(8,128)(2,1)}, u32[]{:S(2)}, u32[]{:S(2)}) %collective-permute-start.2) | collective-permute-done | bytes 524320 | tf_op jit(solution)/shard_map/ppermute | solution.py:18
  35.8 3.2 %collective-permute-start.4 = (bf16[4,32,2048]{2,1,0:T(8,128)(2,1)}, bf16[4,32,2048]{2,1,0:T(8,128)(2,1)S(1)}, u32[]{:S(2)}, u32[]{:S(2)}) collective-permute-start(bf16[4,32,2048]{2,1,0:T(8,128)(2,1)} %collective-permute-done.2), channel_id=1, source_target_pairs={{0,224},{8,232},{16,240},{24,248},{32,0},{40,8},{48,16},{56,24},{6... | collective-permute-start | bytes 1572872 | tf_op jit(solution)/shard_map/ppermute | solution.py:18
  39.0 1.9 %convolution_convert_fusion.5 = bf16[128,512]{1,0:T(8,128)(2,1)S(1)} fusion(bf16[128,2048]{1,0:T(8,128)(2,1)} %bitcast.7, bf16[512,2048]{1,0:T(8,128)(2,1)S(1)} %copy-done), kind=kOutput, calls=%fused_computation.7 | convolution fusion | flops 268500992 | bytes 2752512 | tf_op jit(solution)/shard_map/dot_general | solution.py:37
  41.0 1.9 %convolution_convert_fusion.6 = bf16[128,512]{1,0:T(8,128)(2,1)S(1)} fusion(bf16[128,2048]{1,0:T(8,128)(2,1)} %bitcast.5, bf16[512,2048]{1,0:T(8,128)(2,1)S(1)} %copy-done), kind=kOutput, calls=%fused_computation.8 | convolution fusion | flops 268500992 | bytes 2752512 | tf_op jit(solution)/shard_map/dot_general | solution.py:37
  43.5 0.7 constant_dynamic-update-slice_fusion.6
  44.2 3.9 %collective-permute-done.4 = bf16[4,32,2048]{2,1,0:T(8,128)(2,1)S(1)} collective-permute-done((bf16[4,32,2048]{2,1,0:T(8,128)(2,1)}, bf16[4,32,2048]{2,1,0:T(8,128)(2,1)S(1)}, u32[]{:S(2)}, u32[]{:S(2)}) %collective-permute-start.4) | collective-permute-done | bytes 524320 | tf_op jit(solution)/shard_map/ppermute | solution.py:18
  48.1 3.8 %collective-permute-start.6 = (bf16[4,32,2048]{2,1,0:T(8,128)(2,1)S(1)}, bf16[4,32,2048]{2,1,0:T(8,128)(2,1)S(1)}, u32[]{:S(2)}, u32[]{:S(2)}) collective-permute-start(bf16[4,32,2048]{2,1,0:T(8,128)(2,1)S(1)} %collective-permute-done.4), channel_id=1, source_target_pairs={{0,224},{8,232},{16,240},{24,248},{32,0},{40,8},{48,16},{56,24},{6... | collective-permute-start | bytes 1572872 | tf_op jit(solution)/shard_map/ppermute | solution.py:18
  51.9 0.8 convolution_convert_fusion.3
  52.7 1.5 collective-permute-done.3
  54.2 0.8 convolution_convert_fusion.4
  55.1 0.7 constant_dynamic-update-slice_fusion.5
  55.7 0.7 constant_dynamic-update-slice_fusion.4
  56.4 3.9 %collective-permute-done.6 = bf16[4,32,2048]{2,1,0:T(8,128)(2,1)S(1)} collective-permute-done((bf16[4,32,2048]{2,1,0:T(8,128)(2,1)S(1)}, bf16[4,32,2048]{2,1,0:T(8,128)(2,1)S(1)}, u32[]{:S(2)}, u32[]{:S(2)}) %collective-permute-start.6) | collective-permute-done | bytes 524320 | tf_op jit(solution)/shard_map/ppermute | solution.py:18
  60.3 3.6 %collective-permute-start.8 = (bf16[2,32,2048]{2,1,0:T(8,128)(2,1)S(1)}, bf16[2,32,2048]{2,1,0:T(8,128)(2,1)S(1)}, u32[]{:S(2)}, u32[]{:S(2)}) collective-permute-start(bf16[2,32,2048]{2,1,0:T(8,128)(2,1)S(1)} %slice.25), channel_id=1, source_target_pairs={{0,224},{8,232},{16,240},{24,248},{32,0},{40,8},{48,16},{56,24},{6... | collective-permute-start | bytes 786440 | tf_op jit(solution)/shard_map/ppermute | solution.py:18
  63.8 0.8 convolution_convert_fusion.1
  64.7 0.8 collective-permute-done.5
  65.5 0.8 convolution_convert_fusion.2
  66.4 0.7 constant_dynamic-update-slice_fusion.3
  67.1 0.7 constant_dynamic-update-slice_fusion.2
  67.8 0.8 convolution_convert_fusion.9
  68.6 5.1 %collective-permute-done.7 = bf16[2,32,2048]{2,1,0:T(8,128)(2,1)S(1)} collective-permute-done((bf16[2,32,2048]{2,1,0:T(8,128)(2,1)S(1)}, bf16[2,32,2048]{2,1,0:T(8,128)(2,1)S(1)}, u32[]{:S(2)}, u32[]{:S(2)}) %collective-permute-start.7) | collective-permute-done | bytes 262176 | tf_op jit(solution)/shard_map/ppermute | solution.py:18
  73.7 0.8 convolution_convert_fusion.10
  75.8 5.2 %all-to-all-start.1 = ((bf16[8,8,16,512]{3,2,1,0:T(8,128)(2,1)}), bf16[8,8,16,512]{3,2,1,0:T(8,128)(2,1)S(1)}, u32[]{:S(2)}, u32[]{:S(2)}) async-start(bf16[8,8,16,512]{3,2,1,0:T(8,128)(2,1)} %constant_dynamic-update-slice_fusion), calls=%async_computation.1 | async-start | bytes 2097152 | tf_op jit(solution)/shard_map/all_to_all | solution.py:139
  80.9 5.2 %collective-permute-start.9 = (bf16[128,512]{1,0:T(8,128)(2,1)S(1)}, bf16[128,512]{1,0:T(8,128)(2,1)}, u32[]{:S(2)}, u32[]{:S(2)}) collective-permute-start(bf16[128,512]{1,0:T(8,128)(2,1)S(1)} %reshape.133), channel_id=1, source_target_pairs={{0,0},{1,32},{2,64},{3,96},{4,128},{5,160},{6,192},{7,224},{8,8},{... | collective-permute-start | bytes 393224 | tf_op jit(solution)/shard_map/ppermute | solution.py:28
  86.2 12.8 %all-to-all-done.1.parts = bf16[8,8,16,512]{3,2,1,0:T(8,128)(2,1)S(1)} async-done(((bf16[8,8,16,512]{3,2,1,0:T(8,128)(2,1)}), bf16[8,8,16,512]{3,2,1,0:T(8,128)(2,1)S(1)}, u32[]{:S(2)}, u32[]{:S(2)}) %all-to-all-start.1) | async-done | bytes 1048608 | tf_op jit(solution)/shard_map/all_to_all | solution.py:139
  99.0 1.0 copy-done.1
  100.0 2.0 %shard_map.100 = bf16[8,16,512]{2,1,0:T(8,128)(2,1)} custom-call(s32[1]{0:T(128)} %bitcast.22.z, bf16[8,8,16,512]{3,2,1,0:T(8,128)(2,1)} %copy-done.1), custom_call_target="tpu_custom_call" | custom-call | flops 524288 | bytes 1048576 | tf_op jit(solution)/shard_map/pallas_call | solution.py:90
  102.0 1.6 reshape.135
  103.6 11.7 %all-to-all-start.2 = ((bf16[32,4,512]{2,1,0:T(4,128)(2,1)}), bf16[32,4,512]{2,1,0:T(4,128)(2,1)S(1)}, u32[]{:S(2)}, u32[]{:S(2)}) async-start(bf16[32,4,512]{2,1,0:T(4,128)(2,1)} %reshape.135), calls=%async_computation.2 | async-start | bytes 262144 | tf_op jit(solution)/shard_map/all_to_all | solution.py:143
  115.3 0.7 all-gather.2.cloned.1.call-update
  116.0 8.8 %all-to-all-done.2 = bf16[32,4,512]{2,1,0:T(4,128)(2,1)S(1)} async-done(((bf16[32,4,512]{2,1,0:T(4,128)(2,1)}), bf16[32,4,512]{2,1,0:T(4,128)(2,1)S(1)}, u32[]{:S(2)}, u32[]{:S(2)}) %all-to-all-start.2) | async-done | bytes 131104 | tf_op jit(solution)/shard_map/all_to_all | solution.py:143
  124.8 1.4 fusion
  126.3 0.7 copy.24
  127.0 3.4 %all-to-all-start.3 = ((bf16[8,4,4,512]{3,1,2,0:T(4,128)(2,1)}), bf16[8,4,4,512]{3,1,2,0:T(4,128)(2,1)S(1)}, u32[]{:S(2)}, u32[]{:S(2)}) async-start(bf16[8,4,4,512]{3,1,2,0:T(4,128)(2,1)} %copy.24), calls=%async_computation.3 | async-start | bytes 262144 | tf_op jit(solution)/shard_map/all_to_all | solution.py:149
  130.7 7.1 %all-to-all-done.3 = bf16[8,4,4,512]{3,1,2,0:T(4,128)(2,1)S(1)} async-done(((bf16[8,4,4,512]{3,1,2,0:T(4,128)(2,1)}), bf16[8,4,4,512]{3,1,2,0:T(4,128)(2,1)S(1)}, u32[]{:S(2)}, u32[]{:S(2)}) %all-to-all-start.3) | async-done | bytes 131104 | tf_op jit(solution)/shard_map/all_to_all | solution.py:149
  137.9 8.4 %shard_map.101 = bf16[8,32,256]{2,1,0:T(8,128)(2,1)S(1)} custom-call(s32[8,4]{1,0:T(8,128)S(1)} %convert_element_type.68.flags, bf16[32,2048]{1,0:T(8,128)(2,1)S(1)} %bitcast.70, bf16[2048,2048]{1,0:T(8,128)(2,1)} %lmo.1), custom_call_target="tpu_custom_call" | custom-call | flops 268435456 | bytes 8388608 | tf_op jit(solution)/shard_map/pallas_call | solution.py:64
  146.3 8.5 %all_to_all.30 = bf16[8,32,256]{2,1,0:T(8,128)(2,1)S(1)} all-to-all(bf16[8,32,256]{2,1,0:T(8,128)(2,1)S(1)} %shard_map.101), channel_id=1, replica_groups=mesh['grid'=32,'tile'=8] {'tile'}, dimensions={0} | all-to-all | bytes 262144 | tf_op jit(solution)/shard_map/all_to_all | solution.py:155
  154.9 21.0 %all_to_all.31 = bf16[32,32,256]{2,1,0:T(8,128)(2,1)S(1)} all-to-all(bf16[32,32,256]{2,1,0:T(8,128)(2,1)S(1)} %broadcast_in_dim.11), channel_id=1, replica_groups=mesh['grid'=32,'tile'=8] {'grid'}, dimensions={0} | all-to-all | bytes 1048576 | tf_op jit(solution)/shard_map/all_to_all | solution.py:33
  175.9 2.4 %convolution_convert_fusion = bf16[256,512]{1,0:T(8,128)(2,1)} fusion(bf16[1024,256]{1,0:T(8,128)(2,1)S(1)} %bitcast.75, bf16[1024,512]{1,0:T(8,128)(2,1)} %all-gather.2.cloned.1.call-done), kind=kOutput, calls=%fused_computation | convolution fusion | flops 268566528 | bytes 1835008 | tf_op jit(solution)/shard_map/dot_general | solution.py:37
  (51 shorter events, 4.3 us)
Async XLA Ops:
  6.5 18.8 %copy-start = (bf16[512,2048]{1,0:T(8,128)(2,1)S(1)}, bf16[512,2048]{1,0:T(8,128)(2,1)}, u32[]{:S(2)}) copy-start(bf16[512,2048]{1,0:T(8,128)(2,1)} %param.12) | copy-start | bytes 6291460
  6.5 8.8 %copy-start.3 = (f32[16384]{0:T(1024)S(1)}, f32[16384]{0:T(1024)}, u32[]{:S(2)}) copy-start(f32[16384]{0:T(1024)} %param.16) | copy-start | bytes 196612
  6.5 8.9 %copy-start.2 = (f32[3,16384]{1,0:T(4,128)S(1)}, f32[3,16384]{1,0:T(4,128)}, u32[]{:S(2)}) copy-start(f32[3,16384]{1,0:T(4,128)} %param.15) | copy-start | bytes 589828
  9.4 13.9 %all-to-all-start = ((bf16[4,32,2048]{2,1,0:T(8,128)(2,1)}), bf16[4,32,2048]{2,1,0:T(8,128)(2,1)S(1)}, u32[]{:S(2)}, u32[]{:S(2)}) async-start(bf16[4,32,2048]{2,1,0:T(8,128)(2,1)} %broadcast_in_dim.10), calls=%async_computation | async-start | bytes 1048576 | tf_op jit(solution)/shard_map/all_to_all | solution.py:33
  14.7 0.8 collective-permute-start
  23.3 12.5 %collective-permute-start.2 = (bf16[4,32,2048]{2,1,0:T(8,128)(2,1)S(1)}, bf16[4,32,2048]{2,1,0:T(8,128)(2,1)}, u32[]{:S(2)}, u32[]{:S(2)}) collective-permute-start(bf16[4,32,2048]{2,1,0:T(8,128)(2,1)S(1)} %all-to-all-done), channel_id=1, source_target_pairs={{0,224},{8,232},{16,240},{24,248},{32,0},{40,8},{48,16},{56,24},{6... | collective-permute-start | bytes 1572872 | tf_op jit(solution)/shard_map/ppermute | solution.py:18
  23.4 17.5 %collective-permute-start.1 = (bf16[4,32,2048]{2,1,0:T(8,128)(2,1)S(1)}, bf16[4,32,2048]{2,1,0:T(8,128)(2,1)}, u32[]{:S(2)}, u32[]{:S(2)}) collective-permute-start(bf16[4,32,2048]{2,1,0:T(8,128)(2,1)S(1)} %all-to-all-done), channel_id=1, source_target_pairs={{0,32},{8,40},{16,48},{24,56},{32,64},{40,72},{48,80},{56,88},{64,... | collective-permute-start | bytes 1572872 | tf_op jit(solution)/shard_map/ppermute | solution.py:18
  35.8 12.3 %collective-permute-start.4 = (bf16[4,32,2048]{2,1,0:T(8,128)(2,1)}, bf16[4,32,2048]{2,1,0:T(8,128)(2,1)S(1)}, u32[]{:S(2)}, u32[]{:S(2)}) collective-permute-start(bf16[4,32,2048]{2,1,0:T(8,128)(2,1)} %collective-permute-done.2), channel_id=1, source_target_pairs={{0,224},{8,232},{16,240},{24,248},{32,0},{40,8},{48,16},{56,24},{6... | collective-permute-start | bytes 1572872 | tf_op jit(solution)/shard_map/ppermute | solution.py:18
  40.9 13.3 %collective-permute-start.3 = (bf16[4,32,2048]{2,1,0:T(8,128)(2,1)}, bf16[4,32,2048]{2,1,0:T(8,128)(2,1)S(1)}, u32[]{:S(2)}, u32[]{:S(2)}) collective-permute-start(bf16[4,32,2048]{2,1,0:T(8,128)(2,1)} %collective-permute-done.1), channel_id=1, source_target_pairs={{0,32},{8,40},{16,48},{24,56},{32,64},{40,72},{48,80},{56,88},{64,... | collective-permute-start | bytes 1572872 | tf_op jit(solution)/shard_map/ppermute | solution.py:18
  48.1 12.2 %collective-permute-start.6 = (bf16[4,32,2048]{2,1,0:T(8,128)(2,1)S(1)}, bf16[4,32,2048]{2,1,0:T(8,128)(2,1)S(1)}, u32[]{:S(2)}, u32[]{:S(2)}) collective-permute-start(bf16[4,32,2048]{2,1,0:T(8,128)(2,1)S(1)} %collective-permute-done.4), channel_id=1, source_target_pairs={{0,224},{8,232},{16,240},{24,248},{32,0},{40,8},{48,16},{56,24},{6... | collective-permute-start | bytes 1572872 | tf_op jit(solution)/shard_map/ppermute | solution.py:18
  54.2 11.3 %collective-permute-start.5 = (bf16[4,32,2048]{2,1,0:T(8,128)(2,1)S(1)}, bf16[4,32,2048]{2,1,0:T(8,128)(2,1)S(1)}, u32[]{:S(2)}, u32[]{:S(2)}) collective-permute-start(bf16[4,32,2048]{2,1,0:T(8,128)(2,1)S(1)} %collective-permute-done.3), channel_id=1, source_target_pairs={{0,32},{8,40},{16,48},{24,56},{32,64},{40,72},{48,80},{56,88},{64,... | collective-permute-start | bytes 1572872 | tf_op jit(solution)/shard_map/ppermute | solution.py:18
  60.3 7.5 %collective-permute-start.8 = (bf16[2,32,2048]{2,1,0:T(8,128)(2,1)S(1)}, bf16[2,32,2048]{2,1,0:T(8,128)(2,1)S(1)}, u32[]{:S(2)}, u32[]{:S(2)}) collective-permute-start(bf16[2,32,2048]{2,1,0:T(8,128)(2,1)S(1)} %slice.25), channel_id=1, source_target_pairs={{0,224},{8,232},{16,240},{24,248},{32,0},{40,8},{48,16},{56,24},{6... | collective-permute-start | bytes 786440 | tf_op jit(solution)/shard_map/ppermute | solution.py:18
  66.4 7.4 %collective-permute-start.7 = (bf16[2,32,2048]{2,1,0:T(8,128)(2,1)S(1)}, bf16[2,32,2048]{2,1,0:T(8,128)(2,1)S(1)}, u32[]{:S(2)}, u32[]{:S(2)}) collective-permute-start(bf16[2,32,2048]{2,1,0:T(8,128)(2,1)S(1)} %slice.24), channel_id=1, source_target_pairs={{0,32},{8,40},{16,48},{24,56},{32,64},{40,72},{48,80},{56,88},{64,... | collective-permute-start | bytes 786440 | tf_op jit(solution)/shard_map/ppermute | solution.py:18
  74.5 50.3 %copy-start.4 = (s32[32,32]{1,0:T(8,128)S(1)}, s32[32,32]{1,0:T(8,128)}, u32[]{:S(2)}) copy-start(s32[32,32]{1,0:T(8,128)} %param.14) | copy-start | bytes 12292
  75.8 23.2 %all-to-all-start.1 = ((bf16[8,8,16,512]{3,2,1,0:T(8,128)(2,1)}), bf16[8,8,16,512]{3,2,1,0:T(8,128)(2,1)S(1)}, u32[]{:S(2)}, u32[]{:S(2)}) async-start(bf16[8,8,16,512]{3,2,1,0:T(8,128)(2,1)} %constant_dynamic-update-slice_fusion), calls=%async_computation.1 | async-start | bytes 2097152 | tf_op jit(solution)/shard_map/all_to_all | solution.py:139
  80.9 22.7 %collective-permute-start.9 = (bf16[128,512]{1,0:T(8,128)(2,1)S(1)}, bf16[128,512]{1,0:T(8,128)(2,1)}, u32[]{:S(2)}, u32[]{:S(2)}) collective-permute-start(bf16[128,512]{1,0:T(8,128)(2,1)S(1)} %reshape.133), channel_id=1, source_target_pairs={{0,0},{1,32},{2,64},{3,96},{4,128},{5,160},{6,192},{7,224},{8,8},{... | collective-permute-start | bytes 393224 | tf_op jit(solution)/shard_map/ppermute | solution.py:28
  99.0 1.0 copy-start.1
  102.0 28.4 %copy-start.5 = (s32[8,16]{1,0:T(8,128)S(1)}, s32[8,16]{1,0:T(8,128)}, u32[]{:S(2)}) copy-start(s32[8,16]{1,0:T(8,128)} %param.19) | copy-start | bytes 1540
  103.6 21.2 %all-to-all-start.2 = ((bf16[32,4,512]{2,1,0:T(4,128)(2,1)}), bf16[32,4,512]{2,1,0:T(4,128)(2,1)S(1)}, u32[]{:S(2)}, u32[]{:S(2)}) async-start(bf16[32,4,512]{2,1,0:T(4,128)(2,1)} %reshape.135), calls=%async_computation.2 | async-start | bytes 262144 | tf_op jit(solution)/shard_map/all_to_all | solution.py:143
  115.3 60.6 %all-gather.2.cloned.1.call-start = ((), (), s32[]{:S(2)}) async-start(), calls=%async_computation.6 | async-start | bytes 1179648 | tf_op jit(solution)/shard_map/all_gather | solution.py:142
  127.0 10.8 %all-to-all-start.3 = ((bf16[8,4,4,512]{3,1,2,0:T(4,128)(2,1)}), bf16[8,4,4,512]{3,1,2,0:T(4,128)(2,1)S(1)}, u32[]{:S(2)}, u32[]{:S(2)}) async-start(bf16[8,4,4,512]{3,1,2,0:T(4,128)(2,1)} %copy.24), calls=%async_computation.3 | async-start | bytes 262144 | tf_op jit(solution)/shard_map/all_to_all | solution.py:149
Sparse Core Ops, SparseCore 0:
  118.0 24.5 all-gather.1

commit v6 on v5

--- a/solution.py
+++ b/solution.py
@@ -37,65 +37,66 @@
     return lax.dot_general(u, v, (((cu,), (cv,)), ((), ())), preferred_element_type=f32)
 
 
-def region_kernel(flags, pot, lmo, out, acc):
+def region_kernel(pot, lmo, keep, out, acc):
     step = pl.program_id(0)
-    strips, _, width = acc.shape
+    strips, _, width = out.shape
 
     @pl.when(step == 0)
     def _():
         acc[...] = jnp.zeros_like(acc)
 
-    for strip in range(strips):
-
-        @pl.when(flags[strip, step * lmo.shape[0] // BLK] != 0)
-        def _():
-            part = lmo[:, strip * width : (strip + 1) * width]
-            acc[strip] += jnp.dot(pot[...], part, preferred_element_type=f32)
+    part = jnp.dot(pot[...], lmo[...], preferred_element_type=f32)
+    acc[...] += jnp.where(keep[0] != 0, part, 0.0)
 
     @pl.when(step == pl.num_programs(0) - 1)
     def _():
-        out[...] = acc[...].astype(out.dtype)
+        for strip in range(strips):
+            out[strip] = acc[:, strip * width : (strip + 1) * width].astype(out.dtype)
 
 
-def region_product(flags, pot, lmo, rows=256):
-    strips = flags.shape[0]
+def region_product(in_dom, pot, lmo, rows=256):
+    strips, blocks = in_dom.shape
     points, cols = pot.shape
-    width = lmo.shape[1] // strips
+    wide = lmo.shape[1]
+    keep = jnp.repeat(in_dom.T, wide // strips, axis=1).reshape(blocks, 1, wide)
     return pl.pallas_call(
         region_kernel,
         grid=(cols // rows,),
         in_specs=[
-            pl.BlockSpec(memory_space=pltpu.SMEM),
             pl.BlockSpec((points, rows), lambda i: (0, i)),
-            pl.BlockSpec((rows, lmo.shape[1]), lambda i: (i, 0)),
+            pl.BlockSpec((rows, wide), lambda i: (i, 0)),
+            pl.BlockSpec((1, 1, wide), lambda i: (i * rows // BLK, 0, 0)),
         ],
-        out_specs=pl.BlockSpec((strips, points, width), lambda i: (0, 0, 0)),
-        out_shape=jax.ShapeDtypeStruct((strips, points, width), bf16),
-        scratch_shapes=[pltpu.VMEM((strips, points, width), f32)],
+        out_specs=pl.BlockSpec((strips, points, wide // strips), lambda i: (0, 0, 0)),
+        out_shape=jax.ShapeDtypeStruct((strips, points, wide // strips), bf16),
+        scratch_shapes=[pltpu.VMEM((points, wide), f32)],
         compiler_params=pltpu.CompilerParams(vmem_limit_bytes=52 * 2**20),
         cost_estimate=pl.CostEstimate(
-            flops=2 * points * cols * lmo.shape[1], bytes_accessed=2 * lmo.size, transcendentals=0
+            flops=2 * points * cols * wide, bytes_accessed=2 * lmo.size, transcendentals=0
         ),
-    )(flags, pot, lmo)
+    )(pot, lmo, keep)
 
 
-def place_kernel(z, parts, out):
-    for m in range(NZ):
-        total = jnp.sum(parts[:, m].astype(f32), axis=0).astype(out.dtype)
-        out[pl.ds((z[0] + m) % NZ, 1)] = total[None]
+def place_kernel(z, early, late, out):
+    for m in range(-2, 6):
+        part = early[:, m + 2] if m < 3 else late[:, m - 3]
+        total = jnp.sum(part.astype(f32), axis=0)
+        first = (z[0] + m + NZ) % NZ * NY
+        for q in range(NY):
+            out[pl.ds(first + q, 1)] = total[q * QP : (q + 1) * QP].astype(out.dtype)[None]
 
 
-def sum_and_place(z, parts):
+def sum_and_place(z, early, late):
     whole = pl.BlockSpec(memory_space=pltpu.VMEM)
     return pl.pallas_call(
         place_kernel,
-        in_specs=[pl.BlockSpec(memory_space=pltpu.SMEM), whole],
+        in_specs=[pl.BlockSpec(memory_space=pltpu.SMEM), whole, whole],
         out_specs=whole,
-        out_shape=jax.ShapeDtypeStruct(parts.shape[1:], bf16),
+        out_shape=jax.ShapeDtypeStruct((NZ * NY, QP, BLK), bf16),
         cost_estimate=pl.CostEstimate(
-            flops=parts.size, bytes_accessed=2 * parts.size, transcendentals=0
+            flops=early.size, bytes_accessed=2 * early.size, transcendentals=0
         ),
-    )(z.reshape(1), parts)
+    )(z.reshape(1), early, late)
 
 
 def shards(pv, sig, density, core, smask, centers, widths, coords, lmo, dom):
@@ -119,25 +120,28 @@
 
     info = permute_all(info, lambda a, b, c: (a, c // 2, 2 * b + c % 2))[0]
     info, xy = tie((info, xy))
-    parts = product(jnp.zeros((NT, NZ, 16, BLK), bf16), xy, 0)
+    over_tile = lambda v: lax.all_to_all(v, "tile", 0, 0, tiled=True)
+    early = product(jnp.zeros((NT, 5, 16, BLK), bf16), xy, 2)
+    late = jnp.zeros((NT, 3, 16, BLK), bf16)
     up = down = xy
     for s in range(1, 4):
-        up, down = along_z(up, 1), along_z(down, -1)
-        parts = product(parts, up, NZ - s)
-        parts = product(parts, down, s)
+        up, down = tie((along_z(up, 1), along_z(down, -1)))
+        if s < 3:
+            early = product(product(early, up, 2 - s), down, 2 + s)
+        else:
+            late = product(product(late, up, 2), down, 0)
+    early = over_tile(early)
     up, down = along_z(up[: NY // 2], 1), along_z(down[NY // 2 :], -1)
-    parts = product(parts, up, 4)
-    parts = product(parts, down, 4, NT // 2)
+    late = product(product(late, up, 1), down, 1, NT // 2)
 
     named = info[:nblk]
     pts = lax.dynamic_slice_in_dim(info[nblk:].reshape(3, BP), 16 * (j % 2) + QP * y, QP, 1)
     off = centers.reshape(3, nblk, 1, BLK) - pts.reshape(3, 1, QP, 1)
     coef = 1.0 / jnp.sqrt(jnp.sum(off * off, axis=0) + widths.reshape(nblk, 1, BLK))
     coef = coef * named[:, None, None]
-    parts, coef, piece = tie((parts, coef, piece))
+    late, coef, piece = tie((late, coef, piece))
     piece = permute_all(piece, lambda a, b, c: (c, b, a))
-    parts = lax.all_to_all(parts, "tile", 0, 0, tiled=True)
-    term = sum_and_place(z, parts).reshape(NZ * NY, QP, BLK)
+    term = sum_and_place(z, early, over_tile(late))
     term, piece = tie((term, piece))
     x_col = lax.all_gather(piece, "tile", axis=0, tiled=True)
     term = lax.all_to_all(term, "grid", 0, 0, tiled=True)
@@ -154,6 +158,7 @@
     w = region_product(in_dom, pot, lmo)
     w = lax.all_to_all(w, "tile", 0, 0, tiled=True)
     w = jnp.sum(w.astype(f32), axis=0).astype(bf16)
+    w, x_col = tie((w, x_col))
     w_all = spread(w, "grid", NZ * NY).reshape(-1, 256)
     return dot(w_all, x_col, 0, 0).astype(bf16)
 

time: 186 us -> 182 us (0.978)
  waiting for transfers between devices: 60.3 us -> 50.3 us
  starting transfers between devices: 43.3 us -> 46.8 us
  matrix products: 13.3 us -> 16.4 us
    all_to_all x1 -> x2, waiting for transfers between devices: 12.8 us -> 4.66 us  [shards(): over_tile = lambda v: lax.all_to_all(v, 'tile', 0, 0, tiled=True)]
    all_to_all x1 -> x2, starting transfers between devices: 5.15 us -> 9.59 us  [shards(): over_tile = lambda v: lax.all_to_all(v, 'tile', 0, 0, tiled=True)]
    dot_general x10, matrix products: 11.9 us -> 15 us  [dot(): lax.dot_general(u, v, (((cu,), (cv,)), ((), ())), preferred_element_type=...]
    all_to_all x1, starting transfers between devices: 11.7 us -> 14.2 us  [shards(): term = lax.all_to_all(term, 'grid', 0, 0, tiled=True)]
    ppermute x8, starting transfers between devices: 12.8 us -> 10.2 us  [along_z(): return lax.ppermute(x, 'grid', pairs)]
  transfers between devices with their start and end apart: 15 -> 16, of which waited for: 10 -> 11; matrix products, arithmetic and copies ran while one was open for 11% -> 14% of each run, Pallas kernels for 6% -> 5%
where the time goes in v6:
time: 182 us; the launch traced here: 181 us
  waiting for transfers between devices  50.3 us (28%)
  starting transfers between devices  46.8 us (26%)
  blocking collectives  29.7 us (16%)
  matrix products  16.4 us (9%)
  between operations  13.8 us (8%)
  local copies, waits for them, and re-layouts  11.8 us (6%)
  Pallas kernels  8.67 us (5%)
  other arithmetic  3.45 us (2%)
    ppermute x8, waiting for transfers between devices, along_z(): return lax.ppermute(x, 'grid', pairs)  23.2 us
    all_to_all x1, blocking collectives, spread(): lax.all_to_all(copies, axis, 0, 0, tiled=True, axis_index_groups=groups)  21.2 us
    dot_general x10, matrix products, dot(): lax.dot_general(u, v, (((cu,), (cv,)), ((), ())), preferred_element_type=...  15 us
    all_to_all x1, starting transfers between devices, shards(): term = lax.all_to_all(term, 'grid', 0, 0, tiled=True)  14.2 us
    ppermute x8, starting transfers between devices, along_z(): return lax.ppermute(x, 'grid', pairs)  10.2 us
    all_to_all x2, starting transfers between devices, shards(): over_tile = lambda v: lax.all_to_all(v, 'tile', 0, 0, tiled=True)  9.59 us
    all_to_all x1, waiting for transfers between devices, shards(): term = lax.all_to_all(term, 'grid', 0, 0, tiled=True)  8.64 us
    all_to_all x1, blocking collectives, shards(): w = lax.all_to_all(w, 'tile', 0, 0, tiled=True)  8.52 us
  transfers between devices with their start and end apart: 16, of which 11 were waited for; matrix products, arithmetic and copies ran while one was open for 14% of the time, Pallas kernels for 5%

profile of v6, /device:TPU:32, one launch (start us, length us, event | category | flops | bytes accessed | tf_op | source)
XLA Modules:
  0.0 180.9 jit_solution(17719184777726731048)
XLA Ops:
  6.5 0.9 fusion.12
  7.6 0.9 broadcast_multiply_fusion
  8.5 0.9 broadcast_in_dim.12
  9.4 4.5 %all-to-all-start = ((bf16[4,32,2048]{2,1,0:T(8,128)(2,1)}), bf16[4,32,2048]{2,1,0:T(8,128)(2,1)S(1)}, u32[]{:S(2)}, u32[]{:S(2)}) async-start(bf16[4,32,2048]{2,1,0:T(8,128)(2,1)} %broadcast_in_dim.12), calls=%async_computation | async-start | bytes 1048576 | tf_op jit(solution)/shard_map/all_to_all | solution.py:33
  13.8 0.8 reshape.109
  15.5 7.8 %all-to-all-done = bf16[4,32,2048]{2,1,0:T(8,128)(2,1)S(1)} async-done(((bf16[4,32,2048]{2,1,0:T(8,128)(2,1)}), bf16[4,32,2048]{2,1,0:T(8,128)(2,1)S(1)}, u32[]{:S(2)}, u32[]{:S(2)}) %all-to-all-start) | async-done | bytes 524320 | tf_op jit(solution)/shard_map/all_to_all | solution.py:33
  23.4 1.9 %collective-permute-start.1 = (bf16[4,32,2048]{2,1,0:T(8,128)(2,1)S(1)}, bf16[4,32,2048]{2,1,0:T(8,128)(2,1)}, u32[]{:S(2)}, u32[]{:S(2)}) collective-permute-start(bf16[4,32,2048]{2,1,0:T(8,128)(2,1)S(1)} %all-to-all-done), channel_id=1, source_target_pairs={{0,32},{8,40},{16,48},{24,56},{32,64},{40,72},{48,80},{56,88},{64,... | collective-permute-start | bytes 1572872 | tf_op jit(solution)/shard_map/ppermute | solution.py:18
  25.4 0.8 convolution_convert_fusion.5
  26.5 0.7 reshape.120
  27.2 0.9 dynamic_update_slice.31
  28.5 7.3 %collective-permute-done.2 = bf16[4,32,2048]{2,1,0:T(8,128)(2,1)} collective-permute-done((bf16[4,32,2048]{2,1,0:T(8,128)(2,1)S(1)}, bf16[4,32,2048]{2,1,0:T(8,128)(2,1)}, u32[]{:S(2)}, u32[]{:S(2)}) %collective-permute-start.2) | collective-permute-done | bytes 524320 | tf_op jit(solution)/shard_map/ppermute | solution.py:18
  35.8 3.8 %collective-permute-done.1 = bf16[4,32,2048]{2,1,0:T(8,128)(2,1)} collective-permute-done((bf16[4,32,2048]{2,1,0:T(8,128)(2,1)S(1)}, bf16[4,32,2048]{2,1,0:T(8,128)(2,1)}, u32[]{:S(2)}, u32[]{:S(2)}) %collective-permute-start.1) | collective-permute-done | bytes 524320 | tf_op jit(solution)/shard_map/ppermute | solution.py:18
  39.6 1.9 %convolution_convert_fusion.4 = bf16[128,512]{1,0:T(8,128)(2,1)S(1)} fusion(bf16[128,2048]{1,0:T(8,128)(2,1)} %bitcast.15, bf16[512,2048]{1,0:T(8,128)(2,1)S(1)} %copy-done), kind=kOutput, calls=%fused_computation.4 | convolution fusion | flops 268500992 | bytes 2752512 | tf_op jit(solution)/shard_map/dot_general | solution.py:37
  41.5 3.0 %collective-permute-start.4 = (bf16[4,32,2048]{2,1,0:T(8,128)(2,1)}, bf16[4,32,2048]{2,1,0:T(8,128)(2,1)}, u32[]{:S(2)}, u32[]{:S(2)}) collective-permute-start(bf16[4,32,2048]{2,1,0:T(8,128)(2,1)} %collective-permute-done.2), channel_id=1, source_target_pairs={{0,224},{8,232},{16,240},{24,248},{32,0},{40,8},{48,16},{56,24},{6... | collective-permute-start | bytes 1572872 | tf_op jit(solution)/shard_map/ppermute | solution.py:18
  45.2 1.9 %convolution_convert_fusion.3 = bf16[128,512]{1,0:T(8,128)(2,1)S(1)} fusion(bf16[128,2048]{1,0:T(8,128)(2,1)} %bitcast.17, bf16[512,2048]{1,0:T(8,128)(2,1)S(1)} %copy-done), kind=kOutput, calls=%fused_computation.3 | convolution fusion | flops 268500992 | bytes 2752512 | tf_op jit(solution)/shard_map/dot_general | solution.py:37
  47.7 4.3 %collective-permute-done.3 = bf16[4,32,2048]{2,1,0:T(8,128)(2,1)} collective-permute-done((bf16[4,32,2048]{2,1,0:T(8,128)(2,1)}, bf16[4,32,2048]{2,1,0:T(8,128)(2,1)}, u32[]{:S(2)}, u32[]{:S(2)}) %collective-permute-start.3) | collective-permute-done | bytes 524320 | tf_op jit(solution)/shard_map/ppermute | solution.py:18
  52.1 1.3 collective-permute-done.4
  53.3 1.9 %collective-permute-start.5 = (bf16[4,32,2048]{2,1,0:T(8,128)(2,1)}, bf16[4,32,2048]{2,1,0:T(8,128)(2,1)S(1)}, u32[]{:S(2)}, u32[]{:S(2)}) collective-permute-start(bf16[4,32,2048]{2,1,0:T(8,128)(2,1)} %collective-permute-done.3), channel_id=1, source_target_pairs={{0,32},{8,40},{16,48},{24,56},{32,64},{40,72},{48,80},{56,88},{64,... | collective-permute-start | bytes 1572872 | tf_op jit(solution)/shard_map/ppermute | solution.py:18
  55.2 1.9 %convolution_convert_fusion.2 = bf16[128,512]{1,0:T(8,128)(2,1)S(1)} fusion(bf16[128,2048]{1,0:T(8,128)(2,1)} %bitcast.19, bf16[512,2048]{1,0:T(8,128)(2,1)S(1)} %copy-done), kind=kOutput, calls=%fused_computation.2 | convolution fusion | flops 268500992 | bytes 2752512 | tf_op jit(solution)/shard_map/dot_general | solution.py:37
  57.1 1.1 collective-permute-start.6
  58.9 1.9 %convolution_convert_fusion.1 = bf16[128,512]{1,0:T(8,128)(2,1)S(1)} fusion(bf16[128,2048]{1,0:T(8,128)(2,1)} %bitcast.21, bf16[512,2048]{1,0:T(8,128)(2,1)S(1)} %copy-done), kind=kOutput, calls=%fused_computation.1 | convolution fusion | flops 268500992 | bytes 2752512 | tf_op jit(solution)/shard_map/dot_general | solution.py:37
  61.5 5.1 %all-to-all-start.1 = ((bf16[8,5,16,512]{3,2,1,0:T(8,128)(2,1)}), bf16[8,5,16,512]{3,2,1,0:T(8,128)(2,1)S(1)}, u32[]{:S(2)}, u32[]{:S(2)}) async-start(bf16[8,5,16,512]{3,2,1,0:T(8,128)(2,1)} %constant_dynamic-update-slice_fusion), calls=%async_computation.1 | async-start | bytes 1310720 | tf_op jit(solution)/shard_map/all_to_all | solution.py:123
  66.6 1.8 %collective-permute-done.6 = bf16[4,32,2048]{2,1,0:T(8,128)(2,1)} collective-permute-done((bf16[4,32,2048]{2,1,0:T(8,128)(2,1)}, bf16[4,32,2048]{2,1,0:T(8,128)(2,1)}, u32[]{:S(2)}, u32[]{:S(2)}) %collective-permute-start.6) | collective-permute-done | bytes 524320 | tf_op jit(solution)/shard_map/ppermute | solution.py:18
  68.4 1.9 %convolution_convert_fusion.6 = bf16[128,512]{1,0:T(8,128)(2,1)S(1)} fusion(bf16[128,2048]{1,0:T(8,128)(2,1)} %bitcast.5, bf16[512,2048]{1,0:T(8,128)(2,1)S(1)} %copy-done), kind=kOutput, calls=%fused_computation.6 | convolution fusion | flops 268500992 | bytes 2752512 | tf_op jit(solution)/shard_map/dot_general | solution.py:37
  70.3 1.8 %collective-permute-start.7 = (bf16[2,32,2048]{2,1,0:T(8,128)(2,1)S(1)}, bf16[2,32,2048]{2,1,0:T(8,128)(2,1)S(1)}, u32[]{:S(2)}, u32[]{:S(2)}) collective-permute-start(bf16[2,32,2048]{2,1,0:T(8,128)(2,1)S(1)} %slice.20), channel_id=1, source_target_pairs={{0,32},{8,40},{16,48},{24,56},{32,64},{40,72},{48,80},{56,88},{64,... | collective-permute-start | bytes 786440 | tf_op jit(solution)/shard_map/ppermute | solution.py:18
  72.1 0.8 convolution_convert_fusion.7
  73.0 1.0 slice.21
  73.9 0.8 dynamic_update_slice.27
  75.7 3.5 %collective-permute-done.7 = bf16[2,32,2048]{2,1,0:T(8,128)(2,1)S(1)} collective-permute-done((bf16[2,32,2048]{2,1,0:T(8,128)(2,1)S(1)}, bf16[2,32,2048]{2,1,0:T(8,128)(2,1)S(1)}, u32[]{:S(2)}, u32[]{:S(2)}) %collective-permute-start.7) | collective-permute-done | bytes 262176 | tf_op jit(solution)/shard_map/ppermute | solution.py:18
  79.2 0.8 convolution_convert_fusion.10
  80.6 1.2 collective-permute-done.8
  81.8 0.8 convolution_convert_fusion.9
  83.2 4.5 %all-to-all-start.2 = ((bf16[8,3,16,512]{3,2,1,0:T(8,128)(2,1)}), bf16[8,3,16,512]{3,2,1,0:T(8,128)(2,1)S(1)}, u32[]{:S(2)}, u32[]{:S(2)}) async-start(bf16[8,3,16,512]{3,2,1,0:T(8,128)(2,1)} %constant_dynamic-update-slice_fusion.4), calls=%async_computation.2 | async-start | bytes 786432 | tf_op jit(solution)/shard_map/all_to_all | solution.py:123
  87.8 4.2 %collective-permute-start.9 = (bf16[128,512]{1,0:T(8,128)(2,1)S(1)}, bf16[128,512]{1,0:T(8,128)(2,1)}, u32[]{:S(2)}, u32[]{:S(2)}) collective-permute-start(bf16[128,512]{1,0:T(8,128)(2,1)S(1)} %copy-done.4), channel_id=1, source_target_pairs={{0,0},{1,32},{2,64},{3,96},{4,128},{5,160},{6,192},{7,224},{8,8},{... | collective-permute-start | bytes 393224 | tf_op jit(solution)/shard_map/ppermute | solution.py:28
  92.0 4.7 %all-to-all-done.2.late = bf16[8,3,16,512]{3,2,1,0:T(8,128)(2,1)S(1)} async-done(((bf16[8,3,16,512]{3,2,1,0:T(8,128)(2,1)}), bf16[8,3,16,512]{3,2,1,0:T(8,128)(2,1)S(1)}, u32[]{:S(2)}, u32[]{:S(2)}) %all-to-all-start.2) | async-done | bytes 393248 | tf_op jit(solution)/shard_map/all_to_all | solution.py:123
  96.7 0.8 copy-done.2
  97.4 2.0 %shard_map.100 = bf16[32,4,512]{2,1,0:T(4,128)(2,1)} custom-call(s32[1]{0:T(128)} %bitcast.12.z, bf16[8,5,16,512]{3,2,1,0:T(8,128)(2,1)} %copy-done.1, bf16[8,3,16,512]{3,2,1,0:T(8,128)(2,1)} %copy-done.2), custom_call_target="tpu_custom_call" | custom-call | flops 327680 | bytes 655360 | tf_op jit(solution)/shard_map/pallas_call | solution.py:91
  99.4 14.2 %all-to-all-start.3 = ((bf16[32,4,512]{2,1,0:T(4,128)(2,1)}), bf16[32,4,512]{2,1,0:T(4,128)(2,1)S(1)}, u32[]{:S(2)}, u32[]{:S(2)}) async-start(bf16[32,4,512]{2,1,0:T(4,128)(2,1)} %shard_map.100), calls=%async_computation.3 | async-start | bytes 262144 | tf_op jit(solution)/shard_map/all_to_all | solution.py:147
  113.7 0.9 compare_reduce_fusion
  114.6 8.6 %all-to-all-done.3 = bf16[32,4,512]{2,1,0:T(4,128)(2,1)S(1)} async-done(((bf16[32,4,512]{2,1,0:T(4,128)(2,1)}), bf16[32,4,512]{2,1,0:T(4,128)(2,1)S(1)}, u32[]{:S(2)}, u32[]{:S(2)}) %all-to-all-start.3) | async-done | bytes 131104 | tf_op jit(solution)/shard_map/all_to_all | solution.py:147
  123.3 1.4 fusion.1
  124.9 0.7 copy.23
  125.6 3.4 %all-to-all-start.4 = ((bf16[8,4,4,512]{3,1,2,0:T(4,128)(2,1)}), bf16[8,4,4,512]{3,1,2,0:T(4,128)(2,1)S(1)}, u32[]{:S(2)}, u32[]{:S(2)}) async-start(bf16[8,4,4,512]{3,1,2,0:T(4,128)(2,1)} %copy.23), calls=%async_computation.4 | async-start | bytes 262144 | tf_op jit(solution)/shard_map/all_to_all | solution.py:153
  129.2 5.9 %all-to-all-done.4 = bf16[8,4,4,512]{3,1,2,0:T(4,128)(2,1)S(1)} async-done(((bf16[8,4,4,512]{3,1,2,0:T(4,128)(2,1)}), bf16[8,4,4,512]{3,1,2,0:T(4,128)(2,1)S(1)}, u32[]{:S(2)}, u32[]{:S(2)}) %all-to-all-start.4) | async-done | bytes 131104 | tf_op jit(solution)/shard_map/all_to_all | solution.py:153
  135.1 6.7 %shard_map.101 = bf16[8,32,256]{2,1,0:T(8,128)(2,1)S(1)} custom-call(bf16[32,2048]{1,0:T(8,128)(2,1)S(1)} %bitcast.71, bf16[2048,2048]{1,0:T(8,128)(2,1)} %lmo.1, s32[4,1,2048]{2,1,0:T(1,128)S(1)} %reshape_reshape.3.keep), custom_call_target="tpu_custom_call" | custom-call | flops 268435456 | bytes 8388608 | tf_op jit(solution)/shard_map/pallas_call | solution.py:62
  141.8 8.5 %all_to_all.35 = bf16[8,32,256]{2,1,0:T(8,128)(2,1)S(1)} all-to-all(bf16[8,32,256]{2,1,0:T(8,128)(2,1)S(1)} %shard_map.101), channel_id=1, replica_groups=mesh['grid'=32,'tile'=8] {'tile'}, dimensions={0} | all-to-all | bytes 262144 | tf_op jit(solution)/shard_map/all_to_all | solution.py:159
  150.4 21.2 %all_to_all.36 = bf16[32,32,256]{2,1,0:T(8,128)(2,1)S(1)} all-to-all(bf16[32,32,256]{2,1,0:T(8,128)(2,1)S(1)} %broadcast_in_dim.14), channel_id=1, replica_groups=mesh['grid'=32,'tile'=8] {'grid'}, dimensions={0} | all-to-all | bytes 1048576 | tf_op jit(solution)/shard_map/all_to_all | solution.py:33
  171.7 2.4 %convolution_convert_fusion = bf16[256,512]{1,0:T(8,128)(2,1)} fusion(bf16[1024,256]{1,0:T(8,128)(2,1)S(1)} %bitcast.76, bf16[1024,512]{1,0:T(8,128)(2,1)} %all-gather.2.cloned.1.call-done), kind=kOutput, calls=%fused_computation | convolution fusion | flops 268566528 | bytes 1835008 | tf_op jit(solution)/shard_map/dot_general | solution.py:37
  (56 shorter events, 7.3 us)
Async XLA Ops:
  6.5 18.8 %copy-start = (bf16[512,2048]{1,0:T(8,128)(2,1)S(1)}, bf16[512,2048]{1,0:T(8,128)(2,1)}, u32[]{:S(2)}) copy-start(bf16[512,2048]{1,0:T(8,128)(2,1)} %param.12) | copy-start | bytes 6291460
  6.5 8.8 %copy-start.5 = (f32[16384]{0:T(1024)S(1)}, f32[16384]{0:T(1024)}, u32[]{:S(2)}) copy-start(f32[16384]{0:T(1024)} %param.16) | copy-start | bytes 196612
  6.5 8.9 %copy-start.3 = (f32[3,16384]{1,0:T(4,128)S(1)}, f32[3,16384]{1,0:T(4,128)}, u32[]{:S(2)}) copy-start(f32[3,16384]{1,0:T(4,128)} %param.15) | copy-start | bytes 589828
  9.4 13.9 %all-to-all-start = ((bf16[4,32,2048]{2,1,0:T(8,128)(2,1)}), bf16[4,32,2048]{2,1,0:T(8,128)(2,1)S(1)}, u32[]{:S(2)}, u32[]{:S(2)}) async-start(bf16[4,32,2048]{2,1,0:T(8,128)(2,1)} %broadcast_in_dim.12), calls=%async_computation | async-start | bytes 1048576 | tf_op jit(solution)/shard_map/all_to_all | solution.py:33
  14.7 0.8 collective-permute-start
  23.3 12.5 %collective-permute-start.2 = (bf16[4,32,2048]{2,1,0:T(8,128)(2,1)S(1)}, bf16[4,32,2048]{2,1,0:T(8,128)(2,1)}, u32[]{:S(2)}, u32[]{:S(2)}) collective-permute-start(bf16[4,32,2048]{2,1,0:T(8,128)(2,1)S(1)} %all-to-all-done), channel_id=1, source_target_pairs={{0,224},{8,232},{16,240},{24,248},{32,0},{40,8},{48,16},{56,24},{6... | collective-permute-start | bytes 1572872 | tf_op jit(solution)/shard_map/ppermute | solution.py:18
  23.4 16.1 %collective-permute-start.1 = (bf16[4,32,2048]{2,1,0:T(8,128)(2,1)S(1)}, bf16[4,32,2048]{2,1,0:T(8,128)(2,1)}, u32[]{:S(2)}, u32[]{:S(2)}) collective-permute-start(bf16[4,32,2048]{2,1,0:T(8,128)(2,1)S(1)} %all-to-all-done), channel_id=1, source_target_pairs={{0,32},{8,40},{16,48},{24,56},{32,64},{40,72},{48,80},{56,88},{64,... | collective-permute-start | bytes 1572872 | tf_op jit(solution)/shard_map/ppermute | solution.py:18
  39.6 12.5 %collective-permute-start.3 = (bf16[4,32,2048]{2,1,0:T(8,128)(2,1)}, bf16[4,32,2048]{2,1,0:T(8,128)(2,1)}, u32[]{:S(2)}, u32[]{:S(2)}) collective-permute-start(bf16[4,32,2048]{2,1,0:T(8,128)(2,1)} %collective-permute-done.1), channel_id=1, source_target_pairs={{0,32},{8,40},{16,48},{24,56},{32,64},{40,72},{48,80},{56,88},{64,... | collective-permute-start | bytes 1572872 | tf_op jit(solution)/shard_map/ppermute | solution.py:18
  41.5 11.8 %collective-permute-start.4 = (bf16[4,32,2048]{2,1,0:T(8,128)(2,1)}, bf16[4,32,2048]{2,1,0:T(8,128)(2,1)}, u32[]{:S(2)}, u32[]{:S(2)}) collective-permute-start(bf16[4,32,2048]{2,1,0:T(8,128)(2,1)} %collective-permute-done.2), channel_id=1, source_target_pairs={{0,224},{8,232},{16,240},{24,248},{32,0},{40,8},{48,16},{56,24},{6... | collective-permute-start | bytes 1572872 | tf_op jit(solution)/shard_map/ppermute | solution.py:18
  53.3 13.3 %collective-permute-start.5 = (bf16[4,32,2048]{2,1,0:T(8,128)(2,1)}, bf16[4,32,2048]{2,1,0:T(8,128)(2,1)S(1)}, u32[]{:S(2)}, u32[]{:S(2)}) collective-permute-start(bf16[4,32,2048]{2,1,0:T(8,128)(2,1)} %collective-permute-done.3), channel_id=1, source_target_pairs={{0,32},{8,40},{16,48},{24,56},{32,64},{40,72},{48,80},{56,88},{64,... | collective-permute-start | bytes 1572872 | tf_op jit(solution)/shard_map/ppermute | solution.py:18
  57.1 11.3 %collective-permute-start.6 = (bf16[4,32,2048]{2,1,0:T(8,128)(2,1)}, bf16[4,32,2048]{2,1,0:T(8,128)(2,1)}, u32[]{:S(2)}, u32[]{:S(2)}) collective-permute-start(bf16[4,32,2048]{2,1,0:T(8,128)(2,1)} %collective-permute-done.4), channel_id=1, source_target_pairs={{0,224},{8,232},{16,240},{24,248},{32,0},{40,8},{48,16},{56,24},{6... | collective-permute-start | bytes 1572872 | tf_op jit(solution)/shard_map/ppermute | solution.py:18
  61.5 21.8 %all-to-all-start.1 = ((bf16[8,5,16,512]{3,2,1,0:T(8,128)(2,1)}), bf16[8,5,16,512]{3,2,1,0:T(8,128)(2,1)S(1)}, u32[]{:S(2)}, u32[]{:S(2)}) async-start(bf16[8,5,16,512]{3,2,1,0:T(8,128)(2,1)} %constant_dynamic-update-slice_fusion), calls=%async_computation.1 | async-start | bytes 1310720 | tf_op jit(solution)/shard_map/all_to_all | solution.py:123
  70.3 8.9 %collective-permute-start.7 = (bf16[2,32,2048]{2,1,0:T(8,128)(2,1)S(1)}, bf16[2,32,2048]{2,1,0:T(8,128)(2,1)S(1)}, u32[]{:S(2)}, u32[]{:S(2)}) collective-permute-start(bf16[2,32,2048]{2,1,0:T(8,128)(2,1)S(1)} %slice.20), channel_id=1, source_target_pairs={{0,32},{8,40},{16,48},{24,56},{32,64},{40,72},{48,80},{56,88},{64,... | collective-permute-start | bytes 786440 | tf_op jit(solution)/shard_map/ppermute | solution.py:18
  74.7 7.1 %collective-permute-start.8 = (bf16[2,32,2048]{2,1,0:T(8,128)(2,1)S(1)}, bf16[2,32,2048]{2,1,0:T(8,128)(2,1)S(1)}, u32[]{:S(2)}, u32[]{:S(2)}) collective-permute-start(bf16[2,32,2048]{2,1,0:T(8,128)(2,1)S(1)} %slice.21), channel_id=1, source_target_pairs={{0,224},{8,232},{16,240},{24,248},{32,0},{40,8},{48,16},{56,24},{6... | collective-permute-start | bytes 786440 | tf_op jit(solution)/shard_map/ppermute | solution.py:18
  80.0 7.8 %copy-start.4 = (bf16[128,512]{1,0:T(8,128)(2,1)S(1)}, bf16[128,512]{1,0:T(8,128)(2,1)}, u32[]{:S(2)}) copy-start(bf16[128,512]{1,0:T(8,128)(2,1)} %reshape.120) | copy-start | bytes 393220
  82.6 40.7 %copy-start.6 = (s32[32,32]{1,0:T(8,128)S(1)}, s32[32,32]{1,0:T(8,128)}, u32[]{:S(2)}) copy-start(s32[32,32]{1,0:T(8,128)} %param.14) | copy-start | bytes 12292
  83.2 13.4 %copy-start.1 = (bf16[8,5,16,512]{3,2,1,0:T(8,128)(2,1)}, bf16[8,5,16,512]{3,2,1,0:T(8,128)(2,1)S(1)}, u32[]{:S(2)}) copy-start(bf16[8,5,16,512]{3,2,1,0:T(8,128)(2,1)S(1)} %all-to-all-done.1.early) | copy-start | bytes 1966084
  83.2 13.4 %all-to-all-start.2 = ((bf16[8,3,16,512]{3,2,1,0:T(8,128)(2,1)}), bf16[8,3,16,512]{3,2,1,0:T(8,128)(2,1)S(1)}, u32[]{:S(2)}, u32[]{:S(2)}) async-start(bf16[8,3,16,512]{3,2,1,0:T(8,128)(2,1)} %constant_dynamic-update-slice_fusion.4), calls=%async_computation.2 | async-start | bytes 786432 | tf_op jit(solution)/shard_map/all_to_all | solution.py:123
  87.7 62.7 %all-gather.2.cloned.1.call-start = ((), (), s32[]{:S(2)}) async-start(), calls=%async_computation.7 | async-start | bytes 1179648 | tf_op jit(solution)/shard_map/all_gather | solution.py:146
  87.8 11.6 %collective-permute-start.9 = (bf16[128,512]{1,0:T(8,128)(2,1)S(1)}, bf16[128,512]{1,0:T(8,128)(2,1)}, u32[]{:S(2)}, u32[]{:S(2)}) collective-permute-start(bf16[128,512]{1,0:T(8,128)(2,1)S(1)} %copy-done.4), channel_id=1, source_target_pairs={{0,0},{1,32},{2,64},{3,96},{4,128},{5,160},{6,192},{7,224},{8,8},{... | collective-permute-start | bytes 393224 | tf_op jit(solution)/shard_map/ppermute | solution.py:28
  96.6 0.8 copy-start.2
  99.4 23.8 %all-to-all-start.3 = ((bf16[32,4,512]{2,1,0:T(4,128)(2,1)}), bf16[32,4,512]{2,1,0:T(4,128)(2,1)S(1)}, u32[]{:S(2)}, u32[]{:S(2)}) async-start(bf16[32,4,512]{2,1,0:T(4,128)(2,1)} %shard_map.100), calls=%async_computation.3 | async-start | bytes 262144 | tf_op jit(solution)/shard_map/all_to_all | solution.py:147
  125.6 9.4 %all-to-all-start.4 = ((bf16[8,4,4,512]{3,1,2,0:T(4,128)(2,1)}), bf16[8,4,4,512]{3,1,2,0:T(4,128)(2,1)S(1)}, u32[]{:S(2)}, u32[]{:S(2)}) async-start(bf16[8,4,4,512]{3,1,2,0:T(4,128)(2,1)} %copy.23), calls=%async_computation.4 | async-start | bytes 262144 | tf_op jit(solution)/shard_map/all_to_all | solution.py:153
Sparse Core Ops, SparseCore 0:
  99.5 29.1 all-gather.1

commit v7 on v5

--- a/solution.py
+++ b/solution.py
@@ -8,6 +8,7 @@
 NZ, NY, NT = 8, 4, 8
 BP, BLK = 32, 512
 QP = 4
+LEAD = 1
 bf16, f32 = jnp.bfloat16, jnp.float32
 Y_GROUPS = [[z * NY + y for y in range(NY)] for z in range(NZ)]
 tie = lax.optimization_barrier
@@ -28,61 +29,65 @@
     return lax.ppermute(x, ("grid", "tile"), pairs)
 
 
-def spread(x, axis, n, groups=None):
+def spread(x, axis, n):
     copies = jnp.broadcast_to(x[None], (n,) + x.shape)
-    return lax.all_to_all(copies, axis, 0, 0, tiled=True, axis_index_groups=groups)
+    return lax.all_to_all(copies, axis, 0, 0, tiled=True)
 
 
 def dot(u, v, cu, cv):
     return lax.dot_general(u, v, (((cu,), (cv,)), ((), ())), preferred_element_type=f32)
 
 
-def region_kernel(flags, pot, lmo, out, acc):
+def region_kernel(*refs):
+    pots, lmos, keep, out, acc = refs[:4], refs[4:8], refs[8], refs[9], refs[10]
     step = pl.program_id(0)
-    strips, _, width = acc.shape
+    strips, _, width = out.shape
 
     @pl.when(step == 0)
     def _():
         acc[...] = jnp.zeros_like(acc)
 
-    for strip in range(strips):
-
-        @pl.when(flags[strip, step * lmo.shape[0] // BLK] != 0)
-        def _():
-            part = lmo[:, strip * width : (strip + 1) * width]
-            acc[strip] += jnp.dot(pot[...], part, preferred_element_type=f32)
+    total = acc[...]
+    for k in range(4):
+        part = jnp.dot(pots[k][...], lmos[k][...], preferred_element_type=f32)
+        total = total + jnp.where(keep[k] != 0, part, 0.0)
+    acc[...] = total
 
     @pl.when(step == pl.num_programs(0) - 1)
     def _():
-        out[...] = acc[...].astype(out.dtype)
-
-
-def region_product(flags, pot, lmo, rows=256):
-    strips = flags.shape[0]
+        for strip in range(strips):
+            out[strip] = acc[:, strip * width : (strip + 1) * width].astype(out.dtype)
+
+
+def region_product(in_dom, pot, lmo, rows=128):
+    strips, blocks = in_dom.shape
     points, cols = pot.shape
-    width = lmo.shape[1] // strips
+    wide = lmo.shape[1]
+    keep = jnp.repeat(in_dom.T, wide // strips, axis=1).reshape(blocks, 1, wide)
+    steps = BLK // rows
+    starts = [k * steps for k in range(blocks)]
     return pl.pallas_call(
         region_kernel,
-        grid=(cols // rows,),
-        in_specs=[
-            pl.BlockSpec(memory_space=pltpu.SMEM),
-            pl.BlockSpec((points, rows), lambda i: (0, i)),
-            pl.BlockSpec((rows, lmo.shape[1]), lambda i: (i, 0)),
-        ],
-        out_specs=pl.BlockSpec((strips, points, width), lambda i: (0, 0, 0)),
-        out_shape=jax.ShapeDtypeStruct((strips, points, width), bf16),
-        scratch_shapes=[pltpu.VMEM((strips, points, width), f32)],
+        grid=(steps,),
+        in_specs=[pl.BlockSpec((points, rows), lambda i, s=s: (0, s + i)) for s in starts]
+        + [pl.BlockSpec((rows, wide), lambda i, s=s: (s + i, 0)) for s in starts]
+        + [pl.BlockSpec((blocks, 1, wide), lambda i: (0, 0, 0))],
+        out_specs=pl.BlockSpec((strips, points, wide // strips), lambda i: (0, 0, 0)),
+        out_shape=jax.ShapeDtypeStruct((strips, points, wide // strips), bf16),
+        scratch_shapes=[pltpu.VMEM((points, wide), f32)],
         compiler_params=pltpu.CompilerParams(vmem_limit_bytes=52 * 2**20),
         cost_estimate=pl.CostEstimate(
-            flops=2 * points * cols * lmo.shape[1], bytes_accessed=2 * lmo.size, transcendentals=0
+            flops=2 * points * cols * wide, bytes_accessed=2 * lmo.size, transcendentals=0
         ),
-    )(flags, pot, lmo)
+    )(*[pot] * blocks, *[lmo] * blocks, keep)
 
 
 def place_kernel(z, parts, out):
     for m in range(NZ):
-        total = jnp.sum(parts[:, m].astype(f32), axis=0).astype(out.dtype)
-        out[pl.ds((z[0] + m) % NZ, 1)] = total[None]
+        total = jnp.sum(parts[:, m].astype(f32), axis=0)
+        first = (z[0] + m) % NZ * NY
+        for q in range(NY):
+            out[pl.ds(first + q, 1)] = total[q * QP : (q + 1) * QP].astype(out.dtype)[None]
 
 
 def sum_and_place(z, parts):
@@ -91,11 +96,36 @@
         place_kernel,
         in_specs=[pl.BlockSpec(memory_space=pltpu.SMEM), whole],
         out_specs=whole,
-        out_shape=jax.ShapeDtypeStruct(parts.shape[1:], bf16),
+        out_shape=jax.ShapeDtypeStruct((NZ * NY, QP, BLK), bf16),
         cost_estimate=pl.CostEstimate(
             flops=parts.size, bytes_accessed=2 * parts.size, transcendentals=0
         ),
     )(z.reshape(1), parts)
+
+
+def mask_kernel(sig, pv, out):
+    cols = lax.broadcasted_iota(jnp.int32, (1, pv.shape[1]), 1)
+    first = lax.axis_index("tile") * (pv.shape[1] // BLK)
+    ids = first + lax.shift_right_logical(cols, BLK.bit_length() - 1)
+    hit = ids == sig[:, 0:1]
+    for i in range(1, sig.shape[1]):
+        hit = hit | (ids == sig[:, i : i + 1])
+    kept = jnp.where(hit, pv[...].astype(f32), 0.0).astype(out.dtype)
+    for copy in range(out.shape[0]):
+        out[copy] = kept
+
+
+def masked_copies(sig, pv, n):
+    whole = pl.BlockSpec(memory_space=pltpu.VMEM)
+    return pl.pallas_call(
+        mask_kernel,
+        in_specs=[whole, whole],
+        out_specs=whole,
+        out_shape=jax.ShapeDtypeStruct((n,) + pv.shape, pv.dtype),
+        cost_estimate=pl.CostEstimate(
+            flops=pv.size, bytes_accessed=2 * (n + 1) * pv.size, transcendentals=0
+        ),
+    )(sig, pv)
 
 
 def shards(pv, sig, density, core, smask, centers, widths, coords, lmo, dom):
@@ -105,10 +135,9 @@
     cols = pv.shape[1]
     ids = jnp.arange(nblk, dtype=jnp.int32)
     named = jnp.any(sig[0][:, None] == ids[None, :], axis=0).astype(f32)
-    own = lax.dynamic_slice_in_dim(named, 4 * j, 4, 0)
-    masked = pv * jnp.repeat(own, BLK)[None, :].astype(bf16)
-
-    xy = spread(masked, "grid", NY, Y_GROUPS)
+
+    xy = masked_copies(sig, pv, NY)
+    xy = lax.all_to_all(xy, "grid", 0, 0, tiled=True, axis_index_groups=Y_GROUPS)
     info = jnp.concatenate([named, coords.reshape(-1)])[None]
     piece = lax.dynamic_slice_in_dim(xy, y * BLK, BLK, 2)
     piece = piece.reshape(NT, NY, QP, BLK).transpose(1, 0, 2, 3).reshape(NY * BP, BLK)
@@ -125,9 +154,9 @@
         up, down = along_z(up, 1), along_z(down, -1)
         parts = product(parts, up, NZ - s)
         parts = product(parts, down, s)
-    up, down = along_z(up[: NY // 2], 1), along_z(down[NY // 2 :], -1)
+    up, down = along_z(up[:LEAD], 1), along_z(down[LEAD:], -1)
     parts = product(parts, up, 4)
-    parts = product(parts, down, 4, NT // 2)
+    parts = product(parts, down, 4, 2 * LEAD)
 
     named = info[:nblk]
     pts = lax.dynamic_slice_in_dim(info[nblk:].reshape(3, BP), 16 * (j % 2) + QP * y, QP, 1)
@@ -137,7 +166,7 @@
     parts, coef, piece = tie((parts, coef, piece))
     piece = permute_all(piece, lambda a, b, c: (c, b, a))
     parts = lax.all_to_all(parts, "tile", 0, 0, tiled=True)
-    term = sum_and_place(z, parts).reshape(NZ * NY, QP, BLK)
+    term = sum_and_place(z, parts)
     term, piece = tie((term, piece))
     x_col = lax.all_gather(piece, "tile", axis=0, tiled=True)
     term = lax.all_to_all(term, "grid", 0, 0, tiled=True)
@@ -154,6 +183,7 @@
     w = region_product(in_dom, pot, lmo)
     w = lax.all_to_all(w, "tile", 0, 0, tiled=True)
     w = jnp.sum(w.astype(f32), axis=0).astype(bf16)
+    w, x_col = tie((w, x_col))
     w_all = spread(w, "grid", NZ * NY).reshape(-1, 256)
     return dot(w_all, x_col, 0, 0).astype(bf16)
 

time: 186 us -> 180 us (0.968)
  waiting for transfers between devices: 60.3 us -> 55.9 us
    pallas_call x1 -> x2, Pallas kernels: 8.42 us -> 6.94 us  [the longest x1 4.82 us: region_product(): pl.pallas_call(region_kernel, grid=(steps,), in_specs=[pl.BlockSpec((poin...]
  transfers between devices with their start and end apart: 15 -> 15, of which waited for: 10 -> 10; matrix products, arithmetic and copies ran while one was open for 11% -> 12% of each run, Pallas kernels for 6% -> 4%
where the time goes in v7:
time: 180 us; the launch traced here: 179 us
  waiting for transfers between devices  55.9 us (31%)
  starting transfers between devices  44.2 us (25%)
  blocking collectives  29.8 us (17%)
  between operations  13.7 us (8%)
  matrix products  13.3 us (7%)
  local copies, waits for them, and re-layouts  10.4 us (6%)
  Pallas kernels  8.97 us (5%)
  other arithmetic  2.39 us (1%)
    ppermute x8, waiting for transfers between devices, along_z(): return lax.ppermute(x, 'grid', pairs)  22.2 us
    all_to_all x1, blocking collectives, spread(): return lax.all_to_all(copies, axis, 0, 0, tiled=True)  21.3 us
    ppermute x8, starting transfers between devices, along_z(): return lax.ppermute(x, 'grid', pairs)  12.9 us
    all_to_all x1, waiting for transfers between devices, shards(): parts = lax.all_to_all(parts, 'tile', 0, 0, tiled=True)  12.8 us
    dot_general x10, matrix products, dot(): lax.dot_general(u, v, (((cu,), (cv,)), ((), ())), preferred_element_type=...  11.8 us
    all_to_all x1, starting transfers between devices, shards(): term = lax.all_to_all(term, 'grid', 0, 0, tiled=True)  11.5 us
    all_to_all x1, waiting for transfers between devices, shards(): term = lax.all_to_all(term, 'grid', 0, 0, tiled=True)  8.63 us
    all_to_all x1, blocking collectives, shards(): w = lax.all_to_all(w, 'tile', 0, 0, tiled=True)  8.52 us
  transfers between devices with their start and end apart: 15, of which 10 were waited for; matrix products, arithmetic and copies ran while one was open for 12% of the time, Pallas kernels for 4%

profile of v7, /device:TPU:32, one launch (start us, length us, event | category | flops | bytes accessed | tf_op | source)
XLA Modules:
  0.0 178.6 jit_solution(11816266303393140196)
XLA Ops:
  6.5 2.1 %shard_map.100 = bf16[4,32,2048]{2,1,0:T(8,128)(2,1)} custom-call(s32[1,16]{1,0:T(1,128)} %sig.1, bf16[32,2048]{1,0:T(8,128)(2,1)} %pv.1), custom_call_target="tpu_custom_call" | custom-call | flops 65536 | bytes 655360 | tf_op jit(solution)/shard_map/pallas_call | solution.py:120
  8.7 4.5 %all-to-all-start = ((bf16[4,32,2048]{2,1,0:T(8,128)(2,1)}), bf16[4,32,2048]{2,1,0:T(8,128)(2,1)S(1)}, u32[]{:S(2)}, u32[]{:S(2)}) async-start(bf16[4,32,2048]{2,1,0:T(8,128)(2,1)} %shard_map.100), calls=%async_computation | async-start | bytes 1048576 | tf_op jit(solution)/shard_map/all_to_all | solution.py:140
  13.1 0.8 reshape.100
  13.9 0.7 fusion.13
  15.4 0.9 add.43
  16.4 6.2 %all-to-all-done = bf16[4,32,2048]{2,1,0:T(8,128)(2,1)S(1)} async-done(((bf16[4,32,2048]{2,1,0:T(8,128)(2,1)}), bf16[4,32,2048]{2,1,0:T(8,128)(2,1)S(1)}, u32[]{:S(2)}, u32[]{:S(2)}) %all-to-all-start) | async-done | bytes 524320 | tf_op jit(solution)/shard_map/all_to_all | solution.py:140
  22.7 1.9 %collective-permute-start.1 = (bf16[4,32,2048]{2,1,0:T(8,128)(2,1)S(1)}, bf16[4,32,2048]{2,1,0:T(8,128)(2,1)}, u32[]{:S(2)}, u32[]{:S(2)}) collective-permute-start(bf16[4,32,2048]{2,1,0:T(8,128)(2,1)S(1)} %all-to-all-done), channel_id=1, source_target_pairs={{0,32},{8,40},{16,48},{24,56},{32,64},{40,72},{48,80},{56,88},{64,... | collective-permute-start | bytes 1572872 | tf_op jit(solution)/shard_map/ppermute | solution.py:19
  24.6 0.8 convolution_convert_fusion.7
  25.8 1.1 dynamic_update_slice.27
  27.3 7.7 %collective-permute-done.2 = bf16[4,32,2048]{2,1,0:T(8,128)(2,1)} collective-permute-done((bf16[4,32,2048]{2,1,0:T(8,128)(2,1)S(1)}, bf16[4,32,2048]{2,1,0:T(8,128)(2,1)}, u32[]{:S(2)}, u32[]{:S(2)}) %collective-permute-start.2) | collective-permute-done | bytes 524320 | tf_op jit(solution)/shard_map/ppermute | solution.py:19
  35.1 3.2 %collective-permute-start.4 = (bf16[4,32,2048]{2,1,0:T(8,128)(2,1)}, bf16[4,32,2048]{2,1,0:T(8,128)(2,1)S(1)}, u32[]{:S(2)}, u32[]{:S(2)}) collective-permute-start(bf16[4,32,2048]{2,1,0:T(8,128)(2,1)} %collective-permute-done.2), channel_id=1, source_target_pairs={{0,224},{8,232},{16,240},{24,248},{32,0},{40,8},{48,16},{56,24},{6... | collective-permute-start | bytes 1572872 | tf_op jit(solution)/shard_map/ppermute | solution.py:19
  38.3 1.9 %convolution_convert_fusion.5 = bf16[128,512]{1,0:T(8,128)(2,1)S(1)} fusion(bf16[128,2048]{1,0:T(8,128)(2,1)} %bitcast.7, bf16[512,2048]{1,0:T(8,128)(2,1)S(1)} %copy-done), kind=kOutput, calls=%fused_computation.5 | convolution fusion | flops 268500992 | bytes 2752512 | tf_op jit(solution)/shard_map/dot_general | solution.py:38
  40.3 1.9 %convolution_convert_fusion.6 = bf16[128,512]{1,0:T(8,128)(2,1)S(1)} fusion(bf16[128,2048]{1,0:T(8,128)(2,1)} %bitcast.5, bf16[512,2048]{1,0:T(8,128)(2,1)S(1)} %copy-done), kind=kOutput, calls=%fused_computation.6 | convolution fusion | flops 268500992 | bytes 2752512 | tf_op jit(solution)/shard_map/dot_general | solution.py:38
  42.2 0.7 constant_dynamic-update-slice_fusion.7
  42.9 0.7 constant_dynamic-update-slice_fusion.6
  43.5 3.8 %collective-permute-done.4 = bf16[4,32,2048]{2,1,0:T(8,128)(2,1)S(1)} collective-permute-done((bf16[4,32,2048]{2,1,0:T(8,128)(2,1)}, bf16[4,32,2048]{2,1,0:T(8,128)(2,1)S(1)}, u32[]{:S(2)}, u32[]{:S(2)}) %collective-permute-start.4) | collective-permute-done | bytes 524320 | tf_op jit(solution)/shard_map/ppermute | solution.py:19
  47.4 3.8 %collective-permute-start.6 = (bf16[4,32,2048]{2,1,0:T(8,128)(2,1)S(1)}, bf16[4,32,2048]{2,1,0:T(8,128)(2,1)S(1)}, u32[]{:S(2)}, u32[]{:S(2)}) collective-permute-start(bf16[4,32,2048]{2,1,0:T(8,128)(2,1)S(1)} %collective-permute-done.4), channel_id=1, source_target_pairs={{0,224},{8,232},{16,240},{24,248},{32,0},{40,8},{48,16},{56,24},{6... | collective-permute-start | bytes 1572872 | tf_op jit(solution)/shard_map/ppermute | solution.py:19
  51.2 0.8 convolution_convert_fusion.3
  52.0 1.5 collective-permute-done.3
  53.5 0.8 convolution_convert_fusion.4
  54.3 0.7 constant_dynamic-update-slice_fusion.5
  55.0 0.7 constant_dynamic-update-slice_fusion.4
  55.7 3.8 %collective-permute-done.6 = bf16[4,32,2048]{2,1,0:T(8,128)(2,1)S(1)} collective-permute-done((bf16[4,32,2048]{2,1,0:T(8,128)(2,1)S(1)}, bf16[4,32,2048]{2,1,0:T(8,128)(2,1)S(1)}, u32[]{:S(2)}, u32[]{:S(2)}) %collective-permute-start.6) | collective-permute-done | bytes 524320 | tf_op jit(solution)/shard_map/ppermute | solution.py:19
  59.6 3.6 %collective-permute-start.8 = (bf16[3,32,2048]{2,1,0:T(8,128)(2,1)S(1)}, bf16[3,32,2048]{2,1,0:T(8,128)(2,1)S(1)}, u32[]{:S(2)}, u32[]{:S(2)}) collective-permute-start(bf16[3,32,2048]{2,1,0:T(8,128)(2,1)S(1)} %slice.25), channel_id=1, source_target_pairs={{0,224},{8,232},{16,240},{24,248},{32,0},{40,8},{48,16},{56,24},{6... | collective-permute-start | bytes 1179656 | tf_op jit(solution)/shard_map/ppermute | solution.py:19
  63.1 0.8 convolution_convert_fusion.1
  64.0 0.8 collective-permute-done.5
  64.8 0.8 convolution_convert_fusion.2
  65.9 0.7 constant_dynamic-update-slice_fusion.3
  66.6 0.7 constant_dynamic-update-slice_fusion.2
  67.2 4.5 %collective-permute-done.7 = bf16[1,32,2048]{2,1,0:T(8,128)(2,1)S(1)} collective-permute-done((bf16[1,32,2048]{2,1,0:T(8,128)(2,1)S(1)}, bf16[1,32,2048]{2,1,0:T(8,128)(2,1)S(1)}, u32[]{:S(2)}, u32[]{:S(2)}) %collective-permute-start.7) | collective-permute-done | bytes 131104 | tf_op jit(solution)/shard_map/ppermute | solution.py:19
  71.8 0.7 convolution_convert_fusion.10
  73.1 0.8 convolution_convert_fusion.9
  74.6 6.1 %all-to-all-start.1 = ((bf16[8,8,16,512]{3,2,1,0:T(8,128)(2,1)}), bf16[8,8,16,512]{3,2,1,0:T(8,128)(2,1)S(1)}, u32[]{:S(2)}, u32[]{:S(2)}) async-start(bf16[8,8,16,512]{3,2,1,0:T(8,128)(2,1)} %constant_dynamic-update-slice_fusion), calls=%async_computation.1 | async-start | bytes 2097152 | tf_op jit(solution)/shard_map/all_to_all | solution.py:168
  80.7 5.2 %collective-permute-start.9 = (bf16[128,512]{1,0:T(8,128)(2,1)S(1)}, bf16[128,512]{1,0:T(8,128)(2,1)}, u32[]{:S(2)}, u32[]{:S(2)}) collective-permute-start(bf16[128,512]{1,0:T(8,128)(2,1)S(1)} %reshape.121), channel_id=1, source_target_pairs={{0,0},{1,32},{2,64},{3,96},{4,128},{5,160},{6,192},{7,224},{8,8},{... | collective-permute-start | bytes 393224 | tf_op jit(solution)/shard_map/ppermute | solution.py:29
  85.9 12.8 %all-to-all-done.1.parts = bf16[8,8,16,512]{3,2,1,0:T(8,128)(2,1)S(1)} async-done(((bf16[8,8,16,512]{3,2,1,0:T(8,128)(2,1)}), bf16[8,8,16,512]{3,2,1,0:T(8,128)(2,1)S(1)}, u32[]{:S(2)}, u32[]{:S(2)}) %all-to-all-start.1) | async-done | bytes 1048608 | tf_op jit(solution)/shard_map/all_to_all | solution.py:168
  98.7 1.0 copy-done.1
  99.7 2.0 %shard_map.101 = bf16[32,4,512]{2,1,0:T(4,128)(2,1)} custom-call(s32[1]{0:T(128)} %bitcast.22.z, bf16[8,8,16,512]{3,2,1,0:T(8,128)(2,1)} %copy-done.1), custom_call_target="tpu_custom_call" | custom-call | flops 524288 | bytes 1048576 | tf_op jit(solution)/shard_map/pallas_call | solution.py:95
  101.7 11.5 %all-to-all-start.2 = ((bf16[32,4,512]{2,1,0:T(4,128)(2,1)}), bf16[32,4,512]{2,1,0:T(4,128)(2,1)S(1)}, u32[]{:S(2)}, u32[]{:S(2)}) async-start(bf16[32,4,512]{2,1,0:T(4,128)(2,1)} %shard_map.101), calls=%async_computation.2 | async-start | bytes 262144 | tf_op jit(solution)/shard_map/all_to_all | solution.py:172
  113.2 0.9 compare_reduce_fusion
  114.1 8.6 %all-to-all-done.2 = bf16[32,4,512]{2,1,0:T(4,128)(2,1)S(1)} async-done(((bf16[32,4,512]{2,1,0:T(4,128)(2,1)}), bf16[32,4,512]{2,1,0:T(4,128)(2,1)S(1)}, u32[]{:S(2)}, u32[]{:S(2)}) %all-to-all-start.2) | async-done | bytes 131104 | tf_op jit(solution)/shard_map/all_to_all | solution.py:172
  122.9 1.4 fusion.1
  124.5 0.7 copy.23
  125.2 3.4 %all-to-all-start.3 = ((bf16[8,4,4,512]{3,1,2,0:T(4,128)(2,1)}), bf16[8,4,4,512]{3,1,2,0:T(4,128)(2,1)S(1)}, u32[]{:S(2)}, u32[]{:S(2)}) async-start(bf16[8,4,4,512]{3,1,2,0:T(4,128)(2,1)} %copy.23), calls=%async_computation.3 | async-start | bytes 262144 | tf_op jit(solution)/shard_map/all_to_all | solution.py:178
  128.7 5.9 %all-to-all-done.3 = bf16[8,4,4,512]{3,1,2,0:T(4,128)(2,1)S(1)} async-done(((bf16[8,4,4,512]{3,1,2,0:T(4,128)(2,1)}), bf16[8,4,4,512]{3,1,2,0:T(4,128)(2,1)S(1)}, u32[]{:S(2)}, u32[]{:S(2)}) %all-to-all-start.3) | async-done | bytes 131104 | tf_op jit(solution)/shard_map/all_to_all | solution.py:178
  134.7 4.8 %shard_map.102 = bf16[8,32,256]{2,1,0:T(8,128)(2,1)S(1)} custom-call(bf16[32,2048]{1,0:T(8,128)(2,1)S(1)} %bitcast.69, bf16[32,2048]{1,0:T(8,128)(2,1)S(1)} %bitcast.70, bf16[32,2048]{1,0:T(8,128)(2,1)S(1)} %bitcast.71, bf16[32,2048]{1,0:T(8,128)(2,1)S(1)} %bitcast.72, bf16[2048,2048]{1,0:T(8,128)(2,1)} %refs_7_.1, bf16[2048,2048]{1,0:T(8,128)(2,1)} %refs_7_.1, ...), custom_call_target="tpu_custom_call" | custom-call | flops 268435456 | bytes 8388608 | tf_op jit(solution)/shard_map/pallas_call | solution.py:69
  139.5 8.5 %all_to_all.30 = bf16[8,32,256]{2,1,0:T(8,128)(2,1)S(1)} all-to-all(bf16[8,32,256]{2,1,0:T(8,128)(2,1)S(1)} %shard_map.102), channel_id=1, replica_groups=mesh['grid'=32,'tile'=8] {'tile'}, dimensions={0} | all-to-all | bytes 262144 | tf_op jit(solution)/shard_map/all_to_all | solution.py:184
  148.1 21.3 %all_to_all.31 = bf16[32,32,256]{2,1,0:T(8,128)(2,1)S(1)} all-to-all(bf16[32,32,256]{2,1,0:T(8,128)(2,1)S(1)} %broadcast_in_dim.8), channel_id=1, replica_groups=mesh['grid'=32,'tile'=8] {'grid'}, dimensions={0} | all-to-all | bytes 1048576 | tf_op jit(solution)/shard_map/all_to_all | solution.py:34
  169.4 2.4 %convolution_convert_fusion = bf16[256,512]{1,0:T(8,128)(2,1)} fusion(bf16[1024,256]{1,0:T(8,128)(2,1)S(1)} %bitcast.78, bf16[1024,512]{1,0:T(8,128)(2,1)} %all-gather.2.cloned.1.call-done), kind=kOutput, calls=%fused_computation | convolution fusion | flops 268566528 | bytes 1835008 | tf_op jit(solution)/shard_map/dot_general | solution.py:38
  (44 shorter events, 3.9 us)
Async XLA Ops:
  6.5 18.1 %copy-start = (bf16[512,2048]{1,0:T(8,128)(2,1)S(1)}, bf16[512,2048]{1,0:T(8,128)(2,1)}, u32[]{:S(2)}) copy-start(bf16[512,2048]{1,0:T(8,128)(2,1)} %param.12) | copy-start | bytes 6291460
  6.5 9.7 %copy-start.2 = (f32[3,16384]{1,0:T(4,128)S(1)}, f32[3,16384]{1,0:T(4,128)}, u32[]{:S(2)}) copy-start(f32[3,16384]{1,0:T(4,128)} %param.15) | copy-start | bytes 589828
  8.7 13.9 %all-to-all-start = ((bf16[4,32,2048]{2,1,0:T(8,128)(2,1)}), bf16[4,32,2048]{2,1,0:T(8,128)(2,1)S(1)}, u32[]{:S(2)}, u32[]{:S(2)}) async-start(bf16[4,32,2048]{2,1,0:T(8,128)(2,1)} %shard_map.100), calls=%async_computation | async-start | bytes 1048576 | tf_op jit(solution)/shard_map/all_to_all | solution.py:140
  14.7 1.6 collective-permute-start
  22.6 12.5 %collective-permute-start.2 = (bf16[4,32,2048]{2,1,0:T(8,128)(2,1)S(1)}, bf16[4,32,2048]{2,1,0:T(8,128)(2,1)}, u32[]{:S(2)}, u32[]{:S(2)}) collective-permute-start(bf16[4,32,2048]{2,1,0:T(8,128)(2,1)S(1)} %all-to-all-done), channel_id=1, source_target_pairs={{0,224},{8,232},{16,240},{24,248},{32,0},{40,8},{48,16},{56,24},{6... | collective-permute-start | bytes 1572872 | tf_op jit(solution)/shard_map/ppermute | solution.py:19
  22.7 17.5 %collective-permute-start.1 = (bf16[4,32,2048]{2,1,0:T(8,128)(2,1)S(1)}, bf16[4,32,2048]{2,1,0:T(8,128)(2,1)}, u32[]{:S(2)}, u32[]{:S(2)}) collective-permute-start(bf16[4,32,2048]{2,1,0:T(8,128)(2,1)S(1)} %all-to-all-done), channel_id=1, source_target_pairs={{0,32},{8,40},{16,48},{24,56},{32,64},{40,72},{48,80},{56,88},{64,... | collective-permute-start | bytes 1572872 | tf_op jit(solution)/shard_map/ppermute | solution.py:19
  35.1 12.3 %collective-permute-start.4 = (bf16[4,32,2048]{2,1,0:T(8,128)(2,1)}, bf16[4,32,2048]{2,1,0:T(8,128)(2,1)S(1)}, u32[]{:S(2)}, u32[]{:S(2)}) collective-permute-start(bf16[4,32,2048]{2,1,0:T(8,128)(2,1)} %collective-permute-done.2), channel_id=1, source_target_pairs={{0,224},{8,232},{16,240},{24,248},{32,0},{40,8},{48,16},{56,24},{6... | collective-permute-start | bytes 1572872 | tf_op jit(solution)/shard_map/ppermute | solution.py:19
  40.2 13.3 %collective-permute-start.3 = (bf16[4,32,2048]{2,1,0:T(8,128)(2,1)}, bf16[4,32,2048]{2,1,0:T(8,128)(2,1)S(1)}, u32[]{:S(2)}, u32[]{:S(2)}) collective-permute-start(bf16[4,32,2048]{2,1,0:T(8,128)(2,1)} %collective-permute-done.1), channel_id=1, source_target_pairs={{0,32},{8,40},{16,48},{24,56},{32,64},{40,72},{48,80},{56,88},{64,... | collective-permute-start | bytes 1572872 | tf_op jit(solution)/shard_map/ppermute | solution.py:19
  47.4 12.2 %collective-permute-start.6 = (bf16[4,32,2048]{2,1,0:T(8,128)(2,1)S(1)}, bf16[4,32,2048]{2,1,0:T(8,128)(2,1)S(1)}, u32[]{:S(2)}, u32[]{:S(2)}) collective-permute-start(bf16[4,32,2048]{2,1,0:T(8,128)(2,1)S(1)} %collective-permute-done.4), channel_id=1, source_target_pairs={{0,224},{8,232},{16,240},{24,248},{32,0},{40,8},{48,16},{56,24},{6... | collective-permute-start | bytes 1572872 | tf_op jit(solution)/shard_map/ppermute | solution.py:19
  53.5 11.3 %collective-permute-start.5 = (bf16[4,32,2048]{2,1,0:T(8,128)(2,1)S(1)}, bf16[4,32,2048]{2,1,0:T(8,128)(2,1)S(1)}, u32[]{:S(2)}, u32[]{:S(2)}) collective-permute-start(bf16[4,32,2048]{2,1,0:T(8,128)(2,1)S(1)} %collective-permute-done.3), channel_id=1, source_target_pairs={{0,32},{8,40},{16,48},{24,56},{32,64},{40,72},{48,80},{56,88},{64,... | collective-permute-start | bytes 1572872 | tf_op jit(solution)/shard_map/ppermute | solution.py:19
  59.6 13.6 %collective-permute-start.8 = (bf16[3,32,2048]{2,1,0:T(8,128)(2,1)S(1)}, bf16[3,32,2048]{2,1,0:T(8,128)(2,1)S(1)}, u32[]{:S(2)}, u32[]{:S(2)}) collective-permute-start(bf16[3,32,2048]{2,1,0:T(8,128)(2,1)S(1)} %slice.25), channel_id=1, source_target_pairs={{0,224},{8,232},{16,240},{24,248},{32,0},{40,8},{48,16},{56,24},{6... | collective-permute-start | bytes 1179656 | tf_op jit(solution)/shard_map/ppermute | solution.py:19
  65.6 6.2 %collective-permute-start.7 = (bf16[1,32,2048]{2,1,0:T(8,128)(2,1)S(1)}, bf16[1,32,2048]{2,1,0:T(8,128)(2,1)S(1)}, u32[]{:S(2)}, u32[]{:S(2)}) collective-permute-start(bf16[1,32,2048]{2,1,0:T(8,128)(2,1)S(1)} %slice.24), channel_id=1, source_target_pairs={{0,32},{8,40},{16,48},{24,56},{32,64},{40,72},{48,80},{56,88},{64,... | collective-permute-start | bytes 393224 | tf_op jit(solution)/shard_map/ppermute | solution.py:19
  74.6 48.3 %copy-start.3 = (s32[32,32]{1,0:T(8,128)S(1)}, s32[32,32]{1,0:T(8,128)}, u32[]{:S(2)}) copy-start(s32[32,32]{1,0:T(8,128)} %param.14) | copy-start | bytes 12292
  74.6 24.1 %all-to-all-start.1 = ((bf16[8,8,16,512]{3,2,1,0:T(8,128)(2,1)}), bf16[8,8,16,512]{3,2,1,0:T(8,128)(2,1)S(1)}, u32[]{:S(2)}, u32[]{:S(2)}) async-start(bf16[8,8,16,512]{3,2,1,0:T(8,128)(2,1)} %constant_dynamic-update-slice_fusion), calls=%async_computation.1 | async-start | bytes 2097152 | tf_op jit(solution)/shard_map/all_to_all | solution.py:168
  80.6 67.4 %all-gather.2.cloned.1.call-start = ((), (), s32[]{:S(2)}) async-start(), calls=%async_computation.6 | async-start | bytes 1179648 | tf_op jit(solution)/shard_map/all_gather | solution.py:171
  80.7 21.0 %collective-permute-start.9 = (bf16[128,512]{1,0:T(8,128)(2,1)S(1)}, bf16[128,512]{1,0:T(8,128)(2,1)}, u32[]{:S(2)}, u32[]{:S(2)}) collective-permute-start(bf16[128,512]{1,0:T(8,128)(2,1)S(1)} %reshape.121), channel_id=1, source_target_pairs={{0,0},{1,32},{2,64},{3,96},{4,128},{5,160},{6,192},{7,224},{8,8},{... | collective-permute-start | bytes 393224 | tf_op jit(solution)/shard_map/ppermute | solution.py:29
  98.7 1.0 copy-start.1
  101.7 21.1 %all-to-all-start.2 = ((bf16[32,4,512]{2,1,0:T(4,128)(2,1)}), bf16[32,4,512]{2,1,0:T(4,128)(2,1)S(1)}, u32[]{:S(2)}, u32[]{:S(2)}) async-start(bf16[32,4,512]{2,1,0:T(4,128)(2,1)} %shard_map.101), calls=%async_computation.2 | async-start | bytes 262144 | tf_op jit(solution)/shard_map/all_to_all | solution.py:172
  125.2 9.4 %all-to-all-start.3 = ((bf16[8,4,4,512]{3,1,2,0:T(4,128)(2,1)}), bf16[8,4,4,512]{3,1,2,0:T(4,128)(2,1)S(1)}, u32[]{:S(2)}, u32[]{:S(2)}) async-start(bf16[8,4,4,512]{3,1,2,0:T(4,128)(2,1)} %copy.23), calls=%async_computation.3 | async-start | bytes 262144 | tf_op jit(solution)/shard_map/all_to_all | solution.py:178
Sparse Core Ops, SparseCore 0:
  101.8 26.1 all-gather.1

commit v8 on v7

--- a/solution.py
+++ b/solution.py
@@ -82,25 +82,26 @@
     )(*[pot] * blocks, *[lmo] * blocks, keep)
 
 
-def place_kernel(z, parts, out):
+def place_kernel(z, parts, late, out):
     for m in range(NZ):
-        total = jnp.sum(parts[:, m].astype(f32), axis=0)
+        part = late[:, 0] if m == 4 else parts[:, m - (m > 4)]
+        total = jnp.sum(part.astype(f32), axis=0)
         first = (z[0] + m) % NZ * NY
         for q in range(NY):
             out[pl.ds(first + q, 1)] = total[q * QP : (q + 1) * QP].astype(out.dtype)[None]
 
 
-def sum_and_place(z, parts):
+def sum_and_place(z, parts, late):
     whole = pl.BlockSpec(memory_space=pltpu.VMEM)
     return pl.pallas_call(
         place_kernel,
-        in_specs=[pl.BlockSpec(memory_space=pltpu.SMEM), whole],
+        in_specs=[pl.BlockSpec(memory_space=pltpu.SMEM), whole, whole],
         out_specs=whole,
         out_shape=jax.ShapeDtypeStruct((NZ * NY, QP, BLK), bf16),
         cost_estimate=pl.CostEstimate(
             flops=parts.size, bytes_accessed=2 * parts.size, transcendentals=0
         ),
-    )(z.reshape(1), parts)
+    )(z.reshape(1), parts, late)
 
 
 def mask_kernel(sig, pv, out):
@@ -148,25 +149,26 @@
 
     info = permute_all(info, lambda a, b, c: (a, c // 2, 2 * b + c % 2))[0]
     info, xy = tie((info, xy))
-    parts = product(jnp.zeros((NT, NZ, 16, BLK), bf16), xy, 0)
+    parts = product(jnp.zeros((NT, NZ - 1, 16, BLK), bf16), xy, 0)
     up = down = xy
     for s in range(1, 4):
         up, down = along_z(up, 1), along_z(down, -1)
-        parts = product(parts, up, NZ - s)
+        parts = product(parts, up, NZ - s - 1)
         parts = product(parts, down, s)
     up, down = along_z(up[:LEAD], 1), along_z(down[LEAD:], -1)
-    parts = product(parts, up, 4)
-    parts = product(parts, down, 4, 2 * LEAD)
+    over_tile = lambda v: lax.all_to_all(v, "tile", 0, 0, tiled=True)
+    parts = over_tile(parts)
+    late = product(jnp.zeros((NT, 1, 16, BLK), bf16), up, 0)
+    late = product(late, down, 0, 2 * LEAD)
 
     named = info[:nblk]
     pts = lax.dynamic_slice_in_dim(info[nblk:].reshape(3, BP), 16 * (j % 2) + QP * y, QP, 1)
     off = centers.reshape(3, nblk, 1, BLK) - pts.reshape(3, 1, QP, 1)
     coef = 1.0 / jnp.sqrt(jnp.sum(off * off, axis=0) + widths.reshape(nblk, 1, BLK))
     coef = coef * named[:, None, None]
-    parts, coef, piece = tie((parts, coef, piece))
+    late, coef, piece, parts = tie((late, coef, piece, parts))
     piece = permute_all(piece, lambda a, b, c: (c, b, a))
-    parts = lax.all_to_all(parts, "tile", 0, 0, tiled=True)
-    term = sum_and_place(z, parts)
+    term = sum_and_place(z, parts, over_tile(late))
     term, piece = tie((term, piece))
     x_col = lax.all_gather(piece, "tile", axis=0, tiled=True)
     term = lax.all_to_all(term, "grid", 0, 0, tiled=True)

time: 180 us -> 188 us (1.044)
  local copies, waits for them, and re-layouts: 10.4 us -> 14.5 us
  other arithmetic: 2.39 us -> 5.43 us
  starting transfers between devices: 44.2 us -> 46.6 us
  waiting for transfers between devices: 55.9 us -> 53.7 us
    all_to_all x1 -> x2, waiting for transfers between devices: 12.8 us -> 6.08 us  [shards(): over_tile = lambda v: lax.all_to_all(v, 'tile', 0, 0, tiled=True)]
    all_to_all x1 -> x2, starting transfers between devices: 6.05 us -> 12.7 us  [shards(): over_tile = lambda v: lax.all_to_all(v, 'tile', 0, 0, tiled=True)]
    ppermute x8, waiting for transfers between devices: 22.2 us -> 27.3 us  [along_z(): return lax.ppermute(x, 'grid', pairs)]
    all_to_all x1, starting transfers between devices: 11.5 us -> 8.75 us  [shards(): term = lax.all_to_all(term, 'grid', 0, 0, tiled=True)]
    slice x2, local copies, waits for them, and re-layouts: 0.04 us -> 2.42 us  [shards(): up, down = (along_z(up[:LEAD], 1), along_z(down[LEAD:], -1))]
    dynamic_update_slice x9 -> x7, local copies, waits for them, and re-layouts: 6.44 us -> 5.06 us  [product(): lax.dynamic_update_slice(buf, rows.reshape(-1, 1, 16, BLK), (row, slot, 0...]
  transfers between devices with their start and end apart: 15 -> 16, of which waited for: 10 -> 10; matrix products, arithmetic and copies ran while one was open for 12% -> 15% of each run, Pallas kernels for 4% -> 4%
where the time goes in v8:
time: 188 us; the launch traced here: 187 us
  waiting for transfers between devices  53.7 us (29%)
  starting transfers between devices  46.6 us (25%)
  blocking collectives  30.2 us (16%)
  local copies, waits for them, and re-layouts  14.5 us (8%)
  matrix products  14.1 us (8%)
  between operations  13.7 us (7%)
  Pallas kernels  8.93 us (5%)
  other arithmetic  5.43 us (3%)
    ppermute x8, waiting for transfers between devices, along_z(): return lax.ppermute(x, 'grid', pairs)  27.3 us
    all_to_all x1, blocking collectives, spread(): return lax.all_to_all(copies, axis, 0, 0, tiled=True)  21.6 us
    all_to_all x2, starting transfers between devices, shards(): over_tile = lambda v: lax.all_to_all(v, 'tile', 0, 0, tiled=True)  12.7 us
    dot_general x10, matrix products, dot(): lax.dot_general(u, v, (((cu,), (cv,)), ((), ())), preferred_element_type=...  12.7 us
    ppermute x8, starting transfers between devices, along_z(): return lax.ppermute(x, 'grid', pairs)  12.1 us
    all_to_all x1, starting transfers between devices, shards(): term = lax.all_to_all(term, 'grid', 0, 0, tiled=True)  8.75 us
    all_to_all x1, waiting for transfers between devices, shards(): term = lax.all_to_all(term, 'grid', 0, 0, tiled=True)  8.64 us
    all_to_all x1, blocking collectives, shards(): w = lax.all_to_all(w, 'tile', 0, 0, tiled=True)  8.52 us
  transfers between devices with their start and end apart: 16, of which 10 were waited for; matrix products, arithmetic and copies ran while one was open for 15% of the time, Pallas kernels for 4%

profile of v8, /device:TPU:32, one launch (start us, length us, event | category | flops | bytes accessed | tf_op | source)
XLA Modules:
  0.0 187.2 jit_solution(9484831891824301884)
XLA Ops:
  6.5 2.1 %shard_map.100 = bf16[4,32,2048]{2,1,0:T(8,128)(2,1)} custom-call(s32[1,16]{1,0:T(1,128)} %sig.1, bf16[32,2048]{1,0:T(8,128)(2,1)} %pv.1), custom_call_target="tpu_custom_call" | custom-call | flops 65536 | bytes 655360 | tf_op jit(solution)/shard_map/pallas_call | solution.py:121
  8.7 4.5 %all-to-all-start = ((bf16[4,32,2048]{2,1,0:T(8,128)(2,1)}), bf16[4,32,2048]{2,1,0:T(8,128)(2,1)S(1)}, u32[]{:S(2)}, u32[]{:S(2)}) async-start(bf16[4,32,2048]{2,1,0:T(8,128)(2,1)} %shard_map.100), calls=%async_computation | async-start | bytes 1048576 | tf_op jit(solution)/shard_map/all_to_all | solution.py:141
  13.1 0.8 reshape.100
  13.9 0.7 fusion.13
  15.4 1.5 add.43
  17.0 5.6 %all-to-all-done = bf16[4,32,2048]{2,1,0:T(8,128)(2,1)S(1)} async-done(((bf16[4,32,2048]{2,1,0:T(8,128)(2,1)}), bf16[4,32,2048]{2,1,0:T(8,128)(2,1)S(1)}, u32[]{:S(2)}, u32[]{:S(2)}) %all-to-all-start) | async-done | bytes 524320 | tf_op jit(solution)/shard_map/all_to_all | solution.py:141
  22.7 1.9 %collective-permute-start.1 = (bf16[4,32,2048]{2,1,0:T(8,128)(2,1)S(1)}, bf16[4,32,2048]{2,1,0:T(8,128)(2,1)S(1)}, u32[]{:S(2)}, u32[]{:S(2)}) collective-permute-start(bf16[4,32,2048]{2,1,0:T(8,128)(2,1)S(1)} %all-to-all-done), channel_id=1, source_target_pairs={{0,32},{8,40},{16,48},{24,56},{32,64},{40,72},{48,80},{56,88},{64,... | collective-permute-start | bytes 1572872 | tf_op jit(solution)/shard_map/ppermute | solution.py:19
  24.8 0.8 convolution_convert_fusion.7
  25.6 1.0 dynamic_update_slice.26
  26.7 0.8 multiply_reduce_fusion
  27.6 7.5 %collective-permute-done.5 = bf16[4,32,2048]{2,1,0:T(8,128)(2,1)} collective-permute-done((bf16[4,32,2048]{2,1,0:T(8,128)(2,1)S(1)}, bf16[4,32,2048]{2,1,0:T(8,128)(2,1)}, u32[]{:S(2)}, u32[]{:S(2)}) %collective-permute-start.5) | collective-permute-done | bytes 524320 | tf_op jit(solution)/shard_map/ppermute | solution.py:19
  35.1 3.2 %collective-permute-start.6 = (bf16[4,32,2048]{2,1,0:T(8,128)(2,1)}, bf16[4,32,2048]{2,1,0:T(8,128)(2,1)S(1)}, u32[]{:S(2)}, u32[]{:S(2)}) collective-permute-start(bf16[4,32,2048]{2,1,0:T(8,128)(2,1)} %collective-permute-done.5), channel_id=1, source_target_pairs={{0,224},{8,232},{16,240},{24,248},{32,0},{40,8},{48,16},{56,24},{6... | collective-permute-start | bytes 1572872 | tf_op jit(solution)/shard_map/ppermute | solution.py:19
  38.3 1.9 %convolution_convert_fusion.5 = bf16[128,512]{1,0:T(8,128)(2,1)S(1)} fusion(bf16[128,2048]{1,0:T(8,128)(2,1)} %bitcast.12, bf16[512,2048]{1,0:T(8,128)(2,1)S(1)} %copy-done), kind=kOutput, calls=%fused_computation.5 | convolution fusion | flops 268500992 | bytes 2752512 | tf_op jit(solution)/shard_map/dot_general | solution.py:38
  40.3 0.8 convolution_convert_fusion.6
  41.8 0.7 constant_dynamic-update-slice_fusion.4
  42.5 4.9 %collective-permute-done.6 = bf16[4,32,2048]{2,1,0:T(8,128)(2,1)S(1)} collective-permute-done((bf16[4,32,2048]{2,1,0:T(8,128)(2,1)}, bf16[4,32,2048]{2,1,0:T(8,128)(2,1)S(1)}, u32[]{:S(2)}, u32[]{:S(2)}) %collective-permute-start.6) | collective-permute-done | bytes 524320 | tf_op jit(solution)/shard_map/ppermute | solution.py:19
  47.4 3.8 %collective-permute-start.7 = (bf16[4,32,2048]{2,1,0:T(8,128)(2,1)S(1)}, bf16[4,32,2048]{2,1,0:T(8,128)(2,1)S(1)}, u32[]{:S(2)}, u32[]{:S(2)}) collective-permute-start(bf16[4,32,2048]{2,1,0:T(8,128)(2,1)S(1)} %collective-permute-done.6), channel_id=1, source_target_pairs={{0,224},{8,232},{16,240},{24,248},{32,0},{40,8},{48,16},{56,24},{6... | collective-permute-start | bytes 1572872 | tf_op jit(solution)/shard_map/ppermute | solution.py:19
  51.2 0.8 convolution_convert_fusion.3
  52.0 1.3 collective-permute-done.2
  53.3 0.8 convolution_convert_fusion.4
  55.5 3.6 %collective-permute-done.7 = bf16[4,32,2048]{2,1,0:T(8,128)(2,1)S(1)} collective-permute-done((bf16[4,32,2048]{2,1,0:T(8,128)(2,1)S(1)}, bf16[4,32,2048]{2,1,0:T(8,128)(2,1)S(1)}, u32[]{:S(2)}, u32[]{:S(2)}) %collective-permute-start.7) | collective-permute-done | bytes 524320 | tf_op jit(solution)/shard_map/ppermute | solution.py:19
  59.1 0.8 convolution_convert_fusion.1
  59.9 4.7 %collective-permute-done.3 = bf16[4,32,2048]{2,1,0:T(8,128)(2,1)S(1)} collective-permute-done((bf16[4,32,2048]{2,1,0:T(8,128)(2,1)S(1)}, bf16[4,32,2048]{2,1,0:T(8,128)(2,1)S(1)}, u32[]{:S(2)}, u32[]{:S(2)}) %collective-permute-start.3) | collective-permute-done | bytes 524320 | tf_op jit(solution)/shard_map/ppermute | solution.py:19
  64.6 0.8 convolution_convert_fusion.2
  67.4 5.9 %all-to-all-start.1 = ((bf16[8,7,16,512]{3,2,1,0:T(8,128)(2,1)}), bf16[8,7,16,512]{3,2,1,0:T(8,128)(2,1)S(1)}, u32[]{:S(2)}, u32[]{:S(2)}) async-start(bf16[8,7,16,512]{3,2,1,0:T(8,128)(2,1)} %constant_dynamic-update-slice_fusion), calls=%async_computation.1 | async-start | bytes 1835008 | tf_op jit(solution)/shard_map/all_to_all | solution.py:159
  73.3 1.9 %fusion.5 = f32[32,4,512]{2,1,0:T(4,128)} fusion(f32[32,4,512]{2,0,1:T(8,128)} %multiply_reduce_fusion, f32[32]{0:T(128)S(1)} %bitcast.96, f32[32,512]{1,0:T(8,128)} %add.43), kind=kLoop, calls=%fused_computation.19 | loop fusion | flops 131072 | bytes 589952 | tf_op jit(solution)/shard_map/mul | solution.py:168
  75.2 1.8 slice.25
  77.0 2.9 %collective-permute-start.8 = (bf16[3,32,2048]{2,1,0:T(8,128)(2,1)}, bf16[3,32,2048]{2,1,0:T(8,128)(2,1)}, u32[]{:S(2)}, u32[]{:S(2)}) collective-permute-start(bf16[3,32,2048]{2,1,0:T(8,128)(2,1)} %slice.25), channel_id=1, source_target_pairs={{0,224},{8,232},{16,240},{24,248},{32,0},{40,8},{48,16},{56,24},{6... | collective-permute-start | bytes 1179656 | tf_op jit(solution)/shard_map/ppermute | solution.py:19
  80.6 0.9 reshape.106
  81.6 0.7 reshape.107
  82.3 1.6 convolution_convert_fusion.10
  83.9 5.4 %collective-permute-done.8 = bf16[3,32,2048]{2,1,0:T(8,128)(2,1)} collective-permute-done((bf16[3,32,2048]{2,1,0:T(8,128)(2,1)}, bf16[3,32,2048]{2,1,0:T(8,128)(2,1)}, u32[]{:S(2)}, u32[]{:S(2)}) %collective-permute-start.8) | collective-permute-done | bytes 393248 | tf_op jit(solution)/shard_map/ppermute | solution.py:19
  89.3 1.8 convolution_convert_fusion.9
  91.8 4.5 %collective-permute-start.9 = (bf16[128,512]{1,0:T(8,128)(2,1)}, bf16[128,512]{1,0:T(8,128)(2,1)S(1)}, u32[]{:S(2)}, u32[]{:S(2)}) collective-permute-start(bf16[128,512]{1,0:T(8,128)(2,1)} %reshape.107), channel_id=1, source_target_pairs={{0,0},{1,32},{2,64},{3,96},{4,128},{5,160},{6,192},{7,224},{8,8},{... | collective-permute-start | bytes 393224 | tf_op jit(solution)/shard_map/ppermute | solution.py:29
  96.2 6.8 %all-to-all-start.2 = ((bf16[8,1,16,512]{3,2,1,0:T(8,128)(2,1)}), bf16[8,1,16,512]{3,2,1,0:T(8,128)(2,1)S(1)}, u32[]{:S(2)}, u32[]{:S(2)}) async-start(bf16[8,1,16,512]{3,2,1,0:T(8,128)(2,1)} %pad_maximum_fusion), calls=%async_computation.2 | async-start | bytes 262144 | tf_op jit(solution)/shard_map/all_to_all | solution.py:159
  103.1 6.1 %all-to-all-done.2.late = bf16[8,1,16,512]{3,2,1,0:T(8,128)(2,1)S(1)} async-done(((bf16[8,1,16,512]{3,2,1,0:T(8,128)(2,1)}), bf16[8,1,16,512]{3,2,1,0:T(8,128)(2,1)S(1)}, u32[]{:S(2)}, u32[]{:S(2)}) %all-to-all-start.2) | async-done | bytes 131104 | tf_op jit(solution)/shard_map/all_to_all | solution.py:159
  109.9 2.0 %shard_map.101 = bf16[32,4,512]{2,1,0:T(4,128)(2,1)} custom-call(s32[1]{0:T(128)} %bitcast.22.z, bf16[8,7,16,512]{3,2,1,0:T(8,128)(2,1)} %copy-done.1, bf16[8,1,16,512]{3,2,1,0:T(8,128)(2,1)} %copy-done.4), custom_call_target="tpu_custom_call" | custom-call | flops 458752 | bytes 917504 | tf_op jit(solution)/shard_map/pallas_call | solution.py:96
  112.5 8.8 %all-to-all-start.3 = ((bf16[32,4,512]{2,1,0:T(4,128)(2,1)}), bf16[32,4,512]{2,1,0:T(4,128)(2,1)S(1)}, u32[]{:S(2)}, u32[]{:S(2)}) async-start(bf16[32,4,512]{2,1,0:T(4,128)(2,1)} %shard_map.101), calls=%async_computation.3 | async-start | bytes 262144 | tf_op jit(solution)/shard_map/all_to_all | solution.py:174
  121.3 0.9 compare_reduce_fusion
  122.2 8.6 %all-to-all-done.3 = bf16[32,4,512]{2,1,0:T(4,128)(2,1)S(1)} async-done(((bf16[32,4,512]{2,1,0:T(4,128)(2,1)}), bf16[32,4,512]{2,1,0:T(4,128)(2,1)S(1)}, u32[]{:S(2)}, u32[]{:S(2)}) %all-to-all-start.3) | async-done | bytes 131104 | tf_op jit(solution)/shard_map/all_to_all | solution.py:174
  130.9 1.4 fusion.1
  132.5 0.7 copy.23
  133.2 3.4 %all-to-all-start.4 = ((bf16[8,4,4,512]{3,1,2,0:T(4,128)(2,1)}), bf16[8,4,4,512]{3,1,2,0:T(4,128)(2,1)S(1)}, u32[]{:S(2)}, u32[]{:S(2)}) async-start(bf16[8,4,4,512]{3,1,2,0:T(4,128)(2,1)} %copy.23), calls=%async_computation.4 | async-start | bytes 262144 | tf_op jit(solution)/shard_map/all_to_all | solution.py:180
  136.8 6.0 %all-to-all-done.4 = bf16[8,4,4,512]{3,1,2,0:T(4,128)(2,1)S(1)} async-done(((bf16[8,4,4,512]{3,1,2,0:T(4,128)(2,1)}), bf16[8,4,4,512]{3,1,2,0:T(4,128)(2,1)S(1)}, u32[]{:S(2)}, u32[]{:S(2)}) %all-to-all-start.4) | async-done | bytes 131104 | tf_op jit(solution)/shard_map/all_to_all | solution.py:180
  142.8 4.8 %shard_map.102 = bf16[8,32,256]{2,1,0:T(8,128)(2,1)S(1)} custom-call(bf16[32,2048]{1,0:T(8,128)(2,1)S(1)} %bitcast.69, bf16[32,2048]{1,0:T(8,128)(2,1)S(1)} %bitcast.70, bf16[32,2048]{1,0:T(8,128)(2,1)S(1)} %bitcast.71, bf16[32,2048]{1,0:T(8,128)(2,1)S(1)} %bitcast.72, bf16[2048,2048]{1,0:T(8,128)(2,1)} %refs_7_.1, bf16[2048,2048]{1,0:T(8,128)(2,1)} %refs_7_.1, ...), custom_call_target="tpu_custom_call" | custom-call | flops 268435456 | bytes 8388608 | tf_op jit(solution)/shard_map/pallas_call | solution.py:69
  147.7 8.5 %all_to_all.35 = bf16[8,32,256]{2,1,0:T(8,128)(2,1)S(1)} all-to-all(bf16[8,32,256]{2,1,0:T(8,128)(2,1)S(1)} %shard_map.102), channel_id=1, replica_groups=mesh['grid'=32,'tile'=8] {'tile'}, dimensions={0} | all-to-all | bytes 262144 | tf_op jit(solution)/shard_map/all_to_all | solution.py:186
  156.3 21.6 %all_to_all.36 = bf16[32,32,256]{2,1,0:T(8,128)(2,1)S(1)} all-to-all(bf16[32,32,256]{2,1,0:T(8,128)(2,1)S(1)} %broadcast_in_dim.8), channel_id=1, replica_groups=mesh['grid'=32,'tile'=8] {'grid'}, dimensions={0} | all-to-all | bytes 1048576 | tf_op jit(solution)/shard_map/all_to_all | solution.py:34
  178.0 2.4 %convolution_convert_fusion = bf16[256,512]{1,0:T(8,128)(2,1)} fusion(bf16[1024,256]{1,0:T(8,128)(2,1)S(1)} %bitcast.78, bf16[1024,512]{1,0:T(8,128)(2,1)} %all-gather.2.cloned.1.call-done), kind=kOutput, calls=%fused_computation | convolution fusion | flops 268566528 | bytes 1835008 | tf_op jit(solution)/shard_map/dot_general | solution.py:38
  (53 shorter events, 8.5 us)
Async XLA Ops:
  6.5 18.3 %copy-start = (bf16[512,2048]{1,0:T(8,128)(2,1)S(1)}, bf16[512,2048]{1,0:T(8,128)(2,1)}, u32[]{:S(2)}) copy-start(bf16[512,2048]{1,0:T(8,128)(2,1)} %param.12) | copy-start | bytes 6291460
  6.5 10.3 %copy-start.5 = (f32[3,16384]{1,0:T(4,128)S(1)}, f32[3,16384]{1,0:T(4,128)}, u32[]{:S(2)}) copy-start(f32[3,16384]{1,0:T(4,128)} %param.15) | copy-start | bytes 589828
  8.7 13.9 %all-to-all-start = ((bf16[4,32,2048]{2,1,0:T(8,128)(2,1)}), bf16[4,32,2048]{2,1,0:T(8,128)(2,1)S(1)}, u32[]{:S(2)}, u32[]{:S(2)}) async-start(bf16[4,32,2048]{2,1,0:T(8,128)(2,1)} %shard_map.100), calls=%async_computation | async-start | bytes 1048576 | tf_op jit(solution)/shard_map/all_to_all | solution.py:141
  14.7 2.2 %collective-permute-start = (f32[1,128]{1,0:T(1,128)S(1)}, f32[1,128]{1,0:T(1,128)S(1)}, u32[]{:S(2)}, u32[]{:S(2)}) collective-permute-start(f32[1,128]{1,0:T(1,128)S(1)} %maximum_bitcast_fusion), channel_id=1, source_target_pairs={{0,0},{1,1},{2,8},{3,9},{4,16},{5,17},{6,24},{7,25},{8,2},{9,3},{1... | collective-permute-start | bytes 1544 | tf_op jit(solution)/shard_map/ppermute | solution.py:29
  22.6 12.5 %collective-permute-start.5 = (bf16[4,32,2048]{2,1,0:T(8,128)(2,1)S(1)}, bf16[4,32,2048]{2,1,0:T(8,128)(2,1)}, u32[]{:S(2)}, u32[]{:S(2)}) collective-permute-start(bf16[4,32,2048]{2,1,0:T(8,128)(2,1)S(1)} %all-to-all-done), channel_id=1, source_target_pairs={{0,224},{8,232},{16,240},{24,248},{32,0},{40,8},{48,16},{56,24},{6... | collective-permute-start | bytes 1572872 | tf_op jit(solution)/shard_map/ppermute | solution.py:19
  22.7 17.5 %collective-permute-start.1 = (bf16[4,32,2048]{2,1,0:T(8,128)(2,1)S(1)}, bf16[4,32,2048]{2,1,0:T(8,128)(2,1)S(1)}, u32[]{:S(2)}, u32[]{:S(2)}) collective-permute-start(bf16[4,32,2048]{2,1,0:T(8,128)(2,1)S(1)} %all-to-all-done), channel_id=1, source_target_pairs={{0,32},{8,40},{16,48},{24,56},{32,64},{40,72},{48,80},{56,88},{64,... | collective-permute-start | bytes 1572872 | tf_op jit(solution)/shard_map/ppermute | solution.py:19
  35.1 12.3 %collective-permute-start.6 = (bf16[4,32,2048]{2,1,0:T(8,128)(2,1)}, bf16[4,32,2048]{2,1,0:T(8,128)(2,1)S(1)}, u32[]{:S(2)}, u32[]{:S(2)}) collective-permute-start(bf16[4,32,2048]{2,1,0:T(8,128)(2,1)} %collective-permute-done.5), channel_id=1, source_target_pairs={{0,224},{8,232},{16,240},{24,248},{32,0},{40,8},{48,16},{56,24},{6... | collective-permute-start | bytes 1572872 | tf_op jit(solution)/shard_map/ppermute | solution.py:19
  40.2 13.1 %collective-permute-start.2 = (bf16[4,32,2048]{2,1,0:T(8,128)(2,1)S(1)}, bf16[4,32,2048]{2,1,0:T(8,128)(2,1)S(1)}, u32[]{:S(2)}, u32[]{:S(2)}) collective-permute-start(bf16[4,32,2048]{2,1,0:T(8,128)(2,1)S(1)} %collective-permute-done.1), channel_id=1, source_target_pairs={{0,32},{8,40},{16,48},{24,56},{32,64},{40,72},{48,80},{56,88},{64,... | collective-permute-start | bytes 1572872 | tf_op jit(solution)/shard_map/ppermute | solution.py:19
  47.4 11.7 %collective-permute-start.7 = (bf16[4,32,2048]{2,1,0:T(8,128)(2,1)S(1)}, bf16[4,32,2048]{2,1,0:T(8,128)(2,1)S(1)}, u32[]{:S(2)}, u32[]{:S(2)}) collective-permute-start(bf16[4,32,2048]{2,1,0:T(8,128)(2,1)S(1)} %collective-permute-done.6), channel_id=1, source_target_pairs={{0,224},{8,232},{16,240},{24,248},{32,0},{40,8},{48,16},{56,24},{6... | collective-permute-start | bytes 1572872 | tf_op jit(solution)/shard_map/ppermute | solution.py:19
  53.3 11.3 %collective-permute-start.3 = (bf16[4,32,2048]{2,1,0:T(8,128)(2,1)S(1)}, bf16[4,32,2048]{2,1,0:T(8,128)(2,1)S(1)}, u32[]{:S(2)}, u32[]{:S(2)}) collective-permute-start(bf16[4,32,2048]{2,1,0:T(8,128)(2,1)S(1)} %collective-permute-done.2), channel_id=1, source_target_pairs={{0,32},{8,40},{16,48},{24,56},{32,64},{40,72},{48,80},{56,88},{64,... | collective-permute-start | bytes 1572872 | tf_op jit(solution)/shard_map/ppermute | solution.py:19
  59.1 6.4 %copy-start.3 = (bf16[4,32,2048]{2,1,0:T(8,128)(2,1)}, bf16[4,32,2048]{2,1,0:T(8,128)(2,1)S(1)}, u32[]{:S(2)}) copy-start(bf16[4,32,2048]{2,1,0:T(8,128)(2,1)S(1)} %collective-permute-done.7) | copy-start | bytes 1572868
  66.1 16.2 %collective-permute-start.4 = (bf16[1,32,2048]{2,1,0:T(8,128)(2,1)}, bf16[1,32,2048]{2,1,0:T(8,128)(2,1)}, u32[]{:S(2)}, u32[]{:S(2)}) collective-permute-start(bf16[1,32,2048]{2,1,0:T(8,128)(2,1)} %slice.24), channel_id=1, source_target_pairs={{0,32},{8,40},{16,48},{24,56},{32,64},{40,72},{48,80},{56,88},{64,... | collective-permute-start | bytes 393224 | tf_op jit(solution)/shard_map/ppermute | solution.py:19
  67.4 24.4 %all-to-all-start.1 = ((bf16[8,7,16,512]{3,2,1,0:T(8,128)(2,1)}), bf16[8,7,16,512]{3,2,1,0:T(8,128)(2,1)S(1)}, u32[]{:S(2)}, u32[]{:S(2)}) async-start(bf16[8,7,16,512]{3,2,1,0:T(8,128)(2,1)} %constant_dynamic-update-slice_fusion), calls=%async_computation.1 | async-start | bytes 1835008 | tf_op jit(solution)/shard_map/all_to_all | solution.py:159
  77.0 12.3 %collective-permute-start.8 = (bf16[3,32,2048]{2,1,0:T(8,128)(2,1)}, bf16[3,32,2048]{2,1,0:T(8,128)(2,1)}, u32[]{:S(2)}, u32[]{:S(2)}) collective-permute-start(bf16[3,32,2048]{2,1,0:T(8,128)(2,1)} %slice.25), channel_id=1, source_target_pairs={{0,224},{8,232},{16,240},{24,248},{32,0},{40,8},{48,16},{56,24},{6... | collective-permute-start | bytes 1179656 | tf_op jit(solution)/shard_map/ppermute | solution.py:19
  89.3 41.5 %copy-start.2 = (f32[32,4,512]{2,1,0:T(4,128)S(1)}, f32[32,4,512]{2,1,0:T(4,128)}, u32[]{:S(2)}) copy-start(f32[32,4,512]{2,1,0:T(4,128)} %fusion.5) | copy-start | bytes 786436
  89.3 41.6 %copy-start.7 = (s32[32,32]{1,0:T(8,128)S(1)}, s32[32,32]{1,0:T(8,128)}, u32[]{:S(2)}) copy-start(s32[32,32]{1,0:T(8,128)} %param.14) | copy-start | bytes 12292
  91.8 17.4 %copy-start.1 = (bf16[8,7,16,512]{3,2,1,0:T(8,128)(2,1)}, bf16[8,7,16,512]{3,2,1,0:T(8,128)(2,1)S(1)}, u32[]{:S(2)}) copy-start(bf16[8,7,16,512]{3,2,1,0:T(8,128)(2,1)S(1)} %all-to-all-done.1.parts) | copy-start | bytes 2752516
  91.8 20.1 %collective-permute-start.9 = (bf16[128,512]{1,0:T(8,128)(2,1)}, bf16[128,512]{1,0:T(8,128)(2,1)S(1)}, u32[]{:S(2)}, u32[]{:S(2)}) collective-permute-start(bf16[128,512]{1,0:T(8,128)(2,1)} %reshape.107), channel_id=1, source_target_pairs={{0,0},{1,32},{2,64},{3,96},{4,128},{5,160},{6,192},{7,224},{8,8},{... | collective-permute-start | bytes 393224 | tf_op jit(solution)/shard_map/ppermute | solution.py:29
  96.2 12.9 %all-to-all-start.2 = ((bf16[8,1,16,512]{3,2,1,0:T(8,128)(2,1)}), bf16[8,1,16,512]{3,2,1,0:T(8,128)(2,1)S(1)}, u32[]{:S(2)}, u32[]{:S(2)}) async-start(bf16[8,1,16,512]{3,2,1,0:T(8,128)(2,1)} %pad_maximum_fusion), calls=%async_computation.2 | async-start | bytes 262144 | tf_op jit(solution)/shard_map/all_to_all | solution.py:159
  103.1 53.2 %all-gather.2.cloned.1.call-start = ((), (), s32[]{:S(2)}) async-start(), calls=%async_computation.7 | async-start | bytes 1179648 | tf_op jit(solution)/shard_map/all_gather | solution.py:173
  109.2 0.7 copy-start.4
  111.8 0.6 copy-start.6
  112.5 18.3 %all-to-all-start.3 = ((bf16[32,4,512]{2,1,0:T(4,128)(2,1)}), bf16[32,4,512]{2,1,0:T(4,128)(2,1)S(1)}, u32[]{:S(2)}, u32[]{:S(2)}) async-start(bf16[32,4,512]{2,1,0:T(4,128)(2,1)} %shard_map.101), calls=%async_computation.3 | async-start | bytes 262144 | tf_op jit(solution)/shard_map/all_to_all | solution.py:174
  133.2 9.6 %all-to-all-start.4 = ((bf16[8,4,4,512]{3,1,2,0:T(4,128)(2,1)}), bf16[8,4,4,512]{3,1,2,0:T(4,128)(2,1)S(1)}, u32[]{:S(2)}, u32[]{:S(2)}) async-start(bf16[8,4,4,512]{3,1,2,0:T(4,128)(2,1)} %copy.23), calls=%async_computation.4 | async-start | bytes 262144 | tf_op jit(solution)/shard_map/all_to_all | solution.py:180
Sparse Core Ops, SparseCore 0:
  112.6 24.9 all-gather.1

commit v9 on v7

--- a/solution.py
+++ b/solution.py
@@ -82,25 +82,53 @@
     )(*[pot] * blocks, *[lmo] * blocks, keep)
 
 
-def place_kernel(z, parts, out):
+def place_kernel(z, *refs):
+    quarters, out = refs[:4], refs[4]
     for m in range(NZ):
-        total = jnp.sum(parts[:, m].astype(f32), axis=0)
+        total = sum(jnp.sum(part[:, m].astype(f32), axis=0) for part in quarters)
         first = (z[0] + m) % NZ * NY
         for q in range(NY):
             out[pl.ds(first + q, 1)] = total[q * QP : (q + 1) * QP].astype(out.dtype)[None]
 
 
 def sum_and_place(z, parts):
-    whole = pl.BlockSpec(memory_space=pltpu.VMEM)
+    block = (NT // 4,) + parts.shape[1:]
+    shape = (NZ * NY, QP, BLK)
     return pl.pallas_call(
         place_kernel,
-        in_specs=[pl.BlockSpec(memory_space=pltpu.SMEM), whole],
-        out_specs=whole,
-        out_shape=jax.ShapeDtypeStruct((NZ * NY, QP, BLK), bf16),
+        grid=(1,),
+        in_specs=[pl.BlockSpec(memory_space=pltpu.SMEM)]
+        + [pl.BlockSpec(block, lambda i, k=k: (k, 0, 0, 0)) for k in range(4)],
+        out_specs=pl.BlockSpec(shape, lambda i: (0, 0, 0)),
+        out_shape=jax.ShapeDtypeStruct(shape, bf16),
         cost_estimate=pl.CostEstimate(
             flops=parts.size, bytes_accessed=2 * parts.size, transcendentals=0
         ),
-    )(z.reshape(1), parts)
+    )(z.reshape(1), *[parts] * 4)
+
+
+def last_kernel(*refs):
+    n = len(refs) // 2
+    total = 0.0
+    for w, x in zip(refs[:n], refs[n : 2 * n]):
+        total = total + dot(w[...], x[...], 0, 0)
+    refs[-1][...] = total.astype(refs[-1].dtype)
+
+
+def last_product(w, x, streams=4):
+    rows = w.shape[0] // streams
+    shape = (w.shape[1], x.shape[1])
+    at = lambda v, k: pl.BlockSpec((rows, v.shape[1]), lambda i: (k, 0))
+    return pl.pallas_call(
+        last_kernel,
+        grid=(1,),
+        in_specs=[at(v, k) for v in (w, x) for k in range(streams)],
+        out_specs=pl.BlockSpec(shape, lambda i: (0, 0)),
+        out_shape=jax.ShapeDtypeStruct(shape, bf16),
+        cost_estimate=pl.CostEstimate(
+            flops=2 * w.size * x.shape[1], bytes_accessed=2 * (w.size + x.size), transcendentals=0
+        ),
+    )(*[w] * streams, *[x] * streams)
 
 
 def mask_kernel(sig, pv, out):
@@ -185,7 +213,7 @@
     w = jnp.sum(w.astype(f32), axis=0).astype(bf16)
     w, x_col = tie((w, x_col))
     w_all = spread(w, "grid", NZ * NY).reshape(-1, 256)
-    return dot(w_all, x_col, 0, 0).astype(bf16)
+    return last_product(w_all, x_col)
 
 
 def solution(mesh):

time: 180 us -> 180 us (level)
  Pallas kernels: 8.97 us -> 11.5 us
  matrix products: 13.3 us -> 10.9 us
    pallas_call x1 -> x2, Pallas kernels: 2.02 us -> 4.57 us  [the longest x1 2.57 us: last_product(): pl.pallas_call(last_kernel, grid=(1,), in_specs=[at(v, k) for v in (w, x)...]
    dot_general x10 -> x9, matrix products: 11.8 us -> 9.46 us  [dot(): lax.dot_general(u, v, (((cu,), (cv,)), ((), ())), preferred_element_type=...]
where the time goes in v9:
time: 180 us; the launch traced here: 179 us
  waiting for transfers between devices  55.9 us (31%)
  starting transfers between devices  44.1 us (24%)
  blocking collectives  30.5 us (17%)
  between operations  13.7 us (8%)
  Pallas kernels  11.5 us (6%)
  matrix products  10.9 us (6%)
  local copies, waits for them, and re-layouts  10.4 us (6%)
  other arithmetic  2.39 us (1%)
    ppermute x8, waiting for transfers between devices, along_z(): return lax.ppermute(x, 'grid', pairs)  22.2 us
    all_to_all x1, blocking collectives, spread(): return lax.all_to_all(copies, axis, 0, 0, tiled=True)  21.9 us
    ppermute x8, starting transfers between devices, along_z(): return lax.ppermute(x, 'grid', pairs)  12.9 us
    all_to_all x1, waiting for transfers between devices, shards(): parts = lax.all_to_all(parts, 'tile', 0, 0, tiled=True)  12.8 us
    all_to_all x1, starting transfers between devices, shards(): term = lax.all_to_all(term, 'grid', 0, 0, tiled=True)  11.5 us
    dot_general x9, matrix products, dot(): lax.dot_general(u, v, (((cu,), (cv,)), ((), ())), preferred_element_type=...  9.46 us
    all_to_all x1, waiting for transfers between devices, shards(): term = lax.all_to_all(term, 'grid', 0, 0, tiled=True)  8.63 us
    all_to_all x1, blocking collectives, shards(): w = lax.all_to_all(w, 'tile', 0, 0, tiled=True)  8.52 us
  transfers between devices with their start and end apart: 15, of which 10 were waited for; matrix products, arithmetic and copies ran while one was open for 12% of the time, Pallas kernels for 4%

profile of v9, /device:TPU:32, one launch (start us, length us, event | category | flops | bytes accessed | tf_op | source)
XLA Modules:
  0.0 179.3 jit_solution(13125694327724237293)
XLA Ops:
  6.5 2.1 %shard_map.100 = bf16[4,32,2048]{2,1,0:T(8,128)(2,1)} custom-call(s32[1,16]{1,0:T(1,128)} %sig.1, bf16[32,2048]{1,0:T(8,128)(2,1)} %pv.1), custom_call_target="tpu_custom_call" | custom-call | flops 65536 | bytes 655360 | tf_op jit(solution)/shard_map/pallas_call | solution.py:148
  8.7 4.5 %all-to-all-start = ((bf16[4,32,2048]{2,1,0:T(8,128)(2,1)}), bf16[4,32,2048]{2,1,0:T(8,128)(2,1)S(1)}, u32[]{:S(2)}, u32[]{:S(2)}) async-start(bf16[4,32,2048]{2,1,0:T(8,128)(2,1)} %shard_map.100), calls=%async_computation | async-start | bytes 1048576 | tf_op jit(solution)/shard_map/all_to_all | solution.py:168
  13.1 0.8 reshape.100
  13.9 0.7 fusion.13
  15.4 0.9 add.43
  16.4 6.2 %all-to-all-done = bf16[4,32,2048]{2,1,0:T(8,128)(2,1)S(1)} async-done(((bf16[4,32,2048]{2,1,0:T(8,128)(2,1)}), bf16[4,32,2048]{2,1,0:T(8,128)(2,1)S(1)}, u32[]{:S(2)}, u32[]{:S(2)}) %all-to-all-start) | async-done | bytes 524320 | tf_op jit(solution)/shard_map/all_to_all | solution.py:168
  22.7 1.9 %collective-permute-start.1 = (bf16[4,32,2048]{2,1,0:T(8,128)(2,1)S(1)}, bf16[4,32,2048]{2,1,0:T(8,128)(2,1)}, u32[]{:S(2)}, u32[]{:S(2)}) collective-permute-start(bf16[4,32,2048]{2,1,0:T(8,128)(2,1)S(1)} %all-to-all-done), channel_id=1, source_target_pairs={{0,32},{8,40},{16,48},{24,56},{32,64},{40,72},{48,80},{56,88},{64,... | collective-permute-start | bytes 1572872 | tf_op jit(solution)/shard_map/ppermute | solution.py:19
  24.6 0.8 convolution_convert_fusion.6
  25.8 1.1 dynamic_update_slice.27
  27.3 7.7 %collective-permute-done.2 = bf16[4,32,2048]{2,1,0:T(8,128)(2,1)} collective-permute-done((bf16[4,32,2048]{2,1,0:T(8,128)(2,1)S(1)}, bf16[4,32,2048]{2,1,0:T(8,128)(2,1)}, u32[]{:S(2)}, u32[]{:S(2)}) %collective-permute-start.2) | collective-permute-done | bytes 524320 | tf_op jit(solution)/shard_map/ppermute | solution.py:19
  35.1 3.2 %collective-permute-start.4 = (bf16[4,32,2048]{2,1,0:T(8,128)(2,1)}, bf16[4,32,2048]{2,1,0:T(8,128)(2,1)S(1)}, u32[]{:S(2)}, u32[]{:S(2)}) collective-permute-start(bf16[4,32,2048]{2,1,0:T(8,128)(2,1)} %collective-permute-done.2), channel_id=1, source_target_pairs={{0,224},{8,232},{16,240},{24,248},{32,0},{40,8},{48,16},{56,24},{6... | collective-permute-start | bytes 1572872 | tf_op jit(solution)/shard_map/ppermute | solution.py:19
  38.3 1.9 %convolution_convert_fusion.4 = bf16[128,512]{1,0:T(8,128)(2,1)S(1)} fusion(bf16[128,2048]{1,0:T(8,128)(2,1)} %bitcast.7, bf16[512,2048]{1,0:T(8,128)(2,1)S(1)} %copy-done), kind=kOutput, calls=%fused_computation.4 | convolution fusion | flops 268500992 | bytes 2752512 | tf_op jit(solution)/shard_map/dot_general | solution.py:38
  40.3 1.9 %convolution_convert_fusion.5 = bf16[128,512]{1,0:T(8,128)(2,1)S(1)} fusion(bf16[128,2048]{1,0:T(8,128)(2,1)} %bitcast.5, bf16[512,2048]{1,0:T(8,128)(2,1)S(1)} %copy-done), kind=kOutput, calls=%fused_computation.5 | convolution fusion | flops 268500992 | bytes 2752512 | tf_op jit(solution)/shard_map/dot_general | solution.py:38
  42.2 0.7 constant_dynamic-update-slice_fusion.7
  42.9 0.7 constant_dynamic-update-slice_fusion.6
  43.5 3.8 %collective-permute-done.4 = bf16[4,32,2048]{2,1,0:T(8,128)(2,1)S(1)} collective-permute-done((bf16[4,32,2048]{2,1,0:T(8,128)(2,1)}, bf16[4,32,2048]{2,1,0:T(8,128)(2,1)S(1)}, u32[]{:S(2)}, u32[]{:S(2)}) %collective-permute-start.4) | collective-permute-done | bytes 524320 | tf_op jit(solution)/shard_map/ppermute | solution.py:19
  47.4 3.8 %collective-permute-start.6 = (bf16[4,32,2048]{2,1,0:T(8,128)(2,1)S(1)}, bf16[4,32,2048]{2,1,0:T(8,128)(2,1)S(1)}, u32[]{:S(2)}, u32[]{:S(2)}) collective-permute-start(bf16[4,32,2048]{2,1,0:T(8,128)(2,1)S(1)} %collective-permute-done.4), channel_id=1, source_target_pairs={{0,224},{8,232},{16,240},{24,248},{32,0},{40,8},{48,16},{56,24},{6... | collective-permute-start | bytes 1572872 | tf_op jit(solution)/shard_map/ppermute | solution.py:19
  51.2 0.8 convolution_convert_fusion.2
  52.0 1.5 collective-permute-done.3
  53.5 0.8 convolution_convert_fusion.3
  54.3 0.7 constant_dynamic-update-slice_fusion.5
  55.0 0.7 constant_dynamic-update-slice_fusion.4
  55.7 3.8 %collective-permute-done.6 = bf16[4,32,2048]{2,1,0:T(8,128)(2,1)S(1)} collective-permute-done((bf16[4,32,2048]{2,1,0:T(8,128)(2,1)S(1)}, bf16[4,32,2048]{2,1,0:T(8,128)(2,1)S(1)}, u32[]{:S(2)}, u32[]{:S(2)}) %collective-permute-start.6) | collective-permute-done | bytes 524320 | tf_op jit(solution)/shard_map/ppermute | solution.py:19
  59.6 3.6 %collective-permute-start.8 = (bf16[3,32,2048]{2,1,0:T(8,128)(2,1)S(1)}, bf16[3,32,2048]{2,1,0:T(8,128)(2,1)S(1)}, u32[]{:S(2)}, u32[]{:S(2)}) collective-permute-start(bf16[3,32,2048]{2,1,0:T(8,128)(2,1)S(1)} %slice.25), channel_id=1, source_target_pairs={{0,224},{8,232},{16,240},{24,248},{32,0},{40,8},{48,16},{56,24},{6... | collective-permute-start | bytes 1179656 | tf_op jit(solution)/shard_map/ppermute | solution.py:19
  63.1 0.8 convolution_convert_fusion
  64.0 0.8 collective-permute-done.5
  64.8 0.8 convolution_convert_fusion.1
  65.9 0.7 constant_dynamic-update-slice_fusion.3
  66.6 0.7 constant_dynamic-update-slice_fusion.2
  67.2 4.5 %collective-permute-done.7 = bf16[1,32,2048]{2,1,0:T(8,128)(2,1)S(1)} collective-permute-done((bf16[1,32,2048]{2,1,0:T(8,128)(2,1)S(1)}, bf16[1,32,2048]{2,1,0:T(8,128)(2,1)S(1)}, u32[]{:S(2)}, u32[]{:S(2)}) %collective-permute-start.7) | collective-permute-done | bytes 131104 | tf_op jit(solution)/shard_map/ppermute | solution.py:19
  71.8 0.7 convolution_convert_fusion.9
  73.1 0.8 convolution_convert_fusion.8
  74.6 5.9 %all-to-all-start.1 = ((bf16[8,8,16,512]{3,2,1,0:T(8,128)(2,1)}), bf16[8,8,16,512]{3,2,1,0:T(8,128)(2,1)S(1)}, u32[]{:S(2)}, u32[]{:S(2)}) async-start(bf16[8,8,16,512]{3,2,1,0:T(8,128)(2,1)} %constant_dynamic-update-slice_fusion), calls=%async_computation.1 | async-start | bytes 2097152 | tf_op jit(solution)/shard_map/all_to_all | solution.py:196
  80.5 5.2 %collective-permute-start.9 = (bf16[128,512]{1,0:T(8,128)(2,1)S(1)}, bf16[128,512]{1,0:T(8,128)(2,1)}, u32[]{:S(2)}, u32[]{:S(2)}) collective-permute-start(bf16[128,512]{1,0:T(8,128)(2,1)S(1)} %reshape.121), channel_id=1, source_target_pairs={{0,0},{1,32},{2,64},{3,96},{4,128},{5,160},{6,192},{7,224},{8,8},{... | collective-permute-start | bytes 393224 | tf_op jit(solution)/shard_map/ppermute | solution.py:29
  85.8 12.8 %all-to-all-done.1.refs_0_.refs_1_.refs_2_.refs_3_ = bf16[8,8,16,512]{3,2,1,0:T(8,128)(2,1)S(1)} async-done(((bf16[8,8,16,512]{3,2,1,0:T(8,128)(2,1)}), bf16[8,8,16,512]{3,2,1,0:T(8,128)(2,1)S(1)}, u32[]{:S(2)}, u32[]{:S(2)}) %all-to-all-start.1) | async-done | bytes 1048608 | tf_op jit(solution)/shard_map/all_to_all | solution.py:196
  98.6 1.0 copy-done.1
  99.5 2.0 %shard_map.101 = bf16[32,4,512]{2,1,0:T(4,128)(2,1)} custom-call(s32[1]{0:T(128)} %bitcast.22.z, bf16[8,8,16,512]{3,2,1,0:T(8,128)(2,1)} %copy-done.1, bf16[8,8,16,512]{3,2,1,0:T(8,128)(2,1)} %copy-done.1, bf16[8,8,16,512]{3,2,1,0:T(8,128)(2,1)} %copy-done.1, bf16[8,8,16,512]{3,2,1,0:T(8,128)(2,1)} %copy-done.1), custom_call_target="tpu_custom_call" | custom-call | flops 524288 | bytes 1048576 | tf_op jit(solution)/shard_map/pallas_call | solution.py:97
  101.6 11.5 %all-to-all-start.2 = ((bf16[32,4,512]{2,1,0:T(4,128)(2,1)}), bf16[32,4,512]{2,1,0:T(4,128)(2,1)S(1)}, u32[]{:S(2)}, u32[]{:S(2)}) async-start(bf16[32,4,512]{2,1,0:T(4,128)(2,1)} %shard_map.101), calls=%async_computation.2 | async-start | bytes 262144 | tf_op jit(solution)/shard_map/all_to_all | solution.py:200
  113.1 0.9 compare_reduce_fusion
  114.0 8.6 %all-to-all-done.2 = bf16[32,4,512]{2,1,0:T(4,128)(2,1)S(1)} async-done(((bf16[32,4,512]{2,1,0:T(4,128)(2,1)}), bf16[32,4,512]{2,1,0:T(4,128)(2,1)S(1)}, u32[]{:S(2)}, u32[]{:S(2)}) %all-to-all-start.2) | async-done | bytes 131104 | tf_op jit(solution)/shard_map/all_to_all | solution.py:200
  122.7 1.4 fusion.1
  124.3 0.7 copy.20
  125.0 3.4 %all-to-all-start.3 = ((bf16[8,4,4,512]{3,1,2,0:T(4,128)(2,1)}), bf16[8,4,4,512]{3,1,2,0:T(4,128)(2,1)S(1)}, u32[]{:S(2)}, u32[]{:S(2)}) async-start(bf16[8,4,4,512]{3,1,2,0:T(4,128)(2,1)} %copy.20), calls=%async_computation.3 | async-start | bytes 262144 | tf_op jit(solution)/shard_map/all_to_all | solution.py:206
  128.5 5.9 %all-to-all-done.3 = bf16[8,4,4,512]{3,1,2,0:T(4,128)(2,1)S(1)} async-done(((bf16[8,4,4,512]{3,1,2,0:T(4,128)(2,1)}), bf16[8,4,4,512]{3,1,2,0:T(4,128)(2,1)S(1)}, u32[]{:S(2)}, u32[]{:S(2)}) %all-to-all-start.3) | async-done | bytes 131104 | tf_op jit(solution)/shard_map/all_to_all | solution.py:206
  134.5 4.8 %shard_map.102 = bf16[8,32,256]{2,1,0:T(8,128)(2,1)S(1)} custom-call(bf16[32,2048]{1,0:T(8,128)(2,1)S(1)} %bitcast.67, bf16[32,2048]{1,0:T(8,128)(2,1)S(1)} %bitcast.68, bf16[32,2048]{1,0:T(8,128)(2,1)S(1)} %bitcast.69, bf16[32,2048]{1,0:T(8,128)(2,1)S(1)} %bitcast.70, bf16[2048,2048]{1,0:T(8,128)(2,1)} %refs_7_.1, bf16[2048,2048]{1,0:T(8,128)(2,1)} %refs_7_.1, ...), custom_call_target="tpu_custom_call" | custom-call | flops 268435456 | bytes 8388608 | tf_op jit(solution)/shard_map/pallas_call | solution.py:69
  139.3 8.5 %all_to_all.30 = bf16[8,32,256]{2,1,0:T(8,128)(2,1)S(1)} all-to-all(bf16[8,32,256]{2,1,0:T(8,128)(2,1)S(1)} %shard_map.102), channel_id=1, replica_groups=mesh['grid'=32,'tile'=8] {'tile'}, dimensions={0} | all-to-all | bytes 262144 | tf_op jit(solution)/shard_map/all_to_all | solution.py:212
  148.0 21.9 %all_to_all.31 = bf16[32,32,256]{2,1,0:T(8,128)(2,1)} all-to-all(bf16[32,32,256]{2,1,0:T(8,128)(2,1)S(1)} %broadcast_in_dim.8), channel_id=1, replica_groups=mesh['grid'=32,'tile'=8] {'grid'}, dimensions={0} | all-to-all | bytes 1048576 | tf_op jit(solution)/shard_map/all_to_all | solution.py:34
  169.9 2.6 %shard_map.103 = bf16[256,512]{1,0:T(8,128)(2,1)} custom-call(bf16[1024,256]{1,0:T(8,128)(2,1)} %bitcast.71, bf16[1024,256]{1,0:T(8,128)(2,1)} %bitcast.72, bf16[1024,256]{1,0:T(8,128)(2,1)} %bitcast.73, bf16[1024,256]{1,0:T(8,128)(2,1)} %bitcast.74, bf16[1024,512]{1,0:T(8,128)(2,1)} %all-gather.2.cloned.1.call-done.refs_4_.refs_5_.refs_6_.refs_7_, ...), custom_call_target="tpu_custom_call" | custom-call | flops 268435456 | bytes 1572864 | tf_op jit(solution)/shard_map/pallas_call | solution.py:122
  (44 shorter events, 3.9 us)
Async XLA Ops:
  6.5 18.1 %copy-start = (bf16[512,2048]{1,0:T(8,128)(2,1)S(1)}, bf16[512,2048]{1,0:T(8,128)(2,1)}, u32[]{:S(2)}) copy-start(bf16[512,2048]{1,0:T(8,128)(2,1)} %param.12) | copy-start | bytes 6291460
  6.5 9.7 %copy-start.2 = (f32[3,16384]{1,0:T(4,128)S(1)}, f32[3,16384]{1,0:T(4,128)}, u32[]{:S(2)}) copy-start(f32[3,16384]{1,0:T(4,128)} %param.15) | copy-start | bytes 589828
  8.7 13.9 %all-to-all-start = ((bf16[4,32,2048]{2,1,0:T(8,128)(2,1)}), bf16[4,32,2048]{2,1,0:T(8,128)(2,1)S(1)}, u32[]{:S(2)}, u32[]{:S(2)}) async-start(bf16[4,32,2048]{2,1,0:T(8,128)(2,1)} %shard_map.100), calls=%async_computation | async-start | bytes 1048576 | tf_op jit(solution)/shard_map/all_to_all | solution.py:168
  14.7 1.6 collective-permute-start
  22.6 12.5 %collective-permute-start.2 = (bf16[4,32,2048]{2,1,0:T(8,128)(2,1)S(1)}, bf16[4,32,2048]{2,1,0:T(8,128)(2,1)}, u32[]{:S(2)}, u32[]{:S(2)}) collective-permute-start(bf16[4,32,2048]{2,1,0:T(8,128)(2,1)S(1)} %all-to-all-done), channel_id=1, source_target_pairs={{0,224},{8,232},{16,240},{24,248},{32,0},{40,8},{48,16},{56,24},{6... | collective-permute-start | bytes 1572872 | tf_op jit(solution)/shard_map/ppermute | solution.py:19
  22.7 17.5 %collective-permute-start.1 = (bf16[4,32,2048]{2,1,0:T(8,128)(2,1)S(1)}, bf16[4,32,2048]{2,1,0:T(8,128)(2,1)}, u32[]{:S(2)}, u32[]{:S(2)}) collective-permute-start(bf16[4,32,2048]{2,1,0:T(8,128)(2,1)S(1)} %all-to-all-done), channel_id=1, source_target_pairs={{0,32},{8,40},{16,48},{24,56},{32,64},{40,72},{48,80},{56,88},{64,... | collective-permute-start | bytes 1572872 | tf_op jit(solution)/shard_map/ppermute | solution.py:19
  35.1 12.3 %collective-permute-start.4 = (bf16[4,32,2048]{2,1,0:T(8,128)(2,1)}, bf16[4,32,2048]{2,1,0:T(8,128)(2,1)S(1)}, u32[]{:S(2)}, u32[]{:S(2)}) collective-permute-start(bf16[4,32,2048]{2,1,0:T(8,128)(2,1)} %collective-permute-done.2), channel_id=1, source_target_pairs={{0,224},{8,232},{16,240},{24,248},{32,0},{40,8},{48,16},{56,24},{6... | collective-permute-start | bytes 1572872 | tf_op jit(solution)/shard_map/ppermute | solution.py:19
  40.2 13.3 %collective-permute-start.3 = (bf16[4,32,2048]{2,1,0:T(8,128)(2,1)}, bf16[4,32,2048]{2,1,0:T(8,128)(2,1)S(1)}, u32[]{:S(2)}, u32[]{:S(2)}) collective-permute-start(bf16[4,32,2048]{2,1,0:T(8,128)(2,1)} %collective-permute-done.1), channel_id=1, source_target_pairs={{0,32},{8,40},{16,48},{24,56},{32,64},{40,72},{48,80},{56,88},{64,... | collective-permute-start | bytes 1572872 | tf_op jit(solution)/shard_map/ppermute | solution.py:19
  47.4 12.2 %collective-permute-start.6 = (bf16[4,32,2048]{2,1,0:T(8,128)(2,1)S(1)}, bf16[4,32,2048]{2,1,0:T(8,128)(2,1)S(1)}, u32[]{:S(2)}, u32[]{:S(2)}) collective-permute-start(bf16[4,32,2048]{2,1,0:T(8,128)(2,1)S(1)} %collective-permute-done.4), channel_id=1, source_target_pairs={{0,224},{8,232},{16,240},{24,248},{32,0},{40,8},{48,16},{56,24},{6... | collective-permute-start | bytes 1572872 | tf_op jit(solution)/shard_map/ppermute | solution.py:19
  53.5 11.3 %collective-permute-start.5 = (bf16[4,32,2048]{2,1,0:T(8,128)(2,1)S(1)}, bf16[4,32,2048]{2,1,0:T(8,128)(2,1)S(1)}, u32[]{:S(2)}, u32[]{:S(2)}) collective-permute-start(bf16[4,32,2048]{2,1,0:T(8,128)(2,1)S(1)} %collective-permute-done.3), channel_id=1, source_target_pairs={{0,32},{8,40},{16,48},{24,56},{32,64},{40,72},{48,80},{56,88},{64,... | collective-permute-start | bytes 1572872 | tf_op jit(solution)/shard_map/ppermute | solution.py:19
  59.6 13.6 %collective-permute-start.8 = (bf16[3,32,2048]{2,1,0:T(8,128)(2,1)S(1)}, bf16[3,32,2048]{2,1,0:T(8,128)(2,1)S(1)}, u32[]{:S(2)}, u32[]{:S(2)}) collective-permute-start(bf16[3,32,2048]{2,1,0:T(8,128)(2,1)S(1)} %slice.25), channel_id=1, source_target_pairs={{0,224},{8,232},{16,240},{24,248},{32,0},{40,8},{48,16},{56,24},{6... | collective-permute-start | bytes 1179656 | tf_op jit(solution)/shard_map/ppermute | solution.py:19
  65.6 6.2 %collective-permute-start.7 = (bf16[1,32,2048]{2,1,0:T(8,128)(2,1)S(1)}, bf16[1,32,2048]{2,1,0:T(8,128)(2,1)S(1)}, u32[]{:S(2)}, u32[]{:S(2)}) collective-permute-start(bf16[1,32,2048]{2,1,0:T(8,128)(2,1)S(1)} %slice.24), channel_id=1, source_target_pairs={{0,32},{8,40},{16,48},{24,56},{32,64},{40,72},{48,80},{56,88},{64,... | collective-permute-start | bytes 393224 | tf_op jit(solution)/shard_map/ppermute | solution.py:19
  74.6 24.0 %all-to-all-start.1 = ((bf16[8,8,16,512]{3,2,1,0:T(8,128)(2,1)}), bf16[8,8,16,512]{3,2,1,0:T(8,128)(2,1)S(1)}, u32[]{:S(2)}, u32[]{:S(2)}) async-start(bf16[8,8,16,512]{3,2,1,0:T(8,128)(2,1)} %constant_dynamic-update-slice_fusion), calls=%async_computation.1 | async-start | bytes 2097152 | tf_op jit(solution)/shard_map/all_to_all | solution.py:196
  80.5 67.4 %all-gather.2.cloned.1.call-start = ((), (), s32[]{:S(2)}) async-start(), calls=%async_computation.6 | async-start | bytes 1179648 | tf_op jit(solution)/shard_map/all_gather | solution.py:199
  80.5 21.0 %collective-permute-start.9 = (bf16[128,512]{1,0:T(8,128)(2,1)S(1)}, bf16[128,512]{1,0:T(8,128)(2,1)}, u32[]{:S(2)}, u32[]{:S(2)}) collective-permute-start(bf16[128,512]{1,0:T(8,128)(2,1)S(1)} %reshape.121), channel_id=1, source_target_pairs={{0,0},{1,32},{2,64},{3,96},{4,128},{5,160},{6,192},{7,224},{8,8},{... | collective-permute-start | bytes 393224 | tf_op jit(solution)/shard_map/ppermute | solution.py:29
  98.6 1.0 copy-start.1
  99.5 23.2 %copy-start.3 = (s32[32,32]{1,0:T(8,128)S(1)}, s32[32,32]{1,0:T(8,128)}, u32[]{:S(2)}) copy-start(s32[32,32]{1,0:T(8,128)} %param.14) | copy-start | bytes 12292
  101.6 21.1 %all-to-all-start.2 = ((bf16[32,4,512]{2,1,0:T(4,128)(2,1)}), bf16[32,4,512]{2,1,0:T(4,128)(2,1)S(1)}, u32[]{:S(2)}, u32[]{:S(2)}) async-start(bf16[32,4,512]{2,1,0:T(4,128)(2,1)} %shard_map.101), calls=%async_computation.2 | async-start | bytes 262144 | tf_op jit(solution)/shard_map/all_to_all | solution.py:200
  125.0 9.4 %all-to-all-start.3 = ((bf16[8,4,4,512]{3,1,2,0:T(4,128)(2,1)}), bf16[8,4,4,512]{3,1,2,0:T(4,128)(2,1)S(1)}, u32[]{:S(2)}, u32[]{:S(2)}) async-start(bf16[8,4,4,512]{3,1,2,0:T(4,128)(2,1)} %copy.20), calls=%async_computation.3 | async-start | bytes 262144 | tf_op jit(solution)/shard_map/all_to_all | solution.py:206
Sparse Core Ops, SparseCore 0:
  101.7 26.1 all-gather.1

commit v10 on v7

--- a/solution.py
+++ b/solution.py
@@ -82,25 +82,26 @@
     )(*[pot] * blocks, *[lmo] * blocks, keep)
 
 
-def place_kernel(z, parts, out):
+def place_kernel(parts, out):
+    z = lax.axis_index("grid") // NY
     for m in range(NZ):
         total = jnp.sum(parts[:, m].astype(f32), axis=0)
-        first = (z[0] + m) % NZ * NY
+        first = (z + m) % NZ * NY
         for q in range(NY):
             out[pl.ds(first + q, 1)] = total[q * QP : (q + 1) * QP].astype(out.dtype)[None]
 
 
-def sum_and_place(z, parts):
+def sum_and_place(parts):
     whole = pl.BlockSpec(memory_space=pltpu.VMEM)
     return pl.pallas_call(
         place_kernel,
-        in_specs=[pl.BlockSpec(memory_space=pltpu.SMEM), whole],
+        in_specs=[whole],
         out_specs=whole,
         out_shape=jax.ShapeDtypeStruct((NZ * NY, QP, BLK), bf16),
         cost_estimate=pl.CostEstimate(
             flops=parts.size, bytes_accessed=2 * parts.size, transcendentals=0
         ),
-    )(z.reshape(1), parts)
+    )(parts)
 
 
 def mask_kernel(sig, pv, out):
@@ -166,7 +167,7 @@
     parts, coef, piece = tie((parts, coef, piece))
     piece = permute_all(piece, lambda a, b, c: (c, b, a))
     parts = lax.all_to_all(parts, "tile", 0, 0, tiled=True)
-    term = sum_and_place(z, parts)
+    term = sum_and_place(parts)
     term, piece = tie((term, piece))
     x_col = lax.all_gather(piece, "tile", axis=0, tiled=True)
     term = lax.all_to_all(term, "grid", 0, 0, tiled=True)

time: 180 us -> 180 us (level)
  no operation moved by 1% of the time
where the time goes in v10:
time: 180 us; the launch traced here: 179 us
  waiting for transfers between devices  55.9 us (31%)
  starting transfers between devices  44.2 us (25%)
  blocking collectives  29.8 us (17%)
  between operations  13.7 us (8%)
  matrix products  13.3 us (7%)
  local copies, waits for them, and re-layouts  10.4 us (6%)
  Pallas kernels  8.97 us (5%)
  other arithmetic  2.39 us (1%)
    ppermute x8, waiting for transfers between devices, along_z(): return lax.ppermute(x, 'grid', pairs)  22.2 us
    all_to_all x1, blocking collectives, spread(): return lax.all_to_all(copies, axis, 0, 0, tiled=True)  21.3 us
    ppermute x8, starting transfers between devices, along_z(): return lax.ppermute(x, 'grid', pairs)  12.9 us
    all_to_all x1, waiting for transfers between devices, shards(): parts = lax.all_to_all(parts, 'tile', 0, 0, tiled=True)  12.8 us
    dot_general x10, matrix products, dot(): lax.dot_general(u, v, (((cu,), (cv,)), ((), ())), preferred_element_type=...  11.8 us
    all_to_all x1, starting transfers between devices, shards(): term = lax.all_to_all(term, 'grid', 0, 0, tiled=True)  11.5 us
    all_to_all x1, waiting for transfers between devices, shards(): term = lax.all_to_all(term, 'grid', 0, 0, tiled=True)  8.63 us
    all_to_all x1, blocking collectives, shards(): w = lax.all_to_all(w, 'tile', 0, 0, tiled=True)  8.52 us
  transfers between devices with their start and end apart: 15, of which 10 were waited for; matrix products, arithmetic and copies ran while one was open for 12% of the time, Pallas kernels for 4%

profile of v10, /device:TPU:32, one launch (start us, length us, event | category | flops | bytes accessed | tf_op | source)
XLA Modules:
  0.0 178.6 jit_solution(8727735819748226562)
XLA Ops:
  6.5 2.1 %shard_map.100 = bf16[4,32,2048]{2,1,0:T(8,128)(2,1)} custom-call(s32[1,16]{1,0:T(1,128)} %sig.1, bf16[32,2048]{1,0:T(8,128)(2,1)} %pv.1), custom_call_target="tpu_custom_call" | custom-call | flops 65536 | bytes 655360 | tf_op jit(solution)/shard_map/pallas_call | solution.py:121
  8.7 4.5 %all-to-all-start = ((bf16[4,32,2048]{2,1,0:T(8,128)(2,1)}), bf16[4,32,2048]{2,1,0:T(8,128)(2,1)S(1)}, u32[]{:S(2)}, u32[]{:S(2)}) async-start(bf16[4,32,2048]{2,1,0:T(8,128)(2,1)} %shard_map.100), calls=%async_computation | async-start | bytes 1048576 | tf_op jit(solution)/shard_map/all_to_all | solution.py:141
  13.1 0.8 reshape.97
  13.9 0.7 fusion.13
  15.4 0.9 add.42
  16.4 6.2 %all-to-all-done = bf16[4,32,2048]{2,1,0:T(8,128)(2,1)S(1)} async-done(((bf16[4,32,2048]{2,1,0:T(8,128)(2,1)}), bf16[4,32,2048]{2,1,0:T(8,128)(2,1)S(1)}, u32[]{:S(2)}, u32[]{:S(2)}) %all-to-all-start) | async-done | bytes 524320 | tf_op jit(solution)/shard_map/all_to_all | solution.py:141
  22.7 1.9 %collective-permute-start.1 = (bf16[4,32,2048]{2,1,0:T(8,128)(2,1)S(1)}, bf16[4,32,2048]{2,1,0:T(8,128)(2,1)}, u32[]{:S(2)}, u32[]{:S(2)}) collective-permute-start(bf16[4,32,2048]{2,1,0:T(8,128)(2,1)S(1)} %all-to-all-done), channel_id=1, source_target_pairs={{0,32},{8,40},{16,48},{24,56},{32,64},{40,72},{48,80},{56,88},{64,... | collective-permute-start | bytes 1572872 | tf_op jit(solution)/shard_map/ppermute | solution.py:19
  24.6 0.8 convolution_convert_fusion.7
  25.8 1.1 dynamic_update_slice.27
  27.3 7.7 %collective-permute-done.2 = bf16[4,32,2048]{2,1,0:T(8,128)(2,1)} collective-permute-done((bf16[4,32,2048]{2,1,0:T(8,128)(2,1)S(1)}, bf16[4,32,2048]{2,1,0:T(8,128)(2,1)}, u32[]{:S(2)}, u32[]{:S(2)}) %collective-permute-start.2) | collective-permute-done | bytes 524320 | tf_op jit(solution)/shard_map/ppermute | solution.py:19
  35.1 3.2 %collective-permute-start.4 = (bf16[4,32,2048]{2,1,0:T(8,128)(2,1)}, bf16[4,32,2048]{2,1,0:T(8,128)(2,1)S(1)}, u32[]{:S(2)}, u32[]{:S(2)}) collective-permute-start(bf16[4,32,2048]{2,1,0:T(8,128)(2,1)} %collective-permute-done.2), channel_id=1, source_target_pairs={{0,224},{8,232},{16,240},{24,248},{32,0},{40,8},{48,16},{56,24},{6... | collective-permute-start | bytes 1572872 | tf_op jit(solution)/shard_map/ppermute | solution.py:19
  38.3 1.9 %convolution_convert_fusion.5 = bf16[128,512]{1,0:T(8,128)(2,1)S(1)} fusion(bf16[128,2048]{1,0:T(8,128)(2,1)} %bitcast.7, bf16[512,2048]{1,0:T(8,128)(2,1)S(1)} %copy-done), kind=kOutput, calls=%fused_computation.5 | convolution fusion | flops 268500992 | bytes 2752512 | tf_op jit(solution)/shard_map/dot_general | solution.py:38
  40.3 1.9 %convolution_convert_fusion.6 = bf16[128,512]{1,0:T(8,128)(2,1)S(1)} fusion(bf16[128,2048]{1,0:T(8,128)(2,1)} %bitcast.5, bf16[512,2048]{1,0:T(8,128)(2,1)S(1)} %copy-done), kind=kOutput, calls=%fused_computation.6 | convolution fusion | flops 268500992 | bytes 2752512 | tf_op jit(solution)/shard_map/dot_general | solution.py:38
  42.2 0.7 constant_dynamic-update-slice_fusion.7
  42.9 0.7 constant_dynamic-update-slice_fusion.6
  43.5 3.8 %collective-permute-done.4 = bf16[4,32,2048]{2,1,0:T(8,128)(2,1)S(1)} collective-permute-done((bf16[4,32,2048]{2,1,0:T(8,128)(2,1)}, bf16[4,32,2048]{2,1,0:T(8,128)(2,1)S(1)}, u32[]{:S(2)}, u32[]{:S(2)}) %collective-permute-start.4) | collective-permute-done | bytes 524320 | tf_op jit(solution)/shard_map/ppermute | solution.py:19
  47.4 3.8 %collective-permute-start.6 = (bf16[4,32,2048]{2,1,0:T(8,128)(2,1)S(1)}, bf16[4,32,2048]{2,1,0:T(8,128)(2,1)S(1)}, u32[]{:S(2)}, u32[]{:S(2)}) collective-permute-start(bf16[4,32,2048]{2,1,0:T(8,128)(2,1)S(1)} %collective-permute-done.4), channel_id=1, source_target_pairs={{0,224},{8,232},{16,240},{24,248},{32,0},{40,8},{48,16},{56,24},{6... | collective-permute-start | bytes 1572872 | tf_op jit(solution)/shard_map/ppermute | solution.py:19
  51.2 0.8 convolution_convert_fusion.3
  52.0 1.5 collective-permute-done.3
  53.5 0.8 convolution_convert_fusion.4
  54.3 0.7 constant_dynamic-update-slice_fusion.5
  55.0 0.7 constant_dynamic-update-slice_fusion.4
  55.7 3.8 %collective-permute-done.6 = bf16[4,32,2048]{2,1,0:T(8,128)(2,1)S(1)} collective-permute-done((bf16[4,32,2048]{2,1,0:T(8,128)(2,1)S(1)}, bf16[4,32,2048]{2,1,0:T(8,128)(2,1)S(1)}, u32[]{:S(2)}, u32[]{:S(2)}) %collective-permute-start.6) | collective-permute-done | bytes 524320 | tf_op jit(solution)/shard_map/ppermute | solution.py:19
  59.6 3.6 %collective-permute-start.8 = (bf16[3,32,2048]{2,1,0:T(8,128)(2,1)S(1)}, bf16[3,32,2048]{2,1,0:T(8,128)(2,1)S(1)}, u32[]{:S(2)}, u32[]{:S(2)}) collective-permute-start(bf16[3,32,2048]{2,1,0:T(8,128)(2,1)S(1)} %slice.25), channel_id=1, source_target_pairs={{0,224},{8,232},{16,240},{24,248},{32,0},{40,8},{48,16},{56,24},{6... | collective-permute-start | bytes 1179656 | tf_op jit(solution)/shard_map/ppermute | solution.py:19
  63.1 0.8 convolution_convert_fusion.1
  64.0 0.8 collective-permute-done.5
  64.8 0.8 convolution_convert_fusion.2
  65.9 0.7 constant_dynamic-update-slice_fusion.3
  66.6 0.7 constant_dynamic-update-slice_fusion.2
  67.2 4.5 %collective-permute-done.7 = bf16[1,32,2048]{2,1,0:T(8,128)(2,1)S(1)} collective-permute-done((bf16[1,32,2048]{2,1,0:T(8,128)(2,1)S(1)}, bf16[1,32,2048]{2,1,0:T(8,128)(2,1)S(1)}, u32[]{:S(2)}, u32[]{:S(2)}) %collective-permute-start.7) | collective-permute-done | bytes 131104 | tf_op jit(solution)/shard_map/ppermute | solution.py:19
  71.8 0.7 convolution_convert_fusion.10
  73.1 0.8 convolution_convert_fusion.9
  74.6 6.1 %all-to-all-start.1 = ((bf16[8,8,16,512]{3,2,1,0:T(8,128)(2,1)}), bf16[8,8,16,512]{3,2,1,0:T(8,128)(2,1)S(1)}, u32[]{:S(2)}, u32[]{:S(2)}) async-start(bf16[8,8,16,512]{3,2,1,0:T(8,128)(2,1)} %constant_dynamic-update-slice_fusion), calls=%async_computation.1 | async-start | bytes 2097152 | tf_op jit(solution)/shard_map/all_to_all | solution.py:169
  80.7 5.2 %collective-permute-start.9 = (bf16[128,512]{1,0:T(8,128)(2,1)S(1)}, bf16[128,512]{1,0:T(8,128)(2,1)}, u32[]{:S(2)}, u32[]{:S(2)}) collective-permute-start(bf16[128,512]{1,0:T(8,128)(2,1)S(1)} %reshape.118), channel_id=1, source_target_pairs={{0,0},{1,32},{2,64},{3,96},{4,128},{5,160},{6,192},{7,224},{8,8},{... | collective-permute-start | bytes 393224 | tf_op jit(solution)/shard_map/ppermute | solution.py:29
  85.9 12.8 %all-to-all-done.1.parts = bf16[8,8,16,512]{3,2,1,0:T(8,128)(2,1)S(1)} async-done(((bf16[8,8,16,512]{3,2,1,0:T(8,128)(2,1)}), bf16[8,8,16,512]{3,2,1,0:T(8,128)(2,1)S(1)}, u32[]{:S(2)}, u32[]{:S(2)}) %all-to-all-start.1) | async-done | bytes 1048608 | tf_op jit(solution)/shard_map/all_to_all | solution.py:169
  98.7 1.0 copy-done.1
  99.7 2.0 %shard_map.101 = bf16[32,4,512]{2,1,0:T(4,128)(2,1)} custom-call(bf16[8,8,16,512]{3,2,1,0:T(8,128)(2,1)} %copy-done.1), custom_call_target="tpu_custom_call" | custom-call | flops 524288 | bytes 1048576 | tf_op jit(solution)/shard_map/pallas_call | solution.py:96
  101.7 11.5 %all-to-all-start.2 = ((bf16[32,4,512]{2,1,0:T(4,128)(2,1)}), bf16[32,4,512]{2,1,0:T(4,128)(2,1)S(1)}, u32[]{:S(2)}, u32[]{:S(2)}) async-start(bf16[32,4,512]{2,1,0:T(4,128)(2,1)} %shard_map.101), calls=%async_computation.2 | async-start | bytes 262144 | tf_op jit(solution)/shard_map/all_to_all | solution.py:173
  113.2 0.9 compare_reduce_fusion
  114.1 8.6 %all-to-all-done.2 = bf16[32,4,512]{2,1,0:T(4,128)(2,1)S(1)} async-done(((bf16[32,4,512]{2,1,0:T(4,128)(2,1)}), bf16[32,4,512]{2,1,0:T(4,128)(2,1)S(1)}, u32[]{:S(2)}, u32[]{:S(2)}) %all-to-all-start.2) | async-done | bytes 131104 | tf_op jit(solution)/shard_map/all_to_all | solution.py:173
  122.9 1.4 fusion.1
  124.5 0.7 copy.23
  125.2 3.4 %all-to-all-start.3 = ((bf16[8,4,4,512]{3,1,2,0:T(4,128)(2,1)}), bf16[8,4,4,512]{3,1,2,0:T(4,128)(2,1)S(1)}, u32[]{:S(2)}, u32[]{:S(2)}) async-start(bf16[8,4,4,512]{3,1,2,0:T(4,128)(2,1)} %copy.23), calls=%async_computation.3 | async-start | bytes 262144 | tf_op jit(solution)/shard_map/all_to_all | solution.py:179
  128.7 5.9 %all-to-all-done.3 = bf16[8,4,4,512]{3,1,2,0:T(4,128)(2,1)S(1)} async-done(((bf16[8,4,4,512]{3,1,2,0:T(4,128)(2,1)}), bf16[8,4,4,512]{3,1,2,0:T(4,128)(2,1)S(1)}, u32[]{:S(2)}, u32[]{:S(2)}) %all-to-all-start.3) | async-done | bytes 131104 | tf_op jit(solution)/shard_map/all_to_all | solution.py:179
  134.7 4.8 %shard_map.102 = bf16[8,32,256]{2,1,0:T(8,128)(2,1)S(1)} custom-call(bf16[32,2048]{1,0:T(8,128)(2,1)S(1)} %bitcast.68, bf16[32,2048]{1,0:T(8,128)(2,1)S(1)} %bitcast.69, bf16[32,2048]{1,0:T(8,128)(2,1)S(1)} %bitcast.70, bf16[32,2048]{1,0:T(8,128)(2,1)S(1)} %bitcast.71, bf16[2048,2048]{1,0:T(8,128)(2,1)} %refs_7_.1, bf16[2048,2048]{1,0:T(8,128)(2,1)} %refs_7_.1, ...), custom_call_target="tpu_custom_call" | custom-call | flops 268435456 | bytes 8388608 | tf_op jit(solution)/shard_map/pallas_call | solution.py:69
  139.5 8.5 %all_to_all.30 = bf16[8,32,256]{2,1,0:T(8,128)(2,1)S(1)} all-to-all(bf16[8,32,256]{2,1,0:T(8,128)(2,1)S(1)} %shard_map.102), channel_id=1, replica_groups=mesh['grid'=32,'tile'=8] {'tile'}, dimensions={0} | all-to-all | bytes 262144 | tf_op jit(solution)/shard_map/all_to_all | solution.py:185
  148.1 21.3 %all_to_all.31 = bf16[32,32,256]{2,1,0:T(8,128)(2,1)S(1)} all-to-all(bf16[32,32,256]{2,1,0:T(8,128)(2,1)S(1)} %broadcast_in_dim.8), channel_id=1, replica_groups=mesh['grid'=32,'tile'=8] {'grid'}, dimensions={0} | all-to-all | bytes 1048576 | tf_op jit(solution)/shard_map/all_to_all | solution.py:34
  169.4 2.4 %convolution_convert_fusion = bf16[256,512]{1,0:T(8,128)(2,1)} fusion(bf16[1024,256]{1,0:T(8,128)(2,1)S(1)} %bitcast.77, bf16[1024,512]{1,0:T(8,128)(2,1)} %all-gather.2.cloned.1.call-done), kind=kOutput, calls=%fused_computation | convolution fusion | flops 268566528 | bytes 1835008 | tf_op jit(solution)/shard_map/dot_general | solution.py:38
  (44 shorter events, 3.9 us)
Async XLA Ops:
  6.5 18.1 %copy-start = (bf16[512,2048]{1,0:T(8,128)(2,1)S(1)}, bf16[512,2048]{1,0:T(8,128)(2,1)}, u32[]{:S(2)}) copy-start(bf16[512,2048]{1,0:T(8,128)(2,1)} %param.12) | copy-start | bytes 6291460
  6.5 9.7 %copy-start.2 = (f32[3,16384]{1,0:T(4,128)S(1)}, f32[3,16384]{1,0:T(4,128)}, u32[]{:S(2)}) copy-start(f32[3,16384]{1,0:T(4,128)} %param.15) | copy-start | bytes 589828
  8.7 13.9 %all-to-all-start = ((bf16[4,32,2048]{2,1,0:T(8,128)(2,1)}), bf16[4,32,2048]{2,1,0:T(8,128)(2,1)S(1)}, u32[]{:S(2)}, u32[]{:S(2)}) async-start(bf16[4,32,2048]{2,1,0:T(8,128)(2,1)} %shard_map.100), calls=%async_computation | async-start | bytes 1048576 | tf_op jit(solution)/shard_map/all_to_all | solution.py:141
  14.7 1.6 collective-permute-start
  22.6 12.5 %collective-permute-start.2 = (bf16[4,32,2048]{2,1,0:T(8,128)(2,1)S(1)}, bf16[4,32,2048]{2,1,0:T(8,128)(2,1)}, u32[]{:S(2)}, u32[]{:S(2)}) collective-permute-start(bf16[4,32,2048]{2,1,0:T(8,128)(2,1)S(1)} %all-to-all-done), channel_id=1, source_target_pairs={{0,224},{8,232},{16,240},{24,248},{32,0},{40,8},{48,16},{56,24},{6... | collective-permute-start | bytes 1572872 | tf_op jit(solution)/shard_map/ppermute | solution.py:19
  22.7 17.5 %collective-permute-start.1 = (bf16[4,32,2048]{2,1,0:T(8,128)(2,1)S(1)}, bf16[4,32,2048]{2,1,0:T(8,128)(2,1)}, u32[]{:S(2)}, u32[]{:S(2)}) collective-permute-start(bf16[4,32,2048]{2,1,0:T(8,128)(2,1)S(1)} %all-to-all-done), channel_id=1, source_target_pairs={{0,32},{8,40},{16,48},{24,56},{32,64},{40,72},{48,80},{56,88},{64,... | collective-permute-start | bytes 1572872 | tf_op jit(solution)/shard_map/ppermute | solution.py:19
  35.1 12.3 %collective-permute-start.4 = (bf16[4,32,2048]{2,1,0:T(8,128)(2,1)}, bf16[4,32,2048]{2,1,0:T(8,128)(2,1)S(1)}, u32[]{:S(2)}, u32[]{:S(2)}) collective-permute-start(bf16[4,32,2048]{2,1,0:T(8,128)(2,1)} %collective-permute-done.2), channel_id=1, source_target_pairs={{0,224},{8,232},{16,240},{24,248},{32,0},{40,8},{48,16},{56,24},{6... | collective-permute-start | bytes 1572872 | tf_op jit(solution)/shard_map/ppermute | solution.py:19
  40.2 13.3 %collective-permute-start.3 = (bf16[4,32,2048]{2,1,0:T(8,128)(2,1)}, bf16[4,32,2048]{2,1,0:T(8,128)(2,1)S(1)}, u32[]{:S(2)}, u32[]{:S(2)}) collective-permute-start(bf16[4,32,2048]{2,1,0:T(8,128)(2,1)} %collective-permute-done.1), channel_id=1, source_target_pairs={{0,32},{8,40},{16,48},{24,56},{32,64},{40,72},{48,80},{56,88},{64,... | collective-permute-start | bytes 1572872 | tf_op jit(solution)/shard_map/ppermute | solution.py:19
  47.4 12.2 %collective-permute-start.6 = (bf16[4,32,2048]{2,1,0:T(8,128)(2,1)S(1)}, bf16[4,32,2048]{2,1,0:T(8,128)(2,1)S(1)}, u32[]{:S(2)}, u32[]{:S(2)}) collective-permute-start(bf16[4,32,2048]{2,1,0:T(8,128)(2,1)S(1)} %collective-permute-done.4), channel_id=1, source_target_pairs={{0,224},{8,232},{16,240},{24,248},{32,0},{40,8},{48,16},{56,24},{6... | collective-permute-start | bytes 1572872 | tf_op jit(solution)/shard_map/ppermute | solution.py:19
  53.5 11.3 %collective-permute-start.5 = (bf16[4,32,2048]{2,1,0:T(8,128)(2,1)S(1)}, bf16[4,32,2048]{2,1,0:T(8,128)(2,1)S(1)}, u32[]{:S(2)}, u32[]{:S(2)}) collective-permute-start(bf16[4,32,2048]{2,1,0:T(8,128)(2,1)S(1)} %collective-permute-done.3), channel_id=1, source_target_pairs={{0,32},{8,40},{16,48},{24,56},{32,64},{40,72},{48,80},{56,88},{64,... | collective-permute-start | bytes 1572872 | tf_op jit(solution)/shard_map/ppermute | solution.py:19
  59.6 13.6 %collective-permute-start.8 = (bf16[3,32,2048]{2,1,0:T(8,128)(2,1)S(1)}, bf16[3,32,2048]{2,1,0:T(8,128)(2,1)S(1)}, u32[]{:S(2)}, u32[]{:S(2)}) collective-permute-start(bf16[3,32,2048]{2,1,0:T(8,128)(2,1)S(1)} %slice.25), channel_id=1, source_target_pairs={{0,224},{8,232},{16,240},{24,248},{32,0},{40,8},{48,16},{56,24},{6... | collective-permute-start | bytes 1179656 | tf_op jit(solution)/shard_map/ppermute | solution.py:19
  65.6 6.2 %collective-permute-start.7 = (bf16[1,32,2048]{2,1,0:T(8,128)(2,1)S(1)}, bf16[1,32,2048]{2,1,0:T(8,128)(2,1)S(1)}, u32[]{:S(2)}, u32[]{:S(2)}) collective-permute-start(bf16[1,32,2048]{2,1,0:T(8,128)(2,1)S(1)} %slice.24), channel_id=1, source_target_pairs={{0,32},{8,40},{16,48},{24,56},{32,64},{40,72},{48,80},{56,88},{64,... | collective-permute-start | bytes 393224 | tf_op jit(solution)/shard_map/ppermute | solution.py:19
  74.6 48.3 %copy-start.3 = (s32[32,32]{1,0:T(8,128)S(1)}, s32[32,32]{1,0:T(8,128)}, u32[]{:S(2)}) copy-start(s32[32,32]{1,0:T(8,128)} %param.14) | copy-start | bytes 12292
  74.6 24.1 %all-to-all-start.1 = ((bf16[8,8,16,512]{3,2,1,0:T(8,128)(2,1)}), bf16[8,8,16,512]{3,2,1,0:T(8,128)(2,1)S(1)}, u32[]{:S(2)}, u32[]{:S(2)}) async-start(bf16[8,8,16,512]{3,2,1,0:T(8,128)(2,1)} %constant_dynamic-update-slice_fusion), calls=%async_computation.1 | async-start | bytes 2097152 | tf_op jit(solution)/shard_map/all_to_all | solution.py:169
  80.6 67.4 %all-gather.2.cloned.1.call-start = ((), (), s32[]{:S(2)}) async-start(), calls=%async_computation.6 | async-start | bytes 1179648 | tf_op jit(solution)/shard_map/all_gather | solution.py:172
  80.7 21.0 %collective-permute-start.9 = (bf16[128,512]{1,0:T(8,128)(2,1)S(1)}, bf16[128,512]{1,0:T(8,128)(2,1)}, u32[]{:S(2)}, u32[]{:S(2)}) collective-permute-start(bf16[128,512]{1,0:T(8,128)(2,1)S(1)} %reshape.118), channel_id=1, source_target_pairs={{0,0},{1,32},{2,64},{3,96},{4,128},{5,160},{6,192},{7,224},{8,8},{... | collective-permute-start | bytes 393224 | tf_op jit(solution)/shard_map/ppermute | solution.py:29
  98.7 1.0 copy-start.1
  101.7 21.1 %all-to-all-start.2 = ((bf16[32,4,512]{2,1,0:T(4,128)(2,1)}), bf16[32,4,512]{2,1,0:T(4,128)(2,1)S(1)}, u32[]{:S(2)}, u32[]{:S(2)}) async-start(bf16[32,4,512]{2,1,0:T(4,128)(2,1)} %shard_map.101), calls=%async_computation.2 | async-start | bytes 262144 | tf_op jit(solution)/shard_map/all_to_all | solution.py:173
  125.2 9.4 %all-to-all-start.3 = ((bf16[8,4,4,512]{3,1,2,0:T(4,128)(2,1)}), bf16[8,4,4,512]{3,1,2,0:T(4,128)(2,1)S(1)}, u32[]{:S(2)}, u32[]{:S(2)}) async-start(bf16[8,4,4,512]{3,1,2,0:T(4,128)(2,1)} %copy.23), calls=%async_computation.3 | async-start | bytes 262144 | tf_op jit(solution)/shard_map/all_to_all | solution.py:179
Sparse Core Ops, SparseCore 0:
  101.8 26.1 all-gather.1

commit v11 on v10

--- a/solution.py
+++ b/solution.py
@@ -165,10 +165,10 @@
     coef = 1.0 / jnp.sqrt(jnp.sum(off * off, axis=0) + widths.reshape(nblk, 1, BLK))
     coef = coef * named[:, None, None]
     parts, coef, piece = tie((parts, coef, piece))
-    piece = permute_all(piece, lambda a, b, c: (c, b, a))
     parts = lax.all_to_all(parts, "tile", 0, 0, tiled=True)
     term = sum_and_place(parts)
     term, piece = tie((term, piece))
+    piece = permute_all(piece, lambda a, b, c: (c, b, a))
     x_col = lax.all_gather(piece, "tile", axis=0, tiled=True)
     term = lax.all_to_all(term, "grid", 0, 0, tiled=True)
 

time: 180 us -> 186 us (1.033)
  blocking collectives: 29.8 us -> 52 us
  local copies, waits for them, and re-layouts: 10.4 us -> 3.86 us
  starting transfers between devices: 44.2 us -> 40.2 us
  waiting for transfers between devices: 55.9 us -> 52.7 us
    all_to_all x0 -> x1, blocking collectives: none -> 22.1 us  [shards(): parts = lax.all_to_all(parts, 'tile', 0, 0, tiled=True)]
    all_to_all x1 -> x0, waiting for transfers between devices: 12.8 us -> none  [shards(): parts = lax.all_to_all(parts, 'tile', 0, 0, tiled=True)]
    dynamic_update_slice x9, local copies, waits for them, and re-layouts: 6.44 us -> 0.21 us  [product(): lax.dynamic_update_slice(buf, rows.reshape(-1, 1, 16, BLK), (row, slot, 0...]
    all_to_all x1 -> x0, starting transfers between devices: 6.05 us -> none  [shards(): parts = lax.all_to_all(parts, 'tile', 0, 0, tiled=True)]
    ppermute x8, waiting for transfers between devices: 22.2 us -> 27.2 us  [along_z(): return lax.ppermute(x, 'grid', pairs)]
    ppermute x2, waiting for transfers between devices: 0.01 us -> 4.04 us  [permute_all(): return lax.ppermute(x, ('grid', 'tile'), pairs)]
    all_to_all x1, starting transfers between devices: 11.5 us -> 14.6 us  [shards(): term = lax.all_to_all(term, 'grid', 0, 0, tiled=True)]
  transfers between devices with their start and end apart: 15 -> 14, of which waited for: 10 -> 10; matrix products, arithmetic and copies ran while one was open for 12% -> 7% of each run, Pallas kernels for 4% -> 3%
where the time goes in v11:
time: 186 us; the launch traced here: 185 us
  waiting for transfers between devices  52.7 us (28%)
  blocking collectives  52 us (28%)
  starting transfers between devices  40.2 us (22%)
  between operations  13.8 us (7%)
  matrix products  12.2 us (7%)
  Pallas kernels  8.97 us (5%)
  local copies, waits for them, and re-layouts  3.86 us (2%)
    ppermute x8, waiting for transfers between devices, along_z(): return lax.ppermute(x, 'grid', pairs)  27.2 us
    all_to_all x1, blocking collectives, shards(): parts = lax.all_to_all(parts, 'tile', 0, 0, tiled=True)  22.1 us
    all_to_all x1, blocking collectives, spread(): return lax.all_to_all(copies, axis, 0, 0, tiled=True)  21.4 us
    all_to_all x1, starting transfers between devices, shards(): term = lax.all_to_all(term, 'grid', 0, 0, tiled=True)  14.6 us
    ppermute x8, starting transfers between devices, along_z(): return lax.ppermute(x, 'grid', pairs)  12.9 us
    dot_general x10, matrix products, dot(): lax.dot_general(u, v, (((cu,), (cv,)), ((), ())), preferred_element_type=...  11.8 us
    all_to_all x1, waiting for transfers between devices, shards(): term = lax.all_to_all(term, 'grid', 0, 0, tiled=True)  9.31 us
    all_to_all x1, blocking collectives, shards(): w = lax.all_to_all(w, 'tile', 0, 0, tiled=True)  8.52 us
  transfers between devices with their start and end apart: 14, of which 10 were waited for; matrix products, arithmetic and copies ran while one was open for 7% of the time, Pallas kernels for 3%

profile of v11, /device:TPU:32, one launch (start us, length us, event | category | flops | bytes accessed | tf_op | source)
XLA Modules:
  0.0 185.5 jit_solution(13107974160353207010)
XLA Ops:
  6.5 2.1 %shard_map.100 = bf16[4,32,2048]{2,1,0:T(8,128)(2,1)} custom-call(s32[1,16]{1,0:T(1,128)} %sig.1, bf16[32,2048]{1,0:T(8,128)(2,1)} %pv.1), custom_call_target="tpu_custom_call" | custom-call | flops 65536 | bytes 655360 | tf_op jit(solution)/shard_map/pallas_call | solution.py:121
  8.7 4.5 %all-to-all-start = ((bf16[4,32,2048]{2,1,0:T(8,128)(2,1)}), bf16[4,32,2048]{2,1,0:T(8,128)(2,1)S(1)}, u32[]{:S(2)}, u32[]{:S(2)}) async-start(bf16[4,32,2048]{2,1,0:T(8,128)(2,1)} %shard_map.100), calls=%async_computation | async-start | bytes 1048576 | tf_op jit(solution)/shard_map/all_to_all | solution.py:141
  13.1 0.8 reshape.97
  13.9 0.7 fusion.13
  14.7 0.6 collective-permute-start
  15.4 0.9 add.42
  16.4 6.2 %all-to-all-done = bf16[4,32,2048]{2,1,0:T(8,128)(2,1)S(1)} async-done(((bf16[4,32,2048]{2,1,0:T(8,128)(2,1)}), bf16[4,32,2048]{2,1,0:T(8,128)(2,1)S(1)}, u32[]{:S(2)}, u32[]{:S(2)}) %all-to-all-start) | async-done | bytes 524320 | tf_op jit(solution)/shard_map/all_to_all | solution.py:141
  22.6 0.1 collective-permute-start.2
  22.7 1.9 %collective-permute-start.1 = (bf16[4,32,2048]{2,1,0:T(8,128)(2,1)S(1)}, bf16[4,32,2048]{2,1,0:T(8,128)(2,1)}, u32[]{:S(2)}, u32[]{:S(2)}) collective-permute-start(bf16[4,32,2048]{2,1,0:T(8,128)(2,1)S(1)} %all-to-all-done), channel_id=1, source_target_pairs={{0,32},{8,40},{16,48},{24,56},{32,64},{40,72},{48,80},{56,88},{64,... | collective-permute-start | bytes 1572872 | tf_op jit(solution)/shard_map/ppermute | solution.py:19
  24.6 0.8 convolution_convert_fusion.7
  25.8 0.1 dynamic_update_slice.27
  26.0 0.1 multiply_reduce_fusion
  26.1 0.2 fusion.5
  26.3 8.7 %collective-permute-done.2 = bf16[4,32,2048]{2,1,0:T(8,128)(2,1)} collective-permute-done((bf16[4,32,2048]{2,1,0:T(8,128)(2,1)S(1)}, bf16[4,32,2048]{2,1,0:T(8,128)(2,1)}, u32[]{:S(2)}, u32[]{:S(2)}) %collective-permute-start.2) | collective-permute-done | bytes 524320 | tf_op jit(solution)/shard_map/ppermute | solution.py:19
  35.1 3.2 %collective-permute-start.4 = (bf16[4,32,2048]{2,1,0:T(8,128)(2,1)}, bf16[4,32,2048]{2,1,0:T(8,128)(2,1)S(1)}, u32[]{:S(2)}, u32[]{:S(2)}) collective-permute-start(bf16[4,32,2048]{2,1,0:T(8,128)(2,1)} %collective-permute-done.2), channel_id=1, source_target_pairs={{0,224},{8,232},{16,240},{24,248},{32,0},{40,8},{48,16},{56,24},{6... | collective-permute-start | bytes 1572872 | tf_op jit(solution)/shard_map/ppermute | solution.py:19
  38.3 1.9 %convolution_convert_fusion.5 = bf16[128,512]{1,0:T(8,128)(2,1)S(1)} fusion(bf16[128,2048]{1,0:T(8,128)(2,1)} %bitcast.7, bf16[512,2048]{1,0:T(8,128)(2,1)S(1)} %copy-done), kind=kOutput, calls=%fused_computation.5 | convolution fusion | flops 268500992 | bytes 2752512 | tf_op jit(solution)/shard_map/dot_general | solution.py:38
  40.3 1.9 %convolution_convert_fusion.6 = bf16[128,512]{1,0:T(8,128)(2,1)S(1)} fusion(bf16[128,2048]{1,0:T(8,128)(2,1)} %bitcast.5, bf16[512,2048]{1,0:T(8,128)(2,1)S(1)} %copy-done), kind=kOutput, calls=%fused_computation.6 | convolution fusion | flops 268500992 | bytes 2752512 | tf_op jit(solution)/shard_map/dot_general | solution.py:38
  42.2 5.1 %collective-permute-done.4 = bf16[4,32,2048]{2,1,0:T(8,128)(2,1)S(1)} collective-permute-done((bf16[4,32,2048]{2,1,0:T(8,128)(2,1)}, bf16[4,32,2048]{2,1,0:T(8,128)(2,1)S(1)}, u32[]{:S(2)}, u32[]{:S(2)}) %collective-permute-start.4) | collective-permute-done | bytes 524320 | tf_op jit(solution)/shard_map/ppermute | solution.py:19
  47.4 3.8 %collective-permute-start.6 = (bf16[4,32,2048]{2,1,0:T(8,128)(2,1)S(1)}, bf16[4,32,2048]{2,1,0:T(8,128)(2,1)S(1)}, u32[]{:S(2)}, u32[]{:S(2)}) collective-permute-start(bf16[4,32,2048]{2,1,0:T(8,128)(2,1)S(1)} %collective-permute-done.4), channel_id=1, source_target_pairs={{0,224},{8,232},{16,240},{24,248},{32,0},{40,8},{48,16},{56,24},{6... | collective-permute-start | bytes 1572872 | tf_op jit(solution)/shard_map/ppermute | solution.py:19
  51.2 0.8 convolution_convert_fusion.3
  52.0 1.5 collective-permute-done.3
  53.5 0.8 convolution_convert_fusion.4
  54.4 5.2 %collective-permute-done.6 = bf16[4,32,2048]{2,1,0:T(8,128)(2,1)S(1)} collective-permute-done((bf16[4,32,2048]{2,1,0:T(8,128)(2,1)S(1)}, bf16[4,32,2048]{2,1,0:T(8,128)(2,1)S(1)}, u32[]{:S(2)}, u32[]{:S(2)}) %collective-permute-start.6) | collective-permute-done | bytes 524320 | tf_op jit(solution)/shard_map/ppermute | solution.py:19
  59.6 3.6 %collective-permute-start.8 = (bf16[3,32,2048]{2,1,0:T(8,128)(2,1)S(1)}, bf16[3,32,2048]{2,1,0:T(8,128)(2,1)S(1)}, u32[]{:S(2)}, u32[]{:S(2)}) collective-permute-start(bf16[3,32,2048]{2,1,0:T(8,128)(2,1)S(1)} %slice.25), channel_id=1, source_target_pairs={{0,224},{8,232},{16,240},{24,248},{32,0},{40,8},{48,16},{56,24},{6... | collective-permute-start | bytes 1179656 | tf_op jit(solution)/shard_map/ppermute | solution.py:19
  63.1 0.8 convolution_convert_fusion.1
  64.0 0.8 collective-permute-done.5
  64.8 0.8 convolution_convert_fusion.2
  65.6 0.3 collective-permute-start.7
  65.9 5.8 %collective-permute-done.7 = bf16[1,32,2048]{2,1,0:T(8,128)(2,1)S(1)} collective-permute-done((bf16[1,32,2048]{2,1,0:T(8,128)(2,1)S(1)}, bf16[1,32,2048]{2,1,0:T(8,128)(2,1)S(1)}, u32[]{:S(2)}, u32[]{:S(2)}) %collective-permute-start.7) | collective-permute-done | bytes 131104 | tf_op jit(solution)/shard_map/ppermute | solution.py:19
  71.8 0.7 convolution_convert_fusion.10
  72.5 0.8 convolution_convert_fusion.9
  73.4 22.1 %all_to_all.30.parts = bf16[8,8,16,512]{3,2,1,0:T(8,128)(2,1)} all-to-all(bf16[8,8,16,512]{3,2,1,0:T(8,128)(2,1)S(1)} %constant_dynamic-update-slice_fusion), channel_id=1, replica_groups=mesh['grid'=32,'tile'=8] {'tile'}, dimensions={0} | all-to-all | bytes 2097152 | tf_op jit(solution)/shard_map/all_to_all | solution.py:168
  95.4 2.0 %shard_map.101 = bf16[32,4,512]{2,1,0:T(4,128)(2,1)} custom-call(bf16[8,8,16,512]{3,2,1,0:T(8,128)(2,1)} %all_to_all.30.parts), custom_call_target="tpu_custom_call" | custom-call | flops 524288 | bytes 1048576 | tf_op jit(solution)/shard_map/pallas_call | solution.py:96
  97.5 4.2 %collective-permute-start.9 = (bf16[128,512]{1,0:T(8,128)(2,1)S(1)}, bf16[128,512]{1,0:T(8,128)(2,1)S(1)}, u32[]{:S(2)}, u32[]{:S(2)}) collective-permute-start(bf16[128,512]{1,0:T(8,128)(2,1)S(1)} %reshape.118), channel_id=1, source_target_pairs={{0,0},{1,32},{2,64},{3,96},{4,128},{5,160},{6,192},{7,224},{8,8},{... | collective-permute-start | bytes 393224 | tf_op jit(solution)/shard_map/ppermute | solution.py:29
  101.7 4.0 %collective-permute-done.9 = bf16[128,512]{1,0:T(8,128)(2,1)S(1)} collective-permute-done((bf16[128,512]{1,0:T(8,128)(2,1)S(1)}, bf16[128,512]{1,0:T(8,128)(2,1)S(1)}, u32[]{:S(2)}, u32[]{:S(2)}) %collective-permute-start.9) | collective-permute-done | bytes 131104 | tf_op jit(solution)/shard_map/ppermute | solution.py:29
  105.7 0.6 copy-done.3
  106.4 14.6 %all-to-all-start.2 = ((bf16[32,4,512]{2,1,0:T(4,128)(2,1)}), bf16[32,4,512]{2,1,0:T(4,128)(2,1)S(1)}, u32[]{:S(2)}, u32[]{:S(2)}) async-start(bf16[32,4,512]{2,1,0:T(4,128)(2,1)} %shard_map.101), calls=%async_computation.2 | async-start | bytes 262144 | tf_op jit(solution)/shard_map/all_to_all | solution.py:173
  121.0 0.2 compare_reduce_fusion
  121.2 9.3 %all-to-all-done.2 = bf16[32,4,512]{2,1,0:T(4,128)(2,1)S(1)} async-done(((bf16[32,4,512]{2,1,0:T(4,128)(2,1)}), bf16[32,4,512]{2,1,0:T(4,128)(2,1)S(1)}, u32[]{:S(2)}, u32[]{:S(2)}) %all-to-all-start.2) | async-done | bytes 131104 | tf_op jit(solution)/shard_map/all_to_all | solution.py:173
  130.6 0.4 fusion.1
  131.0 0.2 fusion.3
  131.2 0.7 copy.23
  131.9 3.4 %all-to-all-start.3 = ((bf16[8,4,4,512]{3,1,2,0:T(4,128)(2,1)}), bf16[8,4,4,512]{3,1,2,0:T(4,128)(2,1)S(1)}, u32[]{:S(2)}, u32[]{:S(2)}) async-start(bf16[8,4,4,512]{3,1,2,0:T(4,128)(2,1)} %copy.23), calls=%async_computation.3 | async-start | bytes 262144 | tf_op jit(solution)/shard_map/all_to_all | solution.py:179
  135.4 5.9 %all-to-all-done.3 = bf16[8,4,4,512]{3,1,2,0:T(4,128)(2,1)S(1)} async-done(((bf16[8,4,4,512]{3,1,2,0:T(4,128)(2,1)}), bf16[8,4,4,512]{3,1,2,0:T(4,128)(2,1)S(1)}, u32[]{:S(2)}, u32[]{:S(2)}) %all-to-all-start.3) | async-done | bytes 131104 | tf_op jit(solution)/shard_map/all_to_all | solution.py:179
  141.3 4.8 %shard_map.102 = bf16[8,32,256]{2,1,0:T(8,128)(2,1)S(1)} custom-call(bf16[32,2048]{1,0:T(8,128)(2,1)S(1)} %bitcast.68, bf16[32,2048]{1,0:T(8,128)(2,1)S(1)} %bitcast.69, bf16[32,2048]{1,0:T(8,128)(2,1)S(1)} %bitcast.70, bf16[32,2048]{1,0:T(8,128)(2,1)S(1)} %bitcast.71, bf16[2048,2048]{1,0:T(8,128)(2,1)} %refs_7_.1, bf16[2048,2048]{1,0:T(8,128)(2,1)} %refs_7_.1, ...), custom_call_target="tpu_custom_call" | custom-call | flops 268435456 | bytes 8388608 | tf_op jit(solution)/shard_map/pallas_call | solution.py:69
  146.2 8.5 %all_to_all.31 = bf16[8,32,256]{2,1,0:T(8,128)(2,1)S(1)} all-to-all(bf16[8,32,256]{2,1,0:T(8,128)(2,1)S(1)} %shard_map.102), channel_id=1, replica_groups=mesh['grid'=32,'tile'=8] {'tile'}, dimensions={0} | all-to-all | bytes 262144 | tf_op jit(solution)/shard_map/all_to_all | solution.py:185
  154.8 21.4 %all_to_all.32 = bf16[32,32,256]{2,1,0:T(8,128)(2,1)S(1)} all-to-all(bf16[32,32,256]{2,1,0:T(8,128)(2,1)S(1)} %broadcast_in_dim.8), channel_id=1, replica_groups=mesh['grid'=32,'tile'=8] {'grid'}, dimensions={0} | all-to-all | bytes 1048576 | tf_op jit(solution)/shard_map/all_to_all | solution.py:34
  176.2 2.4 %convolution_convert_fusion = bf16[256,512]{1,0:T(8,128)(2,1)} fusion(bf16[1024,256]{1,0:T(8,128)(2,1)S(1)} %bitcast.77, bf16[1024,512]{1,0:T(8,128)(2,1)} %all-gather.2.cloned.1.call-done), kind=kOutput, calls=%fused_computation | convolution fusion | flops 268566528 | bytes 1835008 | tf_op jit(solution)/shard_map/dot_general | solution.py:38
  (47 shorter events, 1.1 us)
Async XLA Ops:
  6.5 18.1 %copy-start = (bf16[512,2048]{1,0:T(8,128)(2,1)S(1)}, bf16[512,2048]{1,0:T(8,128)(2,1)}, u32[]{:S(2)}) copy-start(bf16[512,2048]{1,0:T(8,128)(2,1)} %param.12) | copy-start | bytes 6291460
  6.5 9.7 %copy-start.2 = (f32[3,16384]{1,0:T(4,128)S(1)}, f32[3,16384]{1,0:T(4,128)}, u32[]{:S(2)}) copy-start(f32[3,16384]{1,0:T(4,128)} %param.15) | copy-start | bytes 589828
  8.7 13.9 %all-to-all-start = ((bf16[4,32,2048]{2,1,0:T(8,128)(2,1)}), bf16[4,32,2048]{2,1,0:T(8,128)(2,1)S(1)}, u32[]{:S(2)}, u32[]{:S(2)}) async-start(bf16[4,32,2048]{2,1,0:T(8,128)(2,1)} %shard_map.100), calls=%async_computation | async-start | bytes 1048576 | tf_op jit(solution)/shard_map/all_to_all | solution.py:141
  13.1 141.6 %all-gather.2.cloned.1.call-start = ((), (), s32[]{:S(2)}) async-start(), calls=%async_computation.6 | async-start | bytes 1179648 | tf_op jit(solution)/shard_map/all_gather | solution.py:172
  14.7 1.6 collective-permute-start
  22.6 12.5 %collective-permute-start.2 = (bf16[4,32,2048]{2,1,0:T(8,128)(2,1)S(1)}, bf16[4,32,2048]{2,1,0:T(8,128)(2,1)}, u32[]{:S(2)}, u32[]{:S(2)}) collective-permute-start(bf16[4,32,2048]{2,1,0:T(8,128)(2,1)S(1)} %all-to-all-done), channel_id=1, source_target_pairs={{0,224},{8,232},{16,240},{24,248},{32,0},{40,8},{48,16},{56,24},{6... | collective-permute-start | bytes 1572872 | tf_op jit(solution)/shard_map/ppermute | solution.py:19
  22.7 17.5 %collective-permute-start.1 = (bf16[4,32,2048]{2,1,0:T(8,128)(2,1)S(1)}, bf16[4,32,2048]{2,1,0:T(8,128)(2,1)}, u32[]{:S(2)}, u32[]{:S(2)}) collective-permute-start(bf16[4,32,2048]{2,1,0:T(8,128)(2,1)S(1)} %all-to-all-done), channel_id=1, source_target_pairs={{0,32},{8,40},{16,48},{24,56},{32,64},{40,72},{48,80},{56,88},{64,... | collective-permute-start | bytes 1572872 | tf_op jit(solution)/shard_map/ppermute | solution.py:19
  35.1 12.3 %collective-permute-start.4 = (bf16[4,32,2048]{2,1,0:T(8,128)(2,1)}, bf16[4,32,2048]{2,1,0:T(8,128)(2,1)S(1)}, u32[]{:S(2)}, u32[]{:S(2)}) collective-permute-start(bf16[4,32,2048]{2,1,0:T(8,128)(2,1)} %collective-permute-done.2), channel_id=1, source_target_pairs={{0,224},{8,232},{16,240},{24,248},{32,0},{40,8},{48,16},{56,24},{6... | collective-permute-start | bytes 1572872 | tf_op jit(solution)/shard_map/ppermute | solution.py:19
  40.2 13.3 %collective-permute-start.3 = (bf16[4,32,2048]{2,1,0:T(8,128)(2,1)}, bf16[4,32,2048]{2,1,0:T(8,128)(2,1)S(1)}, u32[]{:S(2)}, u32[]{:S(2)}) collective-permute-start(bf16[4,32,2048]{2,1,0:T(8,128)(2,1)} %collective-permute-done.1), channel_id=1, source_target_pairs={{0,32},{8,40},{16,48},{24,56},{32,64},{40,72},{48,80},{56,88},{64,... | collective-permute-start | bytes 1572872 | tf_op jit(solution)/shard_map/ppermute | solution.py:19
  47.4 12.2 %collective-permute-start.6 = (bf16[4,32,2048]{2,1,0:T(8,128)(2,1)S(1)}, bf16[4,32,2048]{2,1,0:T(8,128)(2,1)S(1)}, u32[]{:S(2)}, u32[]{:S(2)}) collective-permute-start(bf16[4,32,2048]{2,1,0:T(8,128)(2,1)S(1)} %collective-permute-done.4), channel_id=1, source_target_pairs={{0,224},{8,232},{16,240},{24,248},{32,0},{40,8},{48,16},{56,24},{6... | collective-permute-start | bytes 1572872 | tf_op jit(solution)/shard_map/ppermute | solution.py:19
  53.5 11.3 %collective-permute-start.5 = (bf16[4,32,2048]{2,1,0:T(8,128)(2,1)S(1)}, bf16[4,32,2048]{2,1,0:T(8,128)(2,1)S(1)}, u32[]{:S(2)}, u32[]{:S(2)}) collective-permute-start(bf16[4,32,2048]{2,1,0:T(8,128)(2,1)S(1)} %collective-permute-done.3), channel_id=1, source_target_pairs={{0,32},{8,40},{16,48},{24,56},{32,64},{40,72},{48,80},{56,88},{64,... | collective-permute-start | bytes 1572872 | tf_op jit(solution)/shard_map/ppermute | solution.py:19
  59.6 12.9 %collective-permute-start.8 = (bf16[3,32,2048]{2,1,0:T(8,128)(2,1)S(1)}, bf16[3,32,2048]{2,1,0:T(8,128)(2,1)S(1)}, u32[]{:S(2)}, u32[]{:S(2)}) collective-permute-start(bf16[3,32,2048]{2,1,0:T(8,128)(2,1)S(1)} %slice.25), channel_id=1, source_target_pairs={{0,224},{8,232},{16,240},{24,248},{32,0},{40,8},{48,16},{56,24},{6... | collective-permute-start | bytes 1179656 | tf_op jit(solution)/shard_map/ppermute | solution.py:19
  65.6 6.2 %collective-permute-start.7 = (bf16[1,32,2048]{2,1,0:T(8,128)(2,1)S(1)}, bf16[1,32,2048]{2,1,0:T(8,128)(2,1)S(1)}, u32[]{:S(2)}, u32[]{:S(2)}) collective-permute-start(bf16[1,32,2048]{2,1,0:T(8,128)(2,1)S(1)} %slice.24), channel_id=1, source_target_pairs={{0,32},{8,40},{16,48},{24,56},{32,64},{40,72},{48,80},{56,88},{64,... | collective-permute-start | bytes 393224 | tf_op jit(solution)/shard_map/ppermute | solution.py:19
  73.3 47.7 %copy-start.5 = (s32[8,16]{1,0:T(8,128)S(1)}, s32[8,16]{1,0:T(8,128)}, u32[]{:S(2)}) copy-start(s32[8,16]{1,0:T(8,128)} %param.19) | copy-start | bytes 1540
  73.3 57.2 %copy-start.1 = (bf16[512,512]{1,0:T(8,128)(2,1)S(1)}, bf16[512,512]{1,0:T(8,128)(2,1)}, u32[]{:S(2)}) copy-start(bf16[512,512]{1,0:T(8,128)(2,1)} %param.13) | copy-start | bytes 1572868
  73.4 57.2 %copy-start.4 = (s32[32,32]{1,0:T(8,128)S(1)}, s32[32,32]{1,0:T(8,128)}, u32[]{:S(2)}) copy-start(s32[32,32]{1,0:T(8,128)} %param.14) | copy-start | bytes 12292
  97.5 8.2 %collective-permute-start.9 = (bf16[128,512]{1,0:T(8,128)(2,1)S(1)}, bf16[128,512]{1,0:T(8,128)(2,1)S(1)}, u32[]{:S(2)}, u32[]{:S(2)}) collective-permute-start(bf16[128,512]{1,0:T(8,128)(2,1)S(1)} %reshape.118), channel_id=1, source_target_pairs={{0,0},{1,32},{2,64},{3,96},{4,128},{5,160},{6,192},{7,224},{8,8},{... | collective-permute-start | bytes 393224 | tf_op jit(solution)/shard_map/ppermute | solution.py:29
  105.7 0.6 copy-start.3
  106.4 24.1 %all-to-all-start.2 = ((bf16[32,4,512]{2,1,0:T(4,128)(2,1)}), bf16[32,4,512]{2,1,0:T(4,128)(2,1)S(1)}, u32[]{:S(2)}, u32[]{:S(2)}) async-start(bf16[32,4,512]{2,1,0:T(4,128)(2,1)} %shard_map.101), calls=%async_computation.2 | async-start | bytes 262144 | tf_op jit(solution)/shard_map/all_to_all | solution.py:173
  131.9 9.4 %all-to-all-start.3 = ((bf16[8,4,4,512]{3,1,2,0:T(4,128)(2,1)}), bf16[8,4,4,512]{3,1,2,0:T(4,128)(2,1)S(1)}, u32[]{:S(2)}, u32[]{:S(2)}) async-start(bf16[8,4,4,512]{3,1,2,0:T(4,128)(2,1)} %copy.23), calls=%async_computation.3 | async-start | bytes 262144 | tf_op jit(solution)/shard_map/all_to_all | solution.py:179
Sparse Core Ops, SparseCore 0:
  106.5 29.1 all-gather.1
